TPU v7x, 32 devices: a whole 2x2x4 slice. The times are simulated.
32 devices in a mesh: rows: 4 (over y, core), seq: 8 (over z, x).
Axes of the slice: x: 2, y: 2, z: 4, core: 2. Of those that a mesh axis runs over, the one named last changes fastest.
Arguments:
- block_in: float32 [8, 256, 8, 768], P('rows', None, 'seq'), may hold values from -12 to 12
- segment_ids: int32 [8, 256, 8], P('rows', None, 'seq'), may hold values from 0 to 15, as said below
- valid_mask: int32 [8, 256, 8], P('rows', None, 'seq'), may hold values 0 or 1
- cotangent: float32 [8, 256, 8, 768], P('rows', None, 'seq'), may hold values from -6 to 6
- gain_mix: float32 [768], replicated, may hold values from 0.5 to 1.5
- in_proj: bfloat16 [768, 2304], replicated, may hold values from -0.21875 to 0.21875
- short_taps: float32 [3, 2304], replicated, may hold values from -3 to 3
- long_kernel: float32 [256, 8, 768], P(None, 'seq'), may hold values from -0.3125 to 0.3125
- skip_gain: float32 [768], replicated, may hold values from -3 to 3
- out_proj: bfloat16 [768, 768], replicated, may hold values from -0.21875 to 0.21875
- gain_mlp: float32 [768], replicated, may hold values from 0.5 to 1.5
- up_proj: bfloat16 [768, 3072], replicated, may hold values from -0.21875 to 0.21875
- down_proj: bfloat16 [3072, 768], replicated, may hold values from -0.15625 to 0.15625
Outputs:
- block_out: float32 [8, 256, 8, 768], P('rows', None, 'seq')
- grad_input: float32 [8, 256, 8, 768], P('rows', None, 'seq')
- grad_gain_mix: float32 [768], replicated
- grad_in_proj: float32 [768, 2304], P('seq')
- grad_short_taps: float32 [3, 2304], replicated
- grad_long_kernel: float32 [256, 8, 768], P(None, 'seq')
- grad_skip_gain: float32 [768], replicated
- grad_out_proj: float32 [768, 768], P('seq')
- grad_gain_mlp: float32 [768], replicated
- grad_up_proj: float32 [768, 3072], P('seq')
- grad_down_proj: float32 [3072, 768], P('seq')
- rms_stats: float32 [3], replicated
Inputs may be any that keep to these rules, and one draw needn't show every extreme that they name: `segment_ids`: within a row non-decreasing along t = b * 8 + p, starting at 0 and rising by at most one per position.
All inputs are finite; a program needn't handle non-finite values. No bound on the sum of `valid_mask` on one device may be relied on, other than what follows from the above.
Results may differ from a plain program's by a relative error of at most 0.015.
Values may be sent and summed in bfloat16 or wider, within the bound.
A program may use at most 256 MiB of HBM per device.

v0:
```python
import math

import jax
import jax.numpy as jnp
from jax import lax
from jax.sharding import PartitionSpec as P

EPS = 1e-05
THRESH = 0.003
HIGH = lax.Precision.HIGHEST


def shortened(x):

    def short(part):
        return part.astype(jnp.bfloat16) if part.dtype == jnp.float32 else part

    return jax.tree.map(short, x)


def passed_along(block, axis, distance):
    devices = range(lax.axis_size(axis))
    route = [((i - distance) % len(devices), i) for i in devices]
    return lax.ppermute(block, axis, route)


def norm_scale(value, gain):
    return value * lax.rsqrt(jnp.mean(value * value, axis=-1, keepdims=True) + EPS) * gain


def angle_tables(left_count, right_count, period):
    left_idx = jnp.arange(left_count, dtype=jnp.int32)[:, None]
    right_idx = jnp.arange(right_count, dtype=jnp.int32)[None, :]
    phase = (left_idx * right_idx % period).astype(jnp.float32) * (2.0 * math.pi / period)
    return (jnp.cos(phase), jnp.sin(phase))


def twiddle_tables(shard_index, spec_len, whole_len):
    turned = shard_index * jnp.arange(spec_len, dtype=jnp.int32) % whole_len
    phase = turned.astype(jnp.float32) * (2.0 * math.pi / whole_len)
    return (jnp.cos(phase)[None, :, None], jnp.sin(phase)[None, :, None])


def local_forward(signal, shard_index, whole_len):
    blocks = signal.shape[1]
    cos_table, sin_table = angle_tables(blocks, 2 * blocks, 2 * blocks)
    real_part = jnp.einsum("rjd,jk->rkd", signal, cos_table, precision=HIGH)
    imag_part = -jnp.einsum("rjd,jk->rkd", signal, sin_table, precision=HIGH)
    cos_twid, sin_twid = twiddle_tables(shard_index, 2 * blocks, whole_len)
    out_real = real_part * cos_twid + imag_part * sin_twid
    out_imag = imag_part * cos_twid - real_part * sin_twid
    return (out_real[:, :, None, :], out_imag[:, :, None, :])


def cross_section(real_part, imag_part, direction):
    count = real_part.shape[2]
    cos_table, sin_table = angle_tables(count, count, count)
    re_cos = jnp.einsum("rcpd,pm->rcmd", real_part, cos_table, precision=HIGH)
    re_sin = jnp.einsum("rcpd,pm->rcmd", real_part, sin_table, precision=HIGH)
    im_cos = jnp.einsum("rcpd,pm->rcmd", imag_part, cos_table, precision=HIGH)
    im_sin = jnp.einsum("rcpd,pm->rcmd", imag_part, sin_table, precision=HIGH)
    return (re_cos - direction * im_sin, im_cos + direction * re_sin)


def local_inverse(real_part, imag_part, shard_index, whole_len):
    real_part = real_part[:, :, 0, :]
    imag_part = imag_part[:, :, 0, :]
    spec_len = real_part.shape[1]
    cos_twid, sin_twid = twiddle_tables(shard_index, spec_len, whole_len)
    turned_re = real_part * cos_twid - imag_part * sin_twid
    turned_im = imag_part * cos_twid + real_part * sin_twid
    cos_table, sin_table = angle_tables(spec_len, spec_len // 2, spec_len)
    result = jnp.einsum("rkd,kj->rjd", turned_re, cos_table, precision=HIGH)
    result = result - jnp.einsum("rkd,kj->rjd", turned_im, sin_table, precision=HIGH)
    return result / whole_len


def earlier(members, at_start):
    received = jax.tree.map(
        lambda part, own: part.astype(own.dtype),
        passed_along(shortened(members), "seq", 1),
        members,
    )
    placed = []
    for member in received:
        rolled = jnp.concatenate([jnp.zeros_like(member[:, :1]), member[:, :-1]], axis=1)
        placed.append(jnp.where(at_start, rolled, member))
    return tuple(placed)


def later(member, at_end):
    received = passed_along(member.astype(jnp.bfloat16), "seq", -1).astype(member.dtype)
    rolled = jnp.concatenate([received[:, 1:], jnp.zeros_like(received[:, :1])], axis=1)
    return jnp.where(at_end, rolled, received)


def times_trans(left, right):
    return lax.dot_general(
        left, right, (((1,), (1,)), ((), ())), preferred_element_type=jnp.float32
    )


def trans_times(left, right):
    return lax.dot_general(
        left, right, (((0,), (0,)), ((), ())), preferred_element_type=jnp.float32
    )


def local(
    block_in,
    segment_ids,
    valid_mask,
    cotangent,
    gain_mix,
    in_proj,
    short_taps,
    long_kernel,
    skip_gain,
    out_proj,
    gain_mlp,
    up_proj,
    down_proj,
):
    batch_rows = block_in.shape[0]
    blocks = block_in.shape[1]
    width = block_in.shape[3]
    shard_count = lax.axis_size("seq")
    shard_index = lax.axis_index("seq")
    whole_len = 2 * blocks * shard_count
    tokens = batch_rows * blocks
    at_start = shard_index == 0
    at_end = shard_index == shard_count - 1
    flat_in = block_in.reshape(tokens, width)
    mask_rows = valid_mask[:, :, 0].astype(jnp.float32)[:, :, None]
    normed_one = norm_scale(flat_in, gain_mix).astype(jnp.bfloat16)
    proj_low = jnp.dot(normed_one, in_proj, preferred_element_type=jnp.float32).astype(jnp.bfloat16)
    proj_low = proj_low.reshape(batch_rows, blocks, 3 * width)
    seg_low = segment_ids[:, :, 0].astype(jnp.bfloat16)[:, :, None]
    prev_one = earlier((proj_low, seg_low), at_start)
    prev_two = earlier(prev_one, at_start)
    same_one = (prev_one[1] == seg_low).astype(jnp.float32)
    same_two = (prev_two[1] == seg_low).astype(jnp.float32)
    proj_now = proj_low.astype(jnp.float32)
    proj_one = prev_one[0].astype(jnp.float32)
    proj_two = prev_two[0].astype(jnp.float32)
    conv_short = (
        short_taps[0] * proj_now
        + short_taps[1] * proj_one * same_one
        + short_taps[2] * proj_two * same_two
    )
    query = conv_short[:, :, :width]
    keys = conv_short[:, :, width : 2 * width]
    values = conv_short[:, :, 2 * width :]
    gated = keys * values * mask_rows
    raw_taps = long_kernel[:, 0, :]
    taps_eff = raw_taps - THRESH * jnp.tanh(raw_taps / THRESH)
    kern_re, kern_im = local_forward(taps_eff[None], shard_index, whole_len)
    kern_re, kern_im = (
        lax.all_to_all(
            kern_re.astype(jnp.bfloat16), "seq", split_axis=1, concat_axis=2, tiled=True
        ).astype(kern_re.dtype),
        lax.all_to_all(
            kern_im.astype(jnp.bfloat16), "seq", split_axis=1, concat_axis=2, tiled=True
        ).astype(kern_im.dtype),
    )
    kern_re, kern_im = cross_section(kern_re, kern_im, -1.0)
    gate_re, gate_im = local_forward(gated, shard_index, whole_len)
    gate_re, gate_im = (
        lax.all_to_all(
            gate_re.astype(jnp.bfloat16), "seq", split_axis=1, concat_axis=2, tiled=True
        ).astype(gate_re.dtype),
        lax.all_to_all(
            gate_im.astype(jnp.bfloat16), "seq", split_axis=1, concat_axis=2, tiled=True
        ).astype(gate_im.dtype),
    )
    gate_re, gate_im = cross_section(gate_re, gate_im, -1.0)
    prod_re = gate_re * kern_re - gate_im * kern_im
    prod_im = gate_re * kern_im + gate_im * kern_re
    prod_re, prod_im = cross_section(prod_re, prod_im, 1.0)
    prod_re, prod_im = (
        lax.all_to_all(
            prod_re.astype(jnp.bfloat16), "seq", split_axis=2, concat_axis=1, tiled=True
        ).astype(prod_re.dtype),
        lax.all_to_all(
            prod_im.astype(jnp.bfloat16), "seq", split_axis=2, concat_axis=1, tiled=True
        ).astype(prod_im.dtype),
    )
    long_out = local_inverse(prod_re, prod_im, shard_index, whole_len) + skip_gain * gated
    mixer_low = (query * long_out).reshape(tokens, width).astype(jnp.bfloat16)
    mixer_out = jnp.dot(mixer_low, out_proj, preferred_element_type=jnp.float32)
    resid_mid = flat_in + mixer_out
    normed_two = norm_scale(resid_mid, gain_mlp).astype(jnp.bfloat16)
    up_val = jnp.dot(normed_two, up_proj, preferred_element_type=jnp.float32)
    act_low = jax.nn.gelu(up_val).astype(jnp.bfloat16)
    mlp_out = jnp.dot(act_low, down_proj, preferred_element_type=jnp.float32)
    flat_out = resid_mid + mlp_out
    grad_out = cotangent.reshape(tokens, width)
    grad_mlp = grad_out.astype(jnp.bfloat16)
    grad_down = trans_times(act_low, grad_mlp)
    grad_act = times_trans(grad_mlp, down_proj)
    unused_val, gelu_back = jax.vjp(jax.nn.gelu, up_val)
    grad_upval = gelu_back(grad_act)[0].astype(jnp.bfloat16)
    grad_up = trans_times(normed_two, grad_upval)
    grad_norm_two = times_trans(grad_upval, up_proj)
    unused_two, norm_back_two = jax.vjp(norm_scale, resid_mid, gain_mlp)
    grad_resid, grad_gain_two = norm_back_two(grad_norm_two)
    grad_mid = grad_out + grad_resid
    grad_mix = grad_mid.astype(jnp.bfloat16)
    grad_outp = trans_times(mixer_low, grad_mix)
    grad_prod = times_trans(grad_mix, out_proj).reshape(batch_rows, blocks, width)
    grad_query = grad_prod * long_out
    grad_long = grad_prod * query
    back_re, back_im = local_forward(grad_long, shard_index, whole_len)
    back_re, back_im = (
        lax.all_to_all(
            back_re.astype(jnp.bfloat16), "seq", split_axis=1, concat_axis=2, tiled=True
        ).astype(back_re.dtype),
        lax.all_to_all(
            back_im.astype(jnp.bfloat16), "seq", split_axis=1, concat_axis=2, tiled=True
        ).astype(back_im.dtype),
    )
    back_re, back_im = cross_section(back_re, back_im, -1.0)
    sig_re = kern_re * back_re + kern_im * back_im
    sig_im = kern_re * back_im - kern_im * back_re
    tap_re = jnp.sum(gate_re * back_re + gate_im * back_im, axis=0, keepdims=True)
    tap_im = jnp.sum(gate_re * back_im - gate_im * back_re, axis=0, keepdims=True)
    sig_re, sig_im = cross_section(sig_re, sig_im, 1.0)
    tap_re, tap_im = cross_section(tap_re, tap_im, 1.0)
    sig_re, sig_im, tap_re, tap_im = (
        lax.all_to_all(
            sig_re.astype(jnp.bfloat16), "seq", split_axis=2, concat_axis=1, tiled=True
        ).astype(sig_re.dtype),
        lax.all_to_all(
            sig_im.astype(jnp.bfloat16), "seq", split_axis=2, concat_axis=1, tiled=True
        ).astype(sig_im.dtype),
        lax.all_to_all(
            tap_re.astype(jnp.bfloat16), "seq", split_axis=2, concat_axis=1, tiled=True
        ).astype(tap_re.dtype),
        lax.all_to_all(
            tap_im.astype(jnp.bfloat16), "seq", split_axis=2, concat_axis=1, tiled=True
        ).astype(tap_im.dtype),
    )
    grad_gated = local_inverse(sig_re, sig_im, shard_index, whole_len) + skip_gain * grad_long
    grad_taps_eff = local_inverse(tap_re, tap_im, shard_index, whole_len)[0]
    tanh_val = jnp.tanh(raw_taps / THRESH)
    grad_kernel = (grad_taps_eff * tanh_val * tanh_val)[:, None, :]
    grad_kernel = lax.psum(grad_kernel.astype(jnp.bfloat16), "rows").astype(jnp.float32)
    grad_skip = jnp.sum(grad_long * gated, axis=(0, 1))
    grad_short = jnp.concatenate(
        [grad_query, grad_gated * values * mask_rows, grad_gated * keys * mask_rows], axis=2
    )
    grad_tap_rows = jnp.stack(
        [
            jnp.sum(grad_short * proj_now, axis=(0, 1)),
            jnp.sum(grad_short * proj_one * same_one, axis=(0, 1)),
            jnp.sum(grad_short * proj_two * same_two, axis=(0, 1)),
        ]
    )
    inner_term = short_taps[1] * grad_short * same_one + later(
        short_taps[2] * grad_short * same_two, at_end
    )
    grad_proj = short_taps[0] * grad_short + later(inner_term, at_end)
    grad_proj = grad_proj.reshape(tokens, 3 * width).astype(jnp.bfloat16)
    grad_inp = trans_times(normed_one, grad_proj)
    grad_norm_one = times_trans(grad_proj, in_proj)
    unused_one, norm_back_one = jax.vjp(norm_scale, flat_in, gain_mix)
    grad_first, grad_gain_one = norm_back_one(grad_norm_one)
    grad_flat = grad_mid + grad_first
    mask_flat = mask_rows.reshape(tokens, 1)
    stat_sums = jnp.stack(
        [
            jnp.sum(mask_flat * flat_out * flat_out),
            jnp.sum(mask_flat * mixer_out * mixer_out),
            jnp.sum(mask_flat * mlp_out * mlp_out),
            jnp.sum(mask_flat),
        ]
    )
    grad_gain_one, grad_gain_two, grad_tap_rows, grad_skip, stat_sums = lax.psum(
        (grad_gain_one, grad_gain_two, grad_tap_rows, grad_skip, stat_sums), ("rows", "seq")
    )
    rms_stats = jnp.sqrt(stat_sums[:3] / (jnp.maximum(stat_sums[3], 1.0) * width))
    shares = (
        lax.psum_scatter(grad_inp, "seq", scatter_dimension=0, tiled=True),
        lax.psum_scatter(grad_outp, "seq", scatter_dimension=0, tiled=True),
        lax.psum_scatter(grad_up, "seq", scatter_dimension=0, tiled=True),
        lax.psum_scatter(grad_down, "seq", scatter_dimension=0, tiled=True),
    )
    grad_inp, grad_outp, grad_up, grad_down = (
        lax.psum(shares[0].astype(jnp.bfloat16), "rows").astype(jnp.float32),
        lax.psum(shares[1].astype(jnp.bfloat16), "rows").astype(jnp.float32),
        lax.psum(shares[2].astype(jnp.bfloat16), "rows").astype(jnp.float32),
        lax.psum(shares[3].astype(jnp.bfloat16), "rows").astype(jnp.float32),
    )
    return (
        flat_out.reshape(block_in.shape),
        grad_flat.reshape(block_in.shape),
        grad_gain_one,
        grad_inp,
        grad_tap_rows,
        grad_kernel,
        grad_skip,
        grad_outp,
        grad_gain_two,
        grad_up,
        grad_down,
        rms_stats,
    )


def solution(mesh):
    return jax.shard_map(
        local,
        mesh=mesh,
        in_specs=(
            P("rows", None, "seq", None),
            P("rows", None, "seq"),
            P("rows", None, "seq"),
            P("rows", None, "seq", None),
            P(),
            P(),
            P(),
            P(None, "seq", None),
            P(),
            P(),
            P(),
            P(),
            P(),
        ),
        out_specs=(
            P("rows", None, "seq", None),
            P("rows", None, "seq", None),
            P(),
            P("seq", None),
            P(),
            P(None, "seq", None),
            P(),
            P("seq", None),
            P(),
            P("seq", None),
            P("seq", None),
            P(),
        ),
        check_vma=False,
    )
```

profile of v0, /device:TPU:0, one launch (start us, length us, event | category | flops | bytes accessed | tf_op | source)
XLA Modules:
  0.0 1217.9 jit_solution(15514783102854697448)
XLA Ops:
  19.1 54.6 %collective-permute-done = bf16[2,256,2304]{2,1,0:T(8,128)(2,1)} collective-permute-done((bf16[2,256,2304]{2,1,0:T(8,128)(2,1)}, bf16[2,256,2304]{2,1,0:T(8,128)(2,1)}, u32[]{:S(2)}, u32[]{:S(2)}) %collective-permute-start) | collective-permute-done | bytes 2359328 | tf_op jit(solution)/shard_map/ppermute | solution.py:24
  81.3 5.4 fusion.95
  89.6 7.3 reduce.10
  99.8 6.0 all-to-all-start.2
  107.9 37.9 %collective-permute-done.1 = bf16[2,256,1]{1,2,0:T(2,128)(2,1)S(1)} collective-permute-done((bf16[2,256,1]{1,2,0:T(2,128)(2,1)S(1)}, bf16[2,256,1]{1,2,0:T(2,128)(2,1)S(1)}, u32[]{:S(2)}, u32[]{:S(2)}) %collective-permute-start.1) | collective-permute-done | bytes 1056 | tf_op jit(solution)/shard_map/ppermute | solution.py:24
  153.6 7.3 reduce.9
  166.4 6.5 all-to-all-start.3
  172.9 4.3 fusion.9
  179.3 4.7 fusion.124
  184.1 6.9 fusion.45
  193.8 7.7 all-to-all-start.1
  201.5 4.3 copy.73
  205.7 30.7 %all-to-all-done.1 = bf16[2,512,1,768]{3,0,2,1:T(2,128)(2,1)} async-done(((bf16[2,512,1,768]{3,0,2,1:T(2,128)(2,1)}), bf16[2,512,1,768]{3,0,2,1:T(2,128)(2,1)}, u32[]{:S(2)}, u32[]{:S(2)}) %all-to-all-start.1) | async-done | bytes 1572896 | tf_op jit(solution)/shard_map/all_to_all | solution.py:172
  236.4 4.3 all-to-all-start
  240.7 5.5 reshape.332
  248.6 5.9 reshape.330
  262.8 5.9 fusion.61
  268.6 8.5 all-to-all-done
  277.1 4.5 fusion.59
  281.6 4.8 multiply_add_fusion.1
  286.5 5.8 multiply_subtract_fusion.1
  300.2 4.3 all-to-all-start.5
  304.6 5.6 fusion.188
  315.7 25.4 %all-to-all-done.5 = bf16[2,64,8,768]{3,1,0,2:T(8,128)(2,1)} async-done(((bf16[2,64,8,768]{3,1,0,2:T(8,128)(2,1)}), bf16[2,64,8,768]{3,1,0,2:T(8,128)(2,1)}, u32[]{:S(2)}, u32[]{:S(2)}) %all-to-all-start.5) | async-done | bytes 1572896 | tf_op jit(solution)/shard_map/all_to_all | solution.py:184
  341.2 4.3 all-to-all-start.4
  348.3 7.6 fusion.395
  359.4 22.7 %all-to-all-done.4 = bf16[2,64,8,768]{3,1,0,2:T(8,128)(2,1)} async-done(((bf16[2,64,8,768]{3,1,0,2:T(8,128)(2,1)}), bf16[2,64,8,768]{3,1,0,2:T(8,128)(2,1)}, u32[]{:S(2)}, u32[]{:S(2)}) %all-to-all-start.4) | async-done | bytes 1572896 | tf_op jit(solution)/shard_map/all_to_all | solution.py:181
  384.5 5.0 fusion.32
  389.5 7.8 multiply_convert_fusion.4
  398.3 8.7 fusion.6
  411.4 5.9 fusion.42
  420.9 9.9 fusion.387
  433.6 4.8 multiply_reduce_fusion.1
  438.4 4.7 fusion.122
  443.1 7.2 fusion.47
  453.0 4.3 all-to-all-start.7
  461.5 41.9 %all-to-all-done.7 = bf16[2,512,1,768]{3,0,2,1:T(2,128)(2,1)} async-done(((bf16[2,512,1,768]{3,0,2,1:T(2,128)(2,1)}), bf16[2,512,1,768]{3,0,2,1:T(2,128)(2,1)}, u32[]{:S(2)}, u32[]{:S(2)}) %all-to-all-start.7) | async-done | bytes 1572896 | tf_op jit(solution)/shard_map/all_to_all | solution.py:218
  503.5 4.3 all-to-all-start.6
  508.3 8.7 fusion.377
  517.0 5.9 fusion.55
  522.9 57.2 %all-to-all-done.6 = bf16[2,512,1,768]{3,0,2,1:T(2,128)(2,1)} async-done(((bf16[2,512,1,768]{3,0,2,1:T(2,128)(2,1)}), bf16[2,512,1,768]{3,0,2,1:T(2,128)(2,1)}, u32[]{:S(2)}, u32[]{:S(2)}) %all-to-all-start.6) | async-done | bytes 1572896 | tf_op jit(solution)/shard_map/all_to_all | solution.py:215
  580.1 4.5 fusion.53
  584.6 4.8 multiply_subtract_fusion
  589.4 9.3 fusion.21
  606.6 5.6 all-to-all-start.9
  612.3 5.6 fusion.182
  623.6 30.9 %all-to-all-done.9 = bf16[2,64,8,768]{3,1,0,2:T(8,128)(2,1)} async-done(((bf16[2,64,8,768]{3,1,0,2:T(8,128)(2,1)}), bf16[2,64,8,768]{3,1,0,2:T(8,128)(2,1)}, u32[]{:S(2)}, u32[]{:S(2)}) %all-to-all-start.9) | async-done | bytes 1572896 | tf_op jit(solution)/shard_map/all_to_all | solution.py:233
  654.5 4.3 all-to-all-start.8
  662.6 32.8 %all-to-all-done.8 = bf16[2,64,8,768]{3,1,0,2:T(8,128)(2,1)} async-done(((bf16[2,64,8,768]{3,1,0,2:T(8,128)(2,1)}), bf16[2,64,8,768]{3,1,0,2:T(8,128)(2,1)}, u32[]{:S(2)}, u32[]{:S(2)}) %all-to-all-start.8) | async-done | bytes 1572896 | tf_op jit(solution)/shard_map/all_to_all | solution.py:230
  698.1 5.0 fusion.24
  703.2 7.5 multiply_multiply_fusion.6
  710.8 6.8 fusion.11
  720.4 64.0 %collective-permute-done.4 = bf16[2,256,2304]{2,1,0:T(8,128)(2,1)} collective-permute-done((bf16[2,256,2304]{2,1,0:T(8,128)(2,1)}, bf16[2,256,2304]{2,1,0:T(8,128)(2,1)}, u32[]{:S(2)}, u32[]{:S(2)}) %collective-permute-start.4) | collective-permute-done | bytes 2359328 | tf_op jit(solution)/shard_map/ppermute | solution.py:24
  789.4 5.2 collective-permute-start.5
  796.5 97.1 %collective-permute-done.5 = bf16[2,256,2304]{2,1,0:T(8,128)(2,1)S(1)} collective-permute-done((bf16[2,256,2304]{2,1,0:T(8,128)(2,1)S(1)}, bf16[2,256,2304]{2,1,0:T(8,128)(2,1)S(1)}, u32[]{:S(2)}, u32[]{:S(2)}) %collective-permute-start.5) | collective-permute-done | bytes 2359328 | tf_op jit(solution)/shard_map/ppermute | solution.py:24
  896.4 5.0 fusion.396
  906.9 23.9 %all-to-all-start.11 = ((bf16[1,64,8,768]{3,1,0,2:T(8,128)(2,1)}), bf16[1,64,8,768]{3,1,0,2:T(8,128)(2,1)}, u32[]{:S(2)}, u32[]{:S(2)}) async-start(bf16[1,64,8,768]{3,1,0,2:T(8,128)(2,1)} %copy.98), calls=%async_computation.12 | async-start | bytes 1572864 | tf_op jit(solution)/shard_map/all_to_all | solution.py:239
  936.5 8.5 all-to-all-done.11
  957.2 6.1 all-to-all-done.10
  968.6 4.8 fusion.94
  981.6 32.0 %reduce-scatter.9.cloned.1.call-done = f32[96,3072]{1,0:T(8,128)} async-done(((f32[768,3072]{1,0:T(8,128)}), f32[96,3072]{1,0:T(8,128)}) %reduce-scatter.9.cloned.1.call-update) | async-done | bytes 1179664 | tf_op jit(solution)/shard_map/reduce_scatter | solution.py:285
  1015.7 129.5 %reduce-scatter.5.cloned.1.call-done = f32[96,2304]{1,0:T(8,128)} async-done(((f32[768,2304]{1,0:T(8,128)}), f32[96,2304]{1,0:T(8,128)}) %reduce-scatter.5.cloned.1.call-update) | async-done | bytes 884752 | tf_op jit(solution)/shard_map/reduce_scatter | solution.py:283
  1147.3 4.5 multiply_reduce_fusion.2
  1154.9 41.4 %all-reduce.6 = (f32[768]{0:T(1024)}, f32[3,2304]{1,0:T(4,128)}, f32[768]{0:T(1024)}, f32[768]{0:T(1024)}, f32[4]{0:T(128)}) all-reduce(f32[768]{0:T(1024)S(1)} %get-tuple-element.66, f32[3,2304]{1,0:T(4,128)} %pad_maximum_fusion.1, f32[768]{0:T(1024)S(1)} %copy-done.78, ...), channel_id=1, replica_groups=mesh['rows'=4,'seq'=8] {'rows','seq'}, use_global_device_ids=true, to_apply=%region_5.6 | all-reduce | flops 9220 | bytes 73760 | tf_op jit(solution)/shard_map/psum | solution.py:278
  (305 shorter events, 187.6 us)
Async XLA Ops:
  16.1 57.5 %collective-permute-start = (bf16[2,256,2304]{2,1,0:T(8,128)(2,1)}, bf16[2,256,2304]{2,1,0:T(8,128)(2,1)}, u32[]{:S(2)}, u32[]{:S(2)}) collective-permute-start(bf16[2,256,2304]{2,1,0:T(8,128)(2,1)} %bitcast), channel_id=1, source_target_pairs={{7,0},{0,1},{1,2},{2,3},{3,4},{4,5},{5,6},{6,7},{15,8},{8,9},{9,10... | collective-permute-start | bytes 7077896 | tf_op jit(solution)/shard_map/ppermute | solution.py:24
  77.7 95.2 %collective-permute-start.2 = (bf16[2,256,2304]{2,1,0:T(8,128)(2,1)}, bf16[2,256,2304]{2,1,0:T(8,128)(2,1)}, u32[]{:S(2)}, u32[]{:S(2)}) collective-permute-start(bf16[2,256,2304]{2,1,0:T(8,128)(2,1)} %pad_select_fusion.1), channel_id=1, source_target_pairs={{7,0},{0,1},{1,2},{2,3},{3,4},{4,5},{5,6},{6,7},{15,8},{8,9},{9,10... | collective-permute-start | bytes 7077896 | tf_op jit(solution)/shard_map/ppermute | solution.py:24
  77.7 9.0 copy-start.59
  89.6 16.2 %copy-start.72 = (s32[2,256,1]{1,2,0:T(1,128)S(1)}, s32[2,256,1]{1,2,0:T(1,128)}, u32[]{:S(2)}) copy-start(s32[2,256,1]{1,2,0:T(1,128)} %param.14) | copy-start | bytes 6148
  99.8 66.6 %all-to-all-start.2 = ((bf16[8,2,24576]{2,1,0:T(2,128)(2,1)}), bf16[8,2,24576]{2,1,0:T(2,128)(2,1)}, u32[]{:S(2)}, u32[]{:S(2)}) async-start(bf16[8,2,24576]{2,1,0:T(2,128)(2,1)} %reshape.331), calls=%async_computation.2 | async-start | bytes 1572864 | tf_op jit(solution)/shard_map/all_to_all | solution.py:159
  105.8 40.0 %collective-permute-start.1 = (bf16[2,256,1]{1,2,0:T(2,128)(2,1)S(1)}, bf16[2,256,1]{1,2,0:T(2,128)(2,1)S(1)}, u32[]{:S(2)}, u32[]{:S(2)}) collective-permute-start(bf16[2,256,1]{1,2,0:T(2,128)(2,1)S(1)} %convert_element_type.413), channel_id=1, source_target_pairs={{7,0},{0,1},{1,2},{2,3},{3,4},{4,5},{5,6},{6,7},{15,8},{8,9},{9,10... | collective-permute-start | bytes 3080 | tf_op jit(solution)/shard_map/ppermute | solution.py:24
  146.5 18.6 %collective-permute-start.3 = (bf16[2,256,1]{1,2,0:T(2,128)(2,1)}, bf16[2,256,1]{1,2,0:T(2,128)(2,1)}, u32[]{:S(2)}, u32[]{:S(2)}) collective-permute-start(bf16[2,256,1]{1,2,0:T(2,128)(2,1)} %get-tuple-element.90), channel_id=1, source_target_pairs={{7,0},{0,1},{1,2},{2,3},{3,4},{4,5},{5,6},{6,7},{15,8},{8,9},{9,10... | collective-permute-start | bytes 3080 | tf_op jit(solution)/shard_map/ppermute | solution.py:24
  148.2 24.7 %copy-start.55 = (f32[2304]{0:T(1024)}, f32[2304]{0:T(1024)S(1)}, u32[]{:S(2)}) copy-start(f32[2304]{0:T(1024)S(1)} %get-tuple-element.68) | copy-start | bytes 27652
  166.4 27.4 %all-to-all-start.3 = ((bf16[8,2,24576]{2,1,0:T(2,128)(2,1)}), bf16[8,2,24576]{2,1,0:T(2,128)(2,1)}, u32[]{:S(2)}, u32[]{:S(2)}) async-start(bf16[8,2,24576]{2,1,0:T(2,128)(2,1)} %reshape.329), calls=%async_computation.3 | async-start | bytes 1572864 | tf_op jit(solution)/shard_map/all_to_all | solution.py:162
  193.8 42.6 %all-to-all-start.1 = ((bf16[2,512,1,768]{3,0,2,1:T(2,128)(2,1)}), bf16[2,512,1,768]{3,0,2,1:T(2,128)(2,1)}, u32[]{:S(2)}, u32[]{:S(2)}) async-start(bf16[2,512,1,768]{3,0,2,1:T(2,128)(2,1)} %copy.76), calls=%async_computation.1 | async-start | bytes 3145728 | tf_op jit(solution)/shard_map/all_to_all | solution.py:172
  236.4 40.7 %all-to-all-start = ((bf16[2,512,1,768]{3,0,2,1:T(2,128)(2,1)}), bf16[2,512,1,768]{3,0,2,1:T(2,128)(2,1)}, u32[]{:S(2)}, u32[]{:S(2)}) async-start(bf16[2,512,1,768]{3,0,2,1:T(2,128)(2,1)} %copy.73), calls=%async_computation | async-start | bytes 3145728 | tf_op jit(solution)/shard_map/all_to_all | solution.py:169
  286.4 9.1 copy-start.9
  286.5 5.8 copy-start.1
  300.2 40.9 %all-to-all-start.5 = ((bf16[2,64,8,768]{3,1,0,2:T(8,128)(2,1)}), bf16[2,64,8,768]{3,1,0,2:T(8,128)(2,1)}, u32[]{:S(2)}, u32[]{:S(2)}) async-start(bf16[2,64,8,768]{3,1,0,2:T(8,128)(2,1)} %copy.85), calls=%async_computation.5 | async-start | bytes 3145728 | tf_op jit(solution)/shard_map/all_to_all | solution.py:184
  304.5 6.5 copy-start.13
  341.2 40.9 %all-to-all-start.4 = ((bf16[2,64,8,768]{3,1,0,2:T(8,128)(2,1)}), bf16[2,64,8,768]{3,1,0,2:T(8,128)(2,1)}, u32[]{:S(2)}, u32[]{:S(2)}) async-start(bf16[2,64,8,768]{3,1,0,2:T(8,128)(2,1)} %copy.83), calls=%async_computation.4 | async-start | bytes 3145728 | tf_op jit(solution)/shard_map/all_to_all | solution.py:181
  345.5 628.0 %reduce-scatter.7.cloned.1.call-start = ((), (), s32[]{:S(2)}) async-start(), calls=%async_computation.17 | async-start | bytes 2654208 | tf_op jit(solution)/shard_map/reduce_scatter | solution.py:284
  348.3 7.6 copy-start.51
  384.4 13.8 %slice-start = ((s8[4718592]{0:T(1024)(128)(4,1)}), s8[4194304]{0:T(1024)(128)(4,1)S(1)}, s32[]{:S(2)}) async-start(s8[4718592]{0:T(1024)(128)(4,1)} %bitcast.447), calls=%async_computation.21 | async-start | bytes 8388608
  384.5 13.8 %slice-start.4 = ((s8[6291456]{0:T(1024)(128)(4,1)}), s8[4194304]{0:T(1024)(128)(4,1)S(1)}, s32[]{:S(2)}) async-start(s8[6291456]{0:T(1024)(128)(4,1)} %bitcast.451), calls=%async_computation.25 | async-start | bytes 8388608
  389.5 7.9 copy-start.29
  389.5 7.8 copy-start.49
  389.5 8.8 slice-start.1
  389.5 8.8 slice-start.5
  397.3 13.0 %slice-start.2 = ((s8[4718592]{0:T(1024)(128)(4,1)}), s8[4194304]{0:T(1024)(128)(4,1)S(1)}, s32[]{:S(2)}) async-start(s8[4718592]{0:T(1024)(128)(4,1)} %bitcast.449), calls=%async_computation.23 | async-start | bytes 8388608
  398.2 12.1 copy-start.45
  398.3 12.1 slice-start.3
  420.7 558.7 %reduce-scatter.11.cloned.1.call-start = ((), (), s32[]{:S(2)}) async-start(), calls=%async_computation.19 | async-start | bytes 10616832 | tf_op jit(solution)/shard_map/reduce_scatter | solution.py:286
  453.0 50.4 %all-to-all-start.7 = ((bf16[2,512,1,768]{3,0,2,1:T(2,128)(2,1)}), bf16[2,512,1,768]{3,0,2,1:T(2,128)(2,1)}, u32[]{:S(2)}, u32[]{:S(2)}) async-start(bf16[2,512,1,768]{3,0,2,1:T(2,128)(2,1)} %copy.90), calls=%async_computation.7 | async-start | bytes 3145728 | tf_op jit(solution)/shard_map/all_to_all | solution.py:218
  503.5 76.6 %all-to-all-start.6 = ((bf16[2,512,1,768]{3,0,2,1:T(2,128)(2,1)}), bf16[2,512,1,768]{3,0,2,1:T(2,128)(2,1)}, u32[]{:S(2)}, u32[]{:S(2)}) async-start(bf16[2,512,1,768]{3,0,2,1:T(2,128)(2,1)} %copy.87), calls=%async_computation.6 | async-start | bytes 3145728 | tf_op jit(solution)/shard_map/all_to_all | solution.py:215
  507.8 505.8 %reduce-scatter.9.cloned.1.call-start = ((), (), s32[]{:S(2)}) async-start(), calls=%async_computation.18 | async-start | bytes 10616832 | tf_op jit(solution)/shard_map/reduce_scatter | solution.py:285
  580.1 9.3 copy-start.41
  589.3 12.6 %copy-start.15 = (f32[8,2,64,768]{3,0,2,1:T(8,128)}, f32[8,2,64,768]{3,0,2,1:T(8,128)S(1)}, u32[]{:S(2)}) copy-start(f32[8,2,64,768]{3,0,2,1:T(8,128)S(1)} %multiply_subtract_fusion) | copy-start | bytes 9437188
  589.4 9.4 copy-start.3
  589.4 9.4 copy-start.7
  606.6 47.9 %all-to-all-start.9 = ((bf16[2,64,8,768]{3,1,0,2:T(8,128)(2,1)}), bf16[2,64,8,768]{3,1,0,2:T(8,128)(2,1)}, u32[]{:S(2)}, u32[]{:S(2)}) async-start(bf16[2,64,8,768]{3,1,0,2:T(8,128)(2,1)} %copy.95), calls=%async_computation.9 | async-start | bytes 3145728 | tf_op jit(solution)/shard_map/all_to_all | solution.py:233
  612.3 6.7 copy-start.18
  654.5 40.9 %all-to-all-start.8 = ((bf16[2,64,8,768]{3,1,0,2:T(8,128)(2,1)}), bf16[2,64,8,768]{3,1,0,2:T(8,128)(2,1)}, u32[]{:S(2)}, u32[]{:S(2)}) async-start(bf16[2,64,8,768]{3,1,0,2:T(8,128)(2,1)} %copy.93), calls=%async_computation.8 | async-start | bytes 3145728 | tf_op jit(solution)/shard_map/all_to_all | solution.py:230
  658.8 486.4 %reduce-scatter.5.cloned.1.call-start = ((), (), s32[]{:S(2)}) async-start(), calls=%async_computation.16 | async-start | bytes 7962624 | tf_op jit(solution)/shard_map/reduce_scatter | solution.py:283
  703.2 7.6 copy-start.24
  703.2 7.6 copy-start.58
  703.2 7.6 copy-start.69
  703.2 7.6 copy-start.75
  710.8 6.9 copy-start.20
  710.8 6.9 copy-start.22
  717.7 66.8 %collective-permute-start.4 = (bf16[2,256,2304]{2,1,0:T(8,128)(2,1)}, bf16[2,256,2304]{2,1,0:T(8,128)(2,1)}, u32[]{:S(2)}, u32[]{:S(2)}) collective-permute-start(bf16[2,256,2304]{2,1,0:T(8,128)(2,1)} %get-tuple-element.97), channel_id=1, source_target_pairs={{1,0},{2,1},{3,2},{4,3},{5,4},{6,5},{7,6},{0,7},{9,8},{10,9},{11,1... | collective-permute-start | bytes 7077896 | tf_op jit(solution)/shard_map/ppermute | solution.py:24
  720.4 66.2 %copy-start.21 = (f32[2,256,768]{2,1,0:T(8,128)S(1)}, f32[2,256,768]{2,1,0:T(8,128)}, u32[]{:S(2)}) copy-start(f32[2,256,768]{2,1,0:T(8,128)} %copy-done.20) | copy-start | bytes 4718596
  720.4 66.2 %copy-start.23 = (f32[2,256,768]{2,1,0:T(8,128)S(1)}, f32[2,256,768]{2,1,0:T(8,128)}, u32[]{:S(2)}) copy-start(f32[2,256,768]{2,1,0:T(8,128)} %copy-done.22) | copy-start | bytes 4718596
  720.4 66.2 %copy-start.25 = (f32[2,256,768]{2,1,0:T(8,128)S(1)}, f32[2,256,768]{2,1,0:T(8,128)}, u32[]{:S(2)}) copy-start(f32[2,256,768]{2,1,0:T(8,128)} %get-tuple-element.102) | copy-start | bytes 4718596
  720.4 66.2 %copy-start.57 = (f32[2304]{0:T(1024)S(1)}, f32[2304]{0:T(1024)}, u32[]{:S(2)}) copy-start(f32[2304]{0:T(1024)} %get-tuple-element.70) | copy-start | bytes 27652
  786.6 8.1 copy-start.32
  786.6 8.0 copy-start.64
  786.6 8.0 copy-start.82
  789.4 104.2 %collective-permute-start.5 = (bf16[2,256,2304]{2,1,0:T(8,128)(2,1)S(1)}, bf16[2,256,2304]{2,1,0:T(8,128)(2,1)S(1)}, u32[]{:S(2)}, u32[]{:S(2)}) collective-permute-start(bf16[2,256,2304]{2,1,0:T(8,128)(2,1)S(1)} %add_convert_fusion.1), channel_id=1, source_target_pairs={{1,0},{2,1},{3,2},{4,3},{5,4},{6,5},{7,6},{0,7},{9,8},{10,9},{11,1... | collective-permute-start | bytes 7077896 | tf_op jit(solution)/shard_map/ppermute | solution.py:24
  796.5 97.6 %copy-start.56 = (f32[2304]{0:T(1024)S(1)}, f32[2304]{0:T(1024)}, u32[]{:S(2)}) copy-start(f32[2304]{0:T(1024)} %copy-done.55) | copy-start | bytes 27652
  906.9 38.1 %all-to-all-start.11 = ((bf16[1,64,8,768]{3,1,0,2:T(8,128)(2,1)}), bf16[1,64,8,768]{3,1,0,2:T(8,128)(2,1)}, u32[]{:S(2)}, u32[]{:S(2)}) async-start(bf16[1,64,8,768]{3,1,0,2:T(8,128)(2,1)} %copy.98), calls=%async_computation.12 | async-start | bytes 1572864 | tf_op jit(solution)/shard_map/all_to_all | solution.py:239
  935.5 13.8 %copy-start.79 = (s32[2,256,1]{1,2,0:T(1,128)S(1)}, s32[2,256,1]{1,2,0:T(1,128)}, u32[]{:S(2)}) copy-start(s32[2,256,1]{1,2,0:T(1,128)} %param.15) | copy-start | bytes 6148
  945.0 18.3 %all-to-all-start.10 = ((bf16[1,64,8,768]{3,1,0,2:T(8,128)(2,1)}), bf16[1,64,8,768]{3,1,0,2:T(8,128)(2,1)}, u32[]{:S(2)}, u32[]{:S(2)}) async-start(bf16[1,64,8,768]{3,1,0,2:T(8,128)(2,1)} %copy.97), calls=%async_computation.11 | async-start | bytes 1572864 | tf_op jit(solution)/shard_map/all_to_all | solution.py:236
  949.2 253.5 %all-reduce.10.cloned.1.call-start = ((), (), s32[]{:S(2)}) async-start(), calls=%async_computation.20 | async-start | bytes 4325376 | tf_op jit(solution)/shard_map/psum | solution.py:247
  968.6 6.5 copy-start.62
  981.5 165.7 %copy-start.65 = (f32[768]{0:T(1024)S(1)}, f32[768]{0:T(1024)}, u32[]{:S(2)}) copy-start(f32[768]{0:T(1024)} %param.17) | copy-start | bytes 9220
  981.5 165.7 %copy-start.74 = (f32[512]{0:T(512)S(1)}, f32[512]{0:T(512)}, u32[]{:S(2)}) copy-start(f32[512]{0:T(512)} %copy-done.73) | copy-start | bytes 6148
  1202.7 6.2 copy-start.53
  1202.7 7.3 copy-start.52
  (53 other events, 193.5 us)
Sparse Core Ops, SparseCore 0:
  420.8 80.9 reduce-scatter.6
  505.4 242.8 reduce-scatter.10
  751.8 261.6 reduce-scatter.8
  1017.1 128.0 reduce-scatter.4
  1149.1 53.5 all-reduce.9
where the time goes:
time: 1230 us; the launch traced here: 1220 us
  waiting for transfers between devices  683 us (56%)
  matrix products  220 us (18%)
  starting transfers between devices  93.8 us (8%)
  other arithmetic  82.7 us (7%)
  local copies, waits for them, and re-layouts  80.1 us (7%)
  blocking collectives  41.4 us (3%)
  between operations  16.2 us (1%)
    ppermute x6, waiting for transfers between devices, passed_along(): return lax.ppermute(block, axis, route)  254 us
    reduce_scatter x1, waiting for transfers between devices, local(): lax.psum_scatter(grad_inp, 'seq', scatter_dimension=0, tiled=True)  130 us
    all_to_all x1, waiting for transfers between devices, local(): lax.all_to_all(back_re.astype(jnp.bfloat16), 'seq', split_axis=1, concat_...  57.2 us
    unnamed x205, local copies, waits for them, and re-layouts  47 us
    all_to_all x1, waiting for transfers between devices, local(): lax.all_to_all(back_im.astype(jnp.bfloat16), 'seq', split_axis=1, concat_...  41.9 us
    psum x1, blocking collectives, local(): lax.psum((grad_gain_one, grad_gain_two, grad_tap_rows, grad_skip, stat_su...  41.4 us
    all_to_all x1, waiting for transfers between devices, local(): lax.all_to_all(sig_re.astype(jnp.bfloat16), 'seq', split_axis=2, concat_a...  32.8 us
    reduce_scatter x1, waiting for transfers between devices, local(): lax.psum_scatter(grad_up, 'seq', scatter_dimension=0, tiled=True)  32 us
  transfers between devices with their start and end apart: 23, of which 17 were waited for; matrix products, arithmetic and copies ran while one was open for 24% of the time, Pallas kernels for 0%

commit v1 on v0

--- a/solution.py
+++ b/solution.py
@@ -1,8 +1,12 @@
+import functools
 import math
 
 import jax
 import jax.numpy as jnp
+import numpy as np
 from jax import lax
+from jax.experimental import pallas as pl
+from jax.experimental.pallas import tpu as pltpu
 from jax.sharding import PartitionSpec as P
 
 EPS = 1e-05
@@ -106,7 +110,7 @@
     )
 
 
-def local(
+def general_local(
     block_in,
     segment_ids,
     valid_mask,
@@ -307,9 +311,756 @@
     )
 
 
+MESH = pl.DeviceIdType.MESH
+F32 = jnp.float32
+BF16 = jnp.bfloat16
+VMEM_BYTES = 60 * 1024 * 1024
+ROOT_HALF = math.sqrt(0.5)
+C0 = math.sqrt(2.0 / math.pi)
+C1 = 0.044715
+
+
+def dot_nn(a, b):
+    return lax.dot_general(a, b, (((1,), (0,)), ((), ())), preferred_element_type=F32)
+
+
+def dot_nt(a, b):
+    return lax.dot_general(a, b, (((1,), (1,)), ((), ())), preferred_element_type=F32)
+
+
+def fft_points(re, im, sign):
+    n = len(re)
+    if n == 1:
+        return re, im
+    even_r, even_i = fft_points(re[0::2], im[0::2], sign)
+    odd_r, odd_i = fft_points(re[1::2], im[1::2], sign)
+    out_r, out_i = [None] * n, [None] * n
+    for k in range(n // 2):
+        if k == 0:
+            turn_r, turn_i = odd_r[0], odd_i[0]
+        elif 4 * k == n:
+            if sign > 0:
+                out_r[k], out_i[k] = even_r[k] - odd_i[k], even_i[k] + odd_r[k]
+                out_r[k + n // 2], out_i[k + n // 2] = even_r[k] + odd_i[k], even_i[k] - odd_r[k]
+            else:
+                out_r[k], out_i[k] = even_r[k] + odd_i[k], even_i[k] - odd_r[k]
+                out_r[k + n // 2], out_i[k + n // 2] = even_r[k] - odd_i[k], even_i[k] + odd_r[k]
+            continue
+        else:
+            cos, sin = math.cos(2 * math.pi * k / n), sign * math.sin(2 * math.pi * k / n)
+            turn_r = cos * odd_r[k] - sin * odd_i[k]
+            turn_i = cos * odd_i[k] + sin * odd_r[k]
+        out_r[k], out_i[k] = even_r[k] + turn_r, even_i[k] + turn_i
+        out_r[k + n // 2], out_i[k + n // 2] = even_r[k] - turn_r, even_i[k] - turn_i
+    return out_r, out_i
+
+
+def spectrum_tables(blocks, phases):
+    length = blocks * phases
+    b = np.arange(blocks)[:, None]
+    k = np.arange(blocks)[None, :]
+    angle = 2.0 * np.pi * b * (2 * k + 1) / (4.0 * blocks)
+    forward = np.concatenate([np.cos(angle), -np.sin(angle)], axis=1)
+    inverse = np.concatenate([np.cos(angle).T, -np.sin(angle).T], axis=0) / length
+    p = np.arange(phases)[:, None]
+    turn = 2.0 * np.pi * p * (2 * k + 1) / (4.0 * length)
+    turns = np.stack([np.cos(turn), np.sin(turn)], axis=1)[:, :, None, :]
+    turns = np.broadcast_to(turns, (phases, 2, 8, blocks))
+    return (
+        jnp.asarray(forward, BF16),
+        jnp.asarray(inverse, BF16),
+        jnp.asarray(turns, F32),
+    )
+
+
+def greet(n):
+    me = lax.axis_index("seq")
+    barrier = pltpu.get_barrier_semaphore()
+    for j in range(1, n):
+        pl.semaphore_signal(
+            barrier, inc=1, device_id={"seq": lax.rem(me + j, n)}, device_id_type=MESH
+        )
+    return barrier
+
+
+def all_peers(n, start):
+    me = lax.axis_index("seq")
+    for j in range(1, n):
+        start(lax.rem(me + j, n), j)
+
+
+def to_peer(src, dst, send_sem, recv_sem, peer):
+    return pltpu.make_async_remote_copy(
+        src_ref=src,
+        dst_ref=dst,
+        send_sem=send_sem,
+        recv_sem=recv_sem,
+        device_id={"seq": peer},
+        device_id_type=MESH,
+    )
+
+
+def in_kernel(
+    n, x, w, gain, taps, marks,
+    got, got_taps, got_marks, turned,
+    sent, sent_taps, normed, send_sem, recv_sem, small_send, small_recv,
+):
+    me = lax.axis_index("seq")
+    rows, blocks = got.shape[0], got.shape[4]
+    width = x.shape[1]
+    each = width // n
+    mine = pl.ds(pl.multiple_of(me * each, each), each)
+    barrier = greet(n)
+    raw = taps[...]
+    sent_taps[...] = (raw - THRESH * jnp.tanh(raw * (1.0 / THRESH))).T.astype(BF16)
+    pl.semaphore_wait(barrier, n - 1)
+
+    def small_copies(peer, j):
+        part = pl.ds(pl.multiple_of(peer * each, each), each)
+        return (
+            to_peer(marks, got_marks.at[me], small_send.at[0, j], small_recv.at[0, me], peer),
+            to_peer(sent_taps.at[part], got_taps.at[me], small_send.at[1, j], small_recv.at[1, me], peer),
+        )
+
+    def start_small(peer, j):
+        for copy in small_copies(peer, j):
+            copy.start()
+
+    all_peers(n, start_small)
+    got_marks[me] = marks[...]
+    got_taps[me] = sent_taps[mine]
+    for at in range(0, x.shape[0], 128):
+        part = x[at:at + 128, :]
+        scale = lax.rsqrt(jnp.mean(part * part, axis=-1, keepdims=True) + EPS)
+        normed[at:at + 128, :] = (part * scale * gain[...]).astype(BF16)
+
+    def big_copy(r, c, peer, j):
+        part = pl.ds(pl.multiple_of(peer * each, each), each)
+        return to_peer(
+            sent.at[r, c, part], got.at[r, c, me + 2],
+            send_sem.at[r, c, j], recv_sem.at[r, c, me], peer,
+        )
+
+    for r in range(rows):
+        tokens = normed[r * blocks:(r + 1) * blocks, :]
+        for c in (1, 2, 0):
+            for at in range(0, width, 256):
+                piece = dot_nn(tokens, w[:, c * width + at:c * width + at + 256])
+                sent[r, c, at:at + 256, :] = piece.T.astype(BF16)
+            all_peers(n, lambda peer, j: big_copy(r, c, peer, j).start())
+            got[r, c, me + 2] = sent[r, c, mine]
+    for r in range(rows):
+        tokens = normed[r * blocks:(r + 1) * blocks, :]
+        turned[r] = tokens.T
+
+    def wait_small(peer, j):
+        part = pl.ds(pl.multiple_of(peer * each, each), each)
+        to_peer(marks, got_marks.at[peer], small_send.at[0, j], small_recv.at[0, peer], peer).wait()
+        to_peer(sent_taps.at[part], got_taps.at[peer], small_send.at[1, j], small_recv.at[1, peer], peer).wait()
+
+    all_peers(n, wait_small)
+    for r in range(rows):
+        for c in (1, 2, 0):
+            def wait_big(peer, j):
+                part = pl.ds(pl.multiple_of(peer * each, each), each)
+                to_peer(
+                    sent.at[r, c, part], got.at[r, c, peer + 2],
+                    send_sem.at[r, c, j], recv_sem.at[r, c, peer], peer,
+                ).wait()
+
+            all_peers(n, wait_big)
+            for slot in range(2):
+                before = got[r, c, n + slot].astype(F32)
+                got[r, c, slot] = pltpu.roll(before, 1, 1).astype(BF16)
+
+
+def short_conv(got, cols, same, r, c, p, rows):
+    now = got[r, c, p + 2, rows, :].astype(F32)
+    one = got[r, c, p + 1, rows, :].astype(F32) * same[0, p, r:r + 1, :]
+    two = got[r, c, p, rows, :].astype(F32) * same[1, p, r:r + 1, :]
+    value = cols[3 * c, rows, :] * now + cols[3 * c + 1, rows, :] * one + cols[3 * c + 2, rows, :] * two
+    return value, (now, one, two)
+
+
+def spread_cols(cols_in, cols):
+    shape = cols.shape[1:]
+    for i in range(cols.shape[0]):
+        cols[i] = jnp.broadcast_to(cols_in[:, i:i + 1], shape)
+
+
+def to_frequency(source, table, spec):
+    for at in range(0, source.shape[0], 256):
+        spec[at:at + 256, :] = dot_nn(source[at:at + 256, :].astype(BF16), table[...])
+
+
+def load_phases(spec, n, each, at, lane, half):
+    re = [spec[pl.ds(p * each + at, 8), lane:lane + 128] for p in range(n)]
+    im = [spec[pl.ds(p * each + at, 8), half + lane:half + lane + 128] for p in range(n)]
+    return re, im
+
+
+def turn_phases(re, im, turns, lane, sign):
+    out_r, out_i = [re[0]], [im[0]]
+    for p in range(1, len(re)):
+        cos = turns[p, 0, :, lane:lane + 128]
+        sin = turns[p, 1, :, lane:lane + 128]
+        if sign > 0:
+            out_r.append(re[p] * cos - im[p] * sin)
+            out_i.append(im[p] * cos + re[p] * sin)
+        else:
+            out_r.append(re[p] * cos + im[p] * sin)
+            out_i.append(im[p] * cos - re[p] * sin)
+    return out_r, out_i
+
+
+def over_groups(each, blocks, body):
+    for lane in range(0, blocks, 128):
+        def step(g, carry):
+            body(pl.multiple_of(g * 8, 8), lane)
+            return carry
+        lax.fori_loop(0, each // 8, step, 0)
+
+
+def conv_kernel(
+    n, got, got_taps, got_marks, cols_in, table, inverse, turns,
+    mixed, same, spec_taps, spec_gate, gated, long_out,
+    cols, spec, sent, send_sem, recv_sem,
+):
+    me = lax.axis_index("seq")
+    rows, each, blocks = got.shape[0], got.shape[3], got.shape[4]
+    mine = pl.ds(pl.multiple_of(me * each, each), each)
+    barrier = greet(n)
+    spread_cols(cols_in, cols)
+    first_lane = lax.broadcasted_iota(jnp.int32, (rows, blocks), 1) == 0
+    seg = [got_marks[p, 0:rows, :] for p in range(n)]
+    mask = [got_marks[p, rows:2 * rows, :].astype(F32) for p in range(n)]
+    wrapped = [pltpu.roll(seg[n - 2], 1, 1), pltpu.roll(seg[n - 1], 1, 1)]
+    before = wrapped + seg
+    for p in range(n):
+        one = (before[p + 1] == seg[p]).astype(F32)
+        two = (before[p] == seg[p]).astype(F32)
+        if p < 1:
+            one = jnp.where(first_lane, 0.0, one)
+        if p < 2:
+            two = jnp.where(first_lane, 0.0, two)
+        same[0, p] = one
+        same[1, p] = two
+        same[2, p] = mask[p]
+        if p < 2:
+            same[0, n + p] = pltpu.roll(one, blocks - 1, 1)
+            same[1, n + p] = pltpu.roll(two, blocks - 1, 1)
+            same[2, n + p] = jnp.zeros_like(one)
+
+    for p in range(n):
+        spec[p * each:(p + 1) * each, :] = dot_nn(got_taps[p], table[...])
+
+    def taps_group(at, lane):
+        re, im = load_phases(spec, n, each, at, lane, blocks)
+        re, im = turn_phases(re, im, turns, lane, -1)
+        re, im = fft_points(re, im, -1)
+        for k in range(n):
+            spec_taps[k, 0, pl.ds(at, 8), lane:lane + 128] = re[k]
+            spec_taps[k, 1, pl.ds(at, 8), lane:lane + 128] = im[k]
+
+    over_groups(each, blocks, taps_group)
+    pl.semaphore_wait(barrier, n - 1)
+
+    for r in range(rows):
+        def gate_step(p, carry):
+            for at in range(0, each, 32):
+                part = pl.ds(at, 32)
+                keys, _ = short_conv(got, cols, same, r, 1, p, part)
+                values, _ = short_conv(got, cols, same, r, 2, p, part)
+                gated[r, p, part, :] = keys * values * same[2, p, r:r + 1, :]
+            return carry
+
+        lax.fori_loop(0, n, gate_step, 0)
+        for p in range(n):
+            spec[p * each:(p + 1) * each, :] = dot_nn(gated[r, p].astype(BF16), table[...])
+
+        def product_group(at, lane):
+            re, im = load_phases(spec, n, each, at, lane, blocks)
+            re, im = turn_phases(re, im, turns, lane, -1)
+            re, im = fft_points(re, im, -1)
+            out_r, out_i = [], []
+            for k in range(n):
+                spec_gate[r, k, 0, pl.ds(at, 8), lane:lane + 128] = re[k]
+                spec_gate[r, k, 1, pl.ds(at, 8), lane:lane + 128] = im[k]
+                tap_r = spec_taps[k, 0, pl.ds(at, 8), lane:lane + 128]
+                tap_i = spec_taps[k, 1, pl.ds(at, 8), lane:lane + 128]
+                out_r.append(re[k] * tap_r - im[k] * tap_i)
+                out_i.append(re[k] * tap_i + im[k] * tap_r)
+            re, im = fft_points(out_r, out_i, 1)
+            re, im = turn_phases(re, im, turns, lane, 1)
+            for p in range(n):
+                spec[pl.ds(p * each + at, 8), lane:lane + 128] = re[p]
+                spec[pl.ds(p * each + at, 8), blocks + lane:blocks + lane + 128] = im[p]
+
+        over_groups(each, blocks, product_group)
+        for p in range(n):
+            long_out[r, p] = dot_nn(spec[p * each:(p + 1) * each, :].astype(BF16), inverse[...])
+
+        def mix_step(p, carry):
+            for at in range(0, each, 32):
+                part = pl.ds(at, 32)
+                query, _ = short_conv(got, cols, same, r, 0, p, part)
+                total = long_out[r, p, part, :] + cols[9, part, :] * gated[r, p, part, :]
+                long_out[r, p, part, :] = total
+                sent[r, p, part, :] = (query * total).astype(BF16)
+            return carry
+
+        lax.fori_loop(0, n, mix_step, 0)
+        all_peers(n, lambda peer, j: to_peer(
+            sent.at[r, peer], mixed.at[r, mine], send_sem.at[r, j], recv_sem.at[r, me], peer,
+        ).start())
+        mixed[r, mine] = sent[r, me]
+
+    for r in range(rows):
+        def wait(peer, j):
+            part = pl.ds(pl.multiple_of(peer * each, each), each)
+            to_peer(
+                sent.at[r, peer], mixed.at[r, part], send_sem.at[r, j], recv_sem.at[r, peer], peer,
+            ).wait()
+
+        all_peers(n, wait)
+
+
+def mlp_kernel(
+    n, chunk, mixed, x, cot, mask_col, w_out, gain, w_up, w_down,
+    out, back, mid, share_up, share_down, share_out, gain_sum, stats,
+    resid, normed, act, grad_act, acc_out, acc_back, turned, turned_cot, mix_back, sent, send_sem, recv_sem,
+):
+    me = lax.axis_index("seq")
+    rows, blocks = mixed.shape[0], mixed.shape[2]
+    width, hidden = w_up.shape
+    each = width // n
+    mine = pl.ds(pl.multiple_of(me * each, each), each)
+    barrier = greet(n)
+    gain_sum[...] = jnp.zeros_like(gain_sum)
+    stat_out = jnp.zeros((1, width), F32)
+    stat_mix = jnp.zeros((1, width), F32)
+    stat_mlp = jnp.zeros((1, width), F32)
+    for r in range(rows):
+        tokens = slice(r * blocks, (r + 1) * blocks)
+        mask = mask_col[tokens, :]
+        mixer = dot_nn(mixed[r].T, w_out[...])
+        stat_mix += jnp.sum(mixer * mixer * mask, axis=0, keepdims=True)
+        middle = x[tokens, :] + mixer
+        resid[...] = middle
+        scale = lax.rsqrt(jnp.mean(middle * middle, axis=-1, keepdims=True) + EPS)
+        normed[...] = (middle * scale * gain[...]).astype(BF16)
+        turned[:, tokens] = normed[...].T
+        cot_low = cot[tokens, :].astype(BF16)
+        turned_cot[:, tokens] = cot_low.T
+        acc_out[...] = jnp.zeros_like(acc_out)
+        acc_back[...] = jnp.zeros_like(acc_back)
+
+        def hidden_step(j, carry):
+            cols = pl.ds(pl.multiple_of(j * chunk, chunk), chunk)
+            up = dot_nn(normed[...], w_up[:, cols])
+            square = up * up
+            tanh = jnp.tanh(up * (C0 + (C0 * C1) * square))
+            half = 0.5 * (1.0 + tanh)
+            act_low = (up * half).astype(BF16)
+            slope = half + (0.5 * up) * (1.0 - tanh * tanh) * (C0 + (3.0 * C0 * C1) * square)
+            act[tokens, cols] = act_low
+            acc_out[...] += dot_nn(act_low, w_down[cols, :])
+            grad = dot_nt(cot[tokens, :].astype(BF16), w_down[cols, :])
+            grad_low = (grad * slope).astype(BF16)
+            grad_act[tokens, cols] = grad_low
+            acc_back[...] += dot_nt(grad_low, w_up[:, cols])
+            return carry
+
+        lax.fori_loop(0, hidden // chunk, hidden_step, 0)
+        middle = resid[...]
+        mlp = acc_out[...]
+        stat_mlp += jnp.sum(mlp * mlp * mask, axis=0, keepdims=True)
+        whole = middle + mlp
+        stat_out += jnp.sum(whole * whole * mask, axis=0, keepdims=True)
+        out[tokens, :] = whole
+        scale = lax.rsqrt(jnp.mean(middle * middle, axis=-1, keepdims=True) + EPS)
+        grad = acc_back[...]
+        gain_sum[...] += jnp.sum(grad * middle * scale, axis=0, keepdims=True)
+        scaled = grad * gain[...]
+        shift = jnp.mean(scaled * middle, axis=-1, keepdims=True) * (scale * scale * scale)
+        grad_mid = cot[tokens, :] + scaled * scale - middle * shift
+        mid[tokens, :] = grad_mid
+        mix_back[r] = grad_mid.astype(BF16)
+        sent[r] = dot_nt(w_out[...], mix_back[r]).astype(BF16)
+        if r == 0:
+            pl.semaphore_wait(barrier, n - 1)
+
+        def start(peer, j):
+            part = pl.ds(pl.multiple_of(peer * each, each), each)
+            to_peer(
+                sent.at[r, part], back.at[r, me], send_sem.at[r, j], recv_sem.at[r, me], peer,
+            ).start()
+
+        all_peers(n, start)
+        back[r, me] = sent[r, mine]
+
+    stats[0:1, :] = stat_out
+    stats[1:2, :] = stat_mix
+    stats[2:3, :] = stat_mlp
+    stats[3:4, :] = jnp.broadcast_to(
+        jnp.sum(mask_col[...], axis=0, keepdims=True) * (1.0 / width), (1, width)
+    )
+    stats[4:8, :] = jnp.zeros((4, width), F32)
+    share_out[...] = sum(dot_nn(mixed[r], mix_back[r]) for r in range(rows)).astype(BF16)
+
+    def weight_step(j, carry):
+        cols = pl.ds(pl.multiple_of(j * chunk, chunk), chunk)
+        share_up[:, cols] = dot_nn(turned[...], grad_act[:, cols]).astype(BF16)
+        share_down[:, cols] = dot_nn(turned_cot[...], act[:, cols]).astype(BF16)
+        return carry
+
+    lax.fori_loop(0, hidden // chunk, weight_step, 0)
+    for r in range(rows):
+        def wait(peer, j):
+            part = pl.ds(pl.multiple_of(peer * each, each), each)
+            to_peer(
+                sent.at[r, part], back.at[r, peer], send_sem.at[r, j], recv_sem.at[r, peer], peer,
+            ).wait()
+
+        all_peers(n, wait)
+
+
+def back_kernel(
+    n, back, got, same, spec_taps, spec_gate, gated, long_out, cols_in, table, inverse, turns,
+    got_back, grad_taps, col_sums,
+    cols, sums, spec, spec_sum, grad_long, short, sent, send_sem, recv_sem,
+):
+    me = lax.axis_index("seq")
+    rows, each, blocks = got.shape[0], got.shape[3], got.shape[4]
+    mine = pl.ds(pl.multiple_of(me * each, each), each)
+    barrier = greet(n)
+    spread_cols(cols_in, cols)
+    sums[...] = jnp.zeros_like(sums)
+    spec_sum[...] = jnp.zeros_like(spec_sum)
+
+    def tap_sums(c, part, grad, inputs):
+        for i in range(3):
+            sums[3 * c + i, part, :] += grad * inputs[i]
+
+    def spread_back(r, c):
+        for slot in range(2):
+            short[c, n + slot] = pltpu.roll(short[c, slot], blocks - 1, 1)
+
+        def step(p, carry):
+            for at in range(0, each, 32):
+                part = pl.ds(at, 32)
+                value = cols[3 * c, part, :] * short[c, p, part, :]
+                value += cols[3 * c + 1, part, :] * (short[c, p + 1, part, :] * same[0, p + 1, r:r + 1, :])
+                value += cols[3 * c + 2, part, :] * (short[c, p + 2, part, :] * same[1, p + 2, r:r + 1, :])
+                sent[r, c, p, part, :] = value.astype(BF16)
+            return carry
+
+        lax.fori_loop(0, n, step, 0)
+        all_peers(n, lambda peer, j: to_peer(
+            sent.at[r, c, peer], got_back.at[r, c, mine], send_sem.at[r, c, j], recv_sem.at[r, c, me], peer,
+        ).start())
+        got_back[r, c, mine] = sent[r, c, me]
+
+    for r in range(rows):
+        def query_step(p, carry):
+            for at in range(0, each, 32):
+                part = pl.ds(at, 32)
+                grad = back[r, p, part, :].astype(F32)
+                query, inputs = short_conv(got, cols, same, r, 0, p, part)
+                grad_query = grad * long_out[r, p, part, :]
+                value = grad * query
+                grad_long[p, part, :] = value
+                short[0, p, part, :] = grad_query
+                tap_sums(0, part, grad_query, inputs)
+                sums[9, part, :] += value * gated[r, p, part, :]
+            return carry
+
+        lax.fori_loop(0, n, query_step, 0)
+        if r == 0:
+            pl.semaphore_wait(barrier, n - 1)
+        spread_back(r, 0)
+        for p in range(n):
+            spec[p * each:(p + 1) * each, :] = dot_nn(grad_long[p].astype(BF16), table[...])
+
+        def product_group(at, lane):
+            re, im = load_phases(spec, n, each, at, lane, blocks)
+            re, im = turn_phases(re, im, turns, lane, -1)
+            re, im = fft_points(re, im, -1)
+            out_r, out_i = [], []
+            for k in range(n):
+                here = (pl.ds(at, 8), slice(lane, lane + 128))
+                tap_r, tap_i = spec_taps[(k, 0) + here], spec_taps[(k, 1) + here]
+                gate_r, gate_i = spec_gate[(r, k, 0) + here], spec_gate[(r, k, 1) + here]
+                spec_sum[(k, 0) + here] += gate_r * re[k] + gate_i * im[k]
+                spec_sum[(k, 1) + here] += gate_r * im[k] - gate_i * re[k]
+                out_r.append(tap_r * re[k] + tap_i * im[k])
+                out_i.append(tap_r * im[k] - tap_i * re[k])
+            re, im = fft_points(out_r, out_i, 1)
+            re, im = turn_phases(re, im, turns, lane, 1)
+            for p in range(n):
+                spec[pl.ds(p * each + at, 8), lane:lane + 128] = re[p]
+                spec[pl.ds(p * each + at, 8), blocks + lane:blocks + lane + 128] = im[p]
+
+        over_groups(each, blocks, product_group)
+        for p in range(n):
+            short[0, p] = dot_nn(spec[p * each:(p + 1) * each, :].astype(BF16), inverse[...])
+
+        def gate_step(p, carry):
+            for at in range(0, each, 32):
+                part = pl.ds(at, 32)
+                keys, key_inputs = short_conv(got, cols, same, r, 1, p, part)
+                values, value_inputs = short_conv(got, cols, same, r, 2, p, part)
+                grad = short[0, p, part, :] + cols[9, part, :] * grad_long[p, part, :]
+                grad = grad * same[2, p, r:r + 1, :]
+                grad_keys = grad * values
+                grad_values = grad * keys
+                short[1, p, part, :] = grad_keys
+                short[2, p, part, :] = grad_values
+                tap_sums(1, part, grad_keys, key_inputs)
+                tap_sums(2, part, grad_values, value_inputs)
+            return carry
+
+        lax.fori_loop(0, n, gate_step, 0)
+        spread_back(r, 1)
+        spread_back(r, 2)
+
+    def taps_group(at, lane):
+        here = (pl.ds(at, 8), slice(lane, lane + 128))
+        re = [spec_sum[(k, 0) + here] for k in range(n)]
+        im = [spec_sum[(k, 1) + here] for k in range(n)]
+        re, im = fft_points(re, im, 1)
+        re, im = turn_phases(re, im, turns, lane, 1)
+        for p in range(n):
+            spec[pl.ds(p * each + at, 8), lane:lane + 128] = re[p]
+            spec[pl.ds(p * each + at, 8), blocks + lane:blocks + lane + 128] = im[p]
+
+    over_groups(each, blocks, taps_group)
+    for p in range(n):
+        grad_taps[p] = dot_nn(spec[p * each:(p + 1) * each, :].astype(BF16), inverse[...])
+    lanes = lax.broadcasted_iota(jnp.int32, col_sums.shape, 1)
+    total = jnp.zeros(col_sums.shape, F32)
+    for i in range(sums.shape[0]):
+        total = jnp.where(lanes == i, jnp.sum(sums[i], axis=-1, keepdims=True), total)
+    col_sums[...] = total
+    for r in range(rows):
+        for c in range(3):
+            def wait(peer, j):
+                part = pl.ds(pl.multiple_of(peer * each, each), each)
+                to_peer(
+                    sent.at[r, c, peer], got_back.at[r, c, part], send_sem.at[r, c, j], recv_sem.at[r, c, peer], peer,
+                ).wait()
+
+            all_peers(n, wait)
+
+
+def final_kernel(got_back, turned, w_in, x, mid, gain, grad_in, share_in, gain_sum):
+    rows, parts, width, blocks = got_back.shape
+    gain_sum[...] = jnp.zeros_like(gain_sum)
+    for r in range(rows):
+        tokens = slice(r * blocks, (r + 1) * blocks)
+        grad = sum(
+            dot_nn(w_in[:, c * width:(c + 1) * width], got_back[r, c]) for c in range(parts)
+        ).T
+        value = x[tokens, :]
+        scale = lax.rsqrt(jnp.mean(value * value, axis=-1, keepdims=True) + EPS)
+        gain_sum[...] += jnp.sum(grad * value * scale, axis=0, keepdims=True)
+        scaled = grad * gain[...]
+        shift = jnp.mean(scaled * value, axis=-1, keepdims=True) * (scale * scale * scale)
+        grad_in[tokens, :] = mid[tokens, :] + scaled * scale - value * shift
+    for c in range(parts):
+        for at in range(0, width, 256):
+            share_in[:, c * width + at:c * width + at + 256] = sum(
+                dot_nt(turned[r], got_back[r, c, at:at + 256, :]) for r in range(rows)
+            ).astype(BF16)
+
+
+def vmem(count):
+    return [pl.BlockSpec(memory_space=pltpu.VMEM)] * count
+
+
+def call(body, outs, scratch, inputs, collective_id=None):
+    extra = {}
+    if collective_id is not None:
+        extra = dict(collective_id=collective_id, has_side_effects=True)
+    return pl.pallas_call(
+        body,
+        out_shape=tuple(jax.ShapeDtypeStruct(*out) for out in outs),
+        in_specs=vmem(len(inputs)),
+        out_specs=tuple(vmem(len(outs))),
+        scratch_shapes=scratch,
+        compiler_params=pltpu.CompilerParams(vmem_limit_bytes=VMEM_BYTES, **extra),
+    )(*inputs)
+
+
+def local(
+    block_in, segment_ids, valid_mask, cotangent, gain_mix, in_proj, short_taps, long_kernel,
+    skip_gain, out_proj, gain_mlp, up_proj, down_proj,
+):
+    rows, blocks, _, width = block_in.shape
+    hidden = up_proj.shape[1]
+    n = lax.axis_size("seq")
+    me = lax.axis_index("seq")
+    each = width // n
+    tokens = rows * blocks
+    x = block_in.reshape(tokens, width)
+    cot = cotangent.reshape(tokens, width)
+    raw = long_kernel[:, 0, :]
+    marks = jnp.concatenate(
+        [segment_ids[:, :, 0], valid_mask[:, :, 0], jnp.zeros((8 - 2 * rows, blocks), jnp.int32)]
+    )
+    own = lax.dynamic_slice_in_dim(
+        jnp.concatenate([short_taps.reshape(3, 3, width), jnp.broadcast_to(skip_gain, (1, 3, width))]),
+        me * each, each, axis=2,
+    )
+    cols_in = jnp.concatenate([own[:3, c] for c in range(3)] + [own[3, :1]]).T
+    cols_in = jnp.pad(cols_in, ((0, 0), (0, 128 - cols_in.shape[1])))
+    table, inverse, turns = spectrum_tables(blocks, n)
+    dma = pltpu.SemaphoreType.DMA
+
+    got, got_taps, got_marks, turned = call(
+        functools.partial(in_kernel, n),
+        [
+            ((rows, 3, n + 2, each, blocks), BF16),
+            ((n, each, blocks), BF16),
+            ((n,) + marks.shape, jnp.int32),
+            ((rows, width, blocks), BF16),
+        ],
+        [
+            pltpu.VMEM((rows, 3, width, blocks), BF16),
+            pltpu.VMEM((width, blocks), BF16),
+            pltpu.VMEM((tokens, width), BF16),
+            dma((rows, 3, n)), dma((rows, 3, n)), dma((2, n)), dma((2, n)),
+        ],
+        (x, in_proj, gain_mix[None], raw, marks),
+        1,
+    )
+    mixed, same, spec_taps, spec_gate, gated, long_out = call(
+        functools.partial(conv_kernel, n),
+        [
+            ((rows, width, blocks), BF16),
+            ((3, n + 2, rows, blocks), F32),
+            ((n, 2, each, blocks), F32),
+            ((rows, n, 2, each, blocks), F32),
+            ((rows, n, each, blocks), F32),
+            ((rows, n, each, blocks), F32),
+        ],
+        [
+            pltpu.VMEM((10, each, blocks), F32),
+            pltpu.VMEM((width, 2 * blocks), F32),
+            pltpu.VMEM((rows, n, each, blocks), BF16),
+            dma((rows, n)), dma((rows, n)),
+        ],
+        (got, got_taps, got_marks, cols_in, table, inverse, turns),
+        2,
+    )
+    mask_col = valid_mask[:, :, 0].astype(F32).reshape(tokens, 1)
+    chunk = 512
+    block_out, back, mid, share_up, share_down, share_out, gain_two, stats = call(
+        functools.partial(mlp_kernel, n, chunk),
+        [
+            ((tokens, width), F32),
+            ((rows, n, each, blocks), BF16),
+            ((tokens, width), F32),
+            ((width, hidden), BF16),
+            ((width, hidden), BF16),
+            ((width, width), BF16),
+            ((1, width), F32),
+            ((8, width), F32),
+        ],
+        [
+            pltpu.VMEM((blocks, width), F32),
+            pltpu.VMEM((blocks, width), BF16),
+            pltpu.VMEM((tokens, hidden), BF16),
+            pltpu.VMEM((tokens, hidden), BF16),
+            pltpu.VMEM((blocks, width), F32),
+            pltpu.VMEM((blocks, width), F32),
+            pltpu.VMEM((width, tokens), BF16),
+            pltpu.VMEM((width, tokens), BF16),
+            pltpu.VMEM((rows, blocks, width), BF16),
+            pltpu.VMEM((rows, width, blocks), BF16),
+            dma((rows, n)), dma((rows, n)),
+        ],
+        (mixed, x, cot, mask_col, out_proj, gain_mlp[None], up_proj, down_proj),
+        3,
+    )
+    got_back, grad_taps, col_sums = call(
+        functools.partial(back_kernel, n),
+        [
+            ((rows, 3, width, blocks), BF16),
+            ((n, each, blocks), F32),
+            ((each, 128), F32),
+        ],
+        [
+            pltpu.VMEM((10, each, blocks), F32),
+            pltpu.VMEM((10, each, blocks), F32),
+            pltpu.VMEM((width, 2 * blocks), F32),
+            pltpu.VMEM((n, 2, each, blocks), F32),
+            pltpu.VMEM((n, each, blocks), F32),
+            pltpu.VMEM((3, n + 2, each, blocks), F32),
+            pltpu.VMEM((rows, 3, n, each, blocks), BF16),
+            dma((rows, 3, n)), dma((rows, 3, n)),
+        ],
+        (back, got, same, spec_taps, spec_gate, gated, long_out, cols_in, table, inverse, turns),
+        4,
+    )
+    grad_flat, share_in, gain_one = call(
+        final_kernel,
+        [((tokens, width), F32), ((width, 3 * width), BF16), ((1, width), F32)],
+        [],
+        (got_back, turned, in_proj, x, mid, gain_mix[None]),
+    )
+
+    def summed(share):
+        quarter = lax.psum_scatter(share, "rows", scatter_dimension=1, tiled=True)
+        own_rows = lax.psum_scatter(quarter, "seq", scatter_dimension=0, tiled=True)
+        return lax.all_gather(own_rows, "rows", axis=1, tiled=True).astype(F32)
+
+    grad_up = summed(share_up)
+    grad_out = summed(share_out)
+    grad_inp = summed(share_in)
+    quarter = lax.psum_scatter(share_down, "rows", scatter_dimension=0, tiled=True)
+    own_cols = lax.psum_scatter(quarter, "seq", scatter_dimension=1, tiled=True)
+    grad_down = lax.all_gather(own_cols, "rows", axis=0, tiled=True).T.astype(F32)
+
+    taps_back = lax.all_to_all(grad_taps.astype(BF16), "seq", split_axis=0, concat_axis=0, tiled=True)
+    taps_back = lax.psum(taps_back.reshape(width, blocks), "rows").T.astype(F32)
+    tanh = jnp.tanh(raw / THRESH)
+    grad_kernel = (taps_back * tanh * tanh)[:, None, :]
+
+    spread = lax.dynamic_update_slice_in_dim(
+        jnp.zeros((10, width), F32), col_sums[:, :10].T, me * each, axis=1
+    )
+    gain_one, gain_two, stats, spread = lax.psum(
+        (gain_one, gain_two, jnp.sum(stats, axis=1), spread), ("rows", "seq")
+    )
+    grad_tap_rows = jnp.transpose(spread[:9].reshape(3, 3, width), (1, 0, 2)).reshape(3, 3 * width)
+    rms_stats = jnp.sqrt(stats[:3] / (jnp.maximum(stats[3], 1.0) * width))
+    return (
+        block_out.reshape(block_in.shape),
+        grad_flat.reshape(block_in.shape),
+        gain_one[0],
+        grad_inp,
+        grad_tap_rows,
+        grad_kernel,
+        spread[9],
+        grad_out,
+        gain_two[0],
+        grad_up,
+        grad_down,
+        rms_stats,
+    )
+
+
+def chosen(block_in, *rest):
+    rows, blocks, _, width = block_in.shape
+    n = lax.axis_size("seq")
+    fits = blocks % 256 == 0 and width % (32 * n) == 0 and n == 8 and 2 * rows <= 8
+    return (local if fits else general_local)(block_in, *rest)
+
+
 def solution(mesh):
     return jax.shard_map(
-        local,
+        chosen,
         mesh=mesh,
         in_specs=(
             P("rows", None, "seq", None),

time: 1230 us -> 699 us (0.57)
  waiting for transfers between devices: 683 us -> 340 us
  matrix products: 220 us -> 0 us
  Pallas kernels: 0 us -> 212 us
  starting transfers between devices: 93.8 us -> 0.37 us
  other arithmetic: 82.7 us -> 4.51 us
  blocking collectives: 41.4 us -> 86.1 us
  local copies, waits for them, and re-layouts: 80.1 us -> 40.1 us
    all_to_all x12 -> x0, waiting for transfers between devices: 265 us -> none  [the longest x1 57.2 us: local(): lax.all_to_all(back_re.astype(jnp.bfloat16), 'seq', split_axis=1, concat_...]
    ppermute x6 -> x0, waiting for transfers between devices: 254 us -> none  [passed_along(): return lax.ppermute(block, axis, route)]
    dot_general x48 -> x0, matrix products: 220 us -> none  [the longest x4 25.8 us: trans_times(): lax.dot_general(left, right, (((0,), (0,)), ((), ())), preferred_element_...]
    pallas_call x0 -> x5, Pallas kernels: none -> 212 us  [call(): pl.pallas_call(body, out_shape=tuple((jax.ShapeDtypeStruct(*out) for out...]
    reduce_scatter x4 -> x5, waiting for transfers between devices: 162 us -> 260 us  [the longest x3 165 us: summed(): own_rows = lax.psum_scatter(quarter, 'seq', scatter_dimension=0, tiled=True)]
    unnamed x5 -> x12, waiting for transfers between devices: 0.08 us -> 79.9 us
    all_to_all x12 -> x0, starting transfers between devices: 79.6 us -> none  [the longest x1 23.9 us: local(): lax.all_to_all(tap_im.astype(jnp.bfloat16), 'seq', split_axis=2, concat_a...]
    convert_element_type x19 -> x4, other arithmetic: 31.2 us -> 1.24 us  [the longest x1 1.11 us: summed(): return lax.all_gather(own_rows, 'rows', axis=1, tiled=True).astype(F32)]
  transfers between devices with their start and end apart: 23 -> 9, of which waited for: 17 -> 7; matrix products, arithmetic and copies ran while one was open for 24% -> 4% of each run, Pallas kernels for 0% -> 10%
where the time goes in v1:
time: 699 us; the launch traced here: 698 us
  waiting for transfers between devices  340 us (49%)
  Pallas kernels  212 us (30%)
  blocking collectives  86.1 us (12%)
  local copies, waits for them, and re-layouts  40.1 us (6%)
  between operations  14.7 us (2%)
    pallas_call x5, Pallas kernels, call(): pl.pallas_call(body, out_shape=tuple((jax.ShapeDtypeStruct(*out) for out...  212 us
    reduce_scatter x3, waiting for transfers between devices, summed(): own_rows = lax.psum_scatter(quarter, 'seq', scatter_dimension=0, tiled=True)  165 us
    unnamed x12, waiting for transfers between devices  79.9 us
    reduce_scatter x1, waiting for transfers between devices, local(): lax.psum_scatter(share_down, 'rows', scatter_dimension=0, tiled=True)  48.1 us
    reduce_scatter x1, waiting for transfers between devices, summed(): quarter = lax.psum_scatter(share, 'rows', scatter_dimension=1, tiled=True)  47.8 us
    psum x1, blocking collectives, local(): lax.psum((gain_one, gain_two, jnp.sum(stats, axis=1), spread), ('rows', '...  40.5 us
    unnamed x41, local copies, waits for them, and re-layouts  30.8 us
    all_gather x3, blocking collectives, summed(): return lax.all_gather(own_rows, 'rows', axis=1, tiled=True).astype(F32)  20.5 us
  transfers between devices with their start and end apart: 9, of which 7 were waited for; matrix products, arithmetic and copies ran while one was open for 4% of the time, Pallas kernels for 10%

profile of v1, /device:TPU:0, one launch (start us, length us, event | category | flops | bytes accessed | tf_op | source)
XLA Modules:
  0.0 698.1 jit_solution(113100669745057183)
XLA Ops:
  7.2 0.7 broadcast_in_dim.21
  7.9 0.8 fusion.1
  8.7 0.1 copy.46
  8.9 2.7 copy.63
  11.7 0.1 pad.13.clone
  11.7 0.6 broadcast_in_dim.19.gain
  12.3 0.9 copy.73
  13.2 1.2 copy.67
  14.5 0.9 copy.47.mask_col
  15.4 0.6 broadcast_in_dim.22.gain
  15.9 0.6 pad.4.cols_in
  16.6 0.7 add_add_fusion.marks
  17.2 70.2 %shard_map.247 = (bf16[2,3,10,96,256]{4,3,2,1,0:T(8,128)(2,1)}, bf16[8,96,256]{2,1,0:T(8,128)(2,1)}, s32[8,8,256]{2,1,0:T(8,128)}, bf16[2,768,256]{2,1,0:T(8,128)(2,1)}) custom-call(f32[512,768]{1,0:T(8,128)} %bitcast.49, bf16[768,2304]{1,0:T(8,128)(2,1)} %w_in.1, f32[1,768]{1,0:T(1,128)} %broadcast_in_dim.19.gain, f32[256,768]{1,0:T(8,128)} %bitcast.56, ...), custom_call_target="tpu_custom_call" | custom-call | tf_op jit(solution)/shard_map/pallas_call | solution.py:885
  87.4 30.4 %shard_map.248 = (bf16[2,768,256]{2,1,0:T(8,128)(2,1)}, f32[3,10,2,256]{3,2,1,0:T(2,128)}, f32[8,2,96,256]{3,2,1,0:T(8,128)}, f32[2,8,2,96,256]{4,3,2,1,0:T(8,12...) custom-call(bf16[2,3,10,96,256]{4,3,2,1,0:T(8,128)(2,1)} %get-tuple-element.36.got, ...), custom_call_target="tpu_custom_call" | custom-call | tf_op jit(solution)/shard_map/pallas_call | solution.py:885
  117.8 38.9 %shard_map.249 = (f32[512,768]{1,0:T(8,128)}, bf16[2,8,96,256]{3,2,1,0:T(8,128)(2,1)}, f32[512,768]{1,0:T(8,128)}, bf16[768,3072]{1,0:T(8,128)(2,1)}, bf16[768,3...) custom-call(bf16[2,768,256]{2,1,0:T(8,128)(2,1)} %get-tuple-element.39.mixed, ...), custom_call_target="tpu_custom_call" | custom-call | tf_op jit(solution)/shard_map/pallas_call | solution.py:885
  156.7 2.4 copy.59
  159.1 0.0 reduce-scatter.25.cloned.1.call-start
  159.1 62.9 %shard_map.250 = (bf16[2,3,768,256]{3,2,1,0:T(8,128)(2,1)}, f32[8,96,256]{2,1,0:T(8,128)}, f32[96,128]{1,0:T(8,128)}) custom-call(bf16[2,8,96,256]{3,2,1,0:T(8,128)(2,1)} %get-tuple-element.41.back, bf16[2,3,10,96,256]{4,3,2,1,0:T(8,128)(2,1)} %get-tuple-element.36.got, f32[3,10,2,256]{3,2,1,0:T(2,128)} %get-tuple-element.42.same, ...), custom_call_target="tpu_custom_call" | custom-call | tf_op jit(solution)/shard_map/pallas_call | solution.py:885
  222.1 9.6 %shard_map.251 = (f32[512,768]{1,0:T(8,128)}, bf16[768,2304]{1,0:T(8,128)(2,1)}, f32[1,768]{1,0:T(1,128)}) custom-call(bf16[2,3,768,256]{3,2,1,0:T(8,128)(2,1)} %get-tuple-element.47.got_back, bf16[2,768,256]{2,1,0:T(8,128)(2,1)} %get-tuple-element.48.turned, bf16[768,2304]{1,0:T(8,128)(2,1)} %w_in.1, f32[512,768]{1,0:T(8,128)} %bitcast.51, ...), custom_call_target="tpu_custom_call" | custom-call | tf_op jit(solution)/shard_map/pallas_call | solution.py:885
  231.7 5.8 copy.57
  237.5 0.0 reduce-scatter.23.cloned.1.call-start
  237.5 0.7 reduce-scatter.23.cloned.1.call-update
  238.3 0.5 reduce-scatter.19.cloned.1.call-update
  238.8 0.6 copy-done.4
  239.4 17.6 %all_to_all.5 = bf16[8,96,256]{2,1,0:T(8,128)(2,1)S(1)} all-to-all(bf16[8,96,256]{2,1,0:T(8,128)(2,1)S(1)} %convert_element_type.42), channel_id=1, replica_groups=mesh['rows'=4,'seq'=8] {'seq'}, dimensions={0} | all-to-all | bytes 786432 | tf_op jit(solution)/shard_map/all_to_all | solution.py:1025
  257.0 0.9 copy.50
  258.0 0.0 reduce-scatter.17.cloned.1.call-start
  258.1 1.9 copy.60
  260.0 0.0 reduce-scatter.15.cloned.1.call-start
  260.1 20.1 %reduce-scatter.25.cloned.1.call-done = bf16[576,768]{1,0:T(8,128)(2,1)} async-done(((bf16[2304,768]{1,0:T(8,128)(2,1)}), bf16[576,768]{1,0:T(8,128)(2,1)}) %reduce-scatter.25.cloned.1.call-update) | async-done | bytes 884752
  280.2 2.2 copy.58
  282.4 0.0 reduce-scatter.29.cloned.1.call-start
  282.5 48.1 %reduce-scatter.23.cloned.1.call-done = bf16[192,3072]{1,0:T(8,128)(2,1)} async-done(((bf16[768,3072]{1,0:T(8,128)(2,1)}), bf16[192,3072]{1,0:T(8,128)(2,1)}) %reduce-scatter.23.cloned.1.call-update) | async-done | bytes 1179664 | tf_op jit(solution)/shard_map/reduce_scatter | solution.py:1021
  330.6 2.5 copy.61
  333.2 0.0 reduce-scatter.21.cloned.1.call-start
  333.2 47.8 %reduce-scatter.19.cloned.1.call-done = bf16[768,768]{1,0:T(8,128)(2,1)} async-done(((bf16[768,3072]{1,0:T(8,128)(2,1)}), bf16[768,768]{1,0:T(8,128)(2,1)}) %reduce-scatter.19.cloned.1.call-update) | async-done | bytes 1179664 | tf_op jit(solution)/shard_map/reduce_scatter | solution.py:1014
  381.0 0.1 copy.49
  381.2 0.1 reduce_sum.9
  381.3 0.3 dynamic_update_slice.3
  381.6 40.5 %all-reduce.1 = (f32[768]{0:T(1024)}, f32[10,768]{1,0:T(8,128)S(1)}, f32[768]{0:T(1024)}, f32[8]{0:T(128)S(1)}) all-reduce(f32[768]{0:T(1024)S(1)} %reduce, f32[10,768]{1,0:T(8,128)S(1)} %dynamic_update_slice.3, f32[768]{0:T(1024)S(1)} %reduce.2, f32[8]{0:T(128)S(1)} %reduce_sum.9), channel_id=1, replica_groups=mesh['rows'=4,'seq'=8] {'rows','seq'}, use_global_device_ids=true, to_apply=%region_0.1 | all-reduce | flops 9224 | bytes 73792 | tf_op jit(solution)/shard_map/psum | solution.py:1033
  422.1 0.6 slice.35
  422.7 0.6 reshape.69
  423.3 2.8 copy.53
  426.1 2.8 copy.52
  429.5 0.6 slice_reduce_fusion
  430.1 0.5 divide_sqrt_fusion
  430.6 1.1 fusion
  431.7 1.7 copy.54
  433.4 48.5 %reduce-scatter.17.cloned.1.call-done = bf16[96,192]{1,0:T(8,128)(2,1)} async-done(((bf16[768,192]{1,0:T(8,128)(2,1)}), bf16[96,192]{1,0:T(8,128)(2,1)}) %reduce-scatter.17.cloned.1.call-update) | async-done | bytes 36880 | tf_op jit(solution)/shard_map/reduce_scatter | solution.py:1015
  481.9 0.9 copy.51
  482.8 5.6 all_gather.13
  488.4 0.9 copy.55
  489.3 59.3 %reduce-scatter.15.cloned.1.call-done = bf16[96,576]{1,0:T(8,128)(2,1)} async-done(((bf16[768,576]{1,0:T(8,128)(2,1)}), bf16[96,576]{1,0:T(8,128)(2,1)}) %reduce-scatter.15.cloned.1.call-update) | async-done | bytes 110608 | tf_op jit(solution)/shard_map/reduce_scatter | solution.py:1015
  548.6 7.2 %all-gather = bf16[4,576,96]{1,2,0:T(8,128)(2,1)S(1)} all-gather(bf16[1,576,96]{1,2,0:T(8,128)(2,1)} %bitcast.66), channel_id=1, replica_groups=mesh['rows'=4,'seq'=8] {'rows'}, dimensions={0}, use_global_device_ids=true | all-gather | bytes 552960 | tf_op jit(solution)/shard_map/all_gather | solution.py:1016
  555.8 0.3 copy.48
  556.0 1.5 reshape.74
  557.5 58.4 %reduce-scatter.29.cloned.1.call-done = bf16[384,192]{1,0:T(8,128)(2,1)} async-done(((bf16[3072,192]{1,0:T(8,128)(2,1)}), bf16[384,192]{1,0:T(8,128)(2,1)}) %reduce-scatter.29.cloned.1.call-update) | async-done | bytes 147472
  616.0 1.1 copy.62
  617.0 7.5 %all_gather.15 = bf16[768,384]{1,0:T(8,128)(2,1)S(1)} all-gather(bf16[192,384]{1,0:T(8,128)(2,1)S(1)} %copy.62), channel_id=1, replica_groups=mesh['rows'=4,'seq'=8] {'rows'}, dimensions={0}, use_global_device_ids=true | all-gather | bytes 737280 | tf_op jit(solution)/shard_map/all_gather | solution.py:1023
  624.6 0.1 convert_bitcast_fusion
  624.6 1.4 copy.56
  626.0 56.7 %reduce-scatter.21.cloned.1.call-done = bf16[96,768]{1,0:T(8,128)(2,1)} async-done(((bf16[768,768]{1,0:T(8,128)(2,1)}), bf16[96,768]{1,0:T(8,128)(2,1)}) %reduce-scatter.21.cloned.1.call-update) | async-done | bytes 147472 | tf_op jit(solution)/shard_map/reduce_scatter | solution.py:1015
  682.8 7.7 %all_gather.14 = bf16[96,3072]{1,0:T(8,128)(2,1)S(1)} all-gather(bf16[96,768]{1,0:T(8,128)(2,1)} %reduce-scatter.21.cloned.1.call-done), channel_id=1, replica_groups=mesh['rows'=4,'seq'=8] {'rows'}, dimensions={1}, use_global_device_ids=true | all-gather | bytes 737280 | tf_op jit(solution)/shard_map/all_gather | solution.py:1016
  690.5 1.1 convert_element_type.46
  (48 shorter events, 0.4 us)
Async XLA Ops:
  7.2 250.9 %reduce-scatter.27.cloned.1.call-start = ((), (), s32[]{:S(2)}) async-start(), calls=%async_computation.16 | async-start | bytes 1474560
  8.8 2.8 copy-start.7
  8.8 2.8 copy-start.12
  8.9 2.9 copy-start.8
  8.9 3.4 copy-start
  11.6 1.6 copy-start.1
  13.2 2.1 copy-start.9
  159.1 121.1 %reduce-scatter.25.cloned.1.call-start = ((), (), s32[]{:S(2)}) async-start(), calls=%async_computation.15 | async-start | bytes 4423680
  237.5 93.1 %reduce-scatter.23.cloned.1.call-start = ((), (), s32[]{:S(2)}) async-start(), calls=%async_computation.14 | async-start | bytes 5898240 | tf_op jit(solution)/shard_map/reduce_scatter | solution.py:1021
  238.2 142.8 %reduce-scatter.19.cloned.1.call-start = ((), (), s32[]{:S(2)}) async-start(), calls=%async_computation.12 | async-start | bytes 5898240 | tf_op jit(solution)/shard_map/reduce_scatter | solution.py:1014
  238.3 1.1 copy-start.4
  238.8 191.8 %all-reduce.4.cloned.1.call-start = ((), (), s32[]{:S(2)}) async-start(), calls=%async_computation.10 | async-start | bytes 786432 | tf_op jit(solution)/shard_map/psum | solution.py:1026
  258.0 223.9 %reduce-scatter.17.cloned.1.call-start = ((), (), s32[]{:S(2)}) async-start(), calls=%async_computation.11 | async-start | bytes 442368 | tf_op jit(solution)/shard_map/reduce_scatter | solution.py:1015
  260.0 288.5 %reduce-scatter.15.cloned.1.call-start = ((), (), s32[]{:S(2)}) async-start(), calls=%async_computation.9 | async-start | bytes 1105920 | tf_op jit(solution)/shard_map/reduce_scatter | solution.py:1015
  282.4 333.5 %reduce-scatter.29.cloned.1.call-start = ((), (), s32[]{:S(2)}) async-start(), calls=%async_computation.17 | async-start | bytes 1769472
  333.1 47.9 %copy-start.5 = (f32[96,128]{1,0:T(8,128)S(1)}, f32[96,128]{1,0:T(8,128)}, u32[]{:S(2)}) copy-start(f32[96,128]{1,0:T(8,128)} %get-tuple-element.53) | copy-start | bytes 147460
  333.1 48.0 %copy-start.11 = (f32[1,768]{1,0:T(1,128)S(1)}, f32[1,768]{1,0:T(1,128)}, u32[]{:S(2)}) copy-start(f32[1,768]{1,0:T(1,128)} %get-tuple-element.51) | copy-start | bytes 9220
  333.1 48.0 %copy-start.10 = (f32[1,768]{1,0:T(1,128)S(1)}, f32[1,768]{1,0:T(1,128)}, u32[]{:S(2)}) copy-start(f32[1,768]{1,0:T(1,128)} %get-tuple-element.56) | copy-start | bytes 9220
  333.1 48.1 %copy-start.6 = (f32[8,768]{1,0:T(8,128)S(1)}, f32[8,768]{1,0:T(8,128)}, u32[]{:S(2)}) copy-start(f32[8,768]{1,0:T(8,128)} %get-tuple-element.59) | copy-start | bytes 73732
  333.1 90.2 %copy-start.3 = (f32[512,768]{1,0:T(8,128)S(1)}, f32[512,768]{1,0:T(8,128)}, u32[]{:S(2)}) copy-start(f32[512,768]{1,0:T(8,128)} %get-tuple-element.50) | copy-start | bytes 4718596
  333.2 349.6 %reduce-scatter.21.cloned.1.call-start = ((), (), s32[]{:S(2)}) async-start(), calls=%async_computation.13 | async-start | bytes 1327104 | tf_op jit(solution)/shard_map/reduce_scatter | solution.py:1015
  423.3 2.8 copy-start.2
Sparse Core Ops, SparseCore 0:
  159.2 28.3 reduce-scatter.26
  237.6 42.5 reduce-scatter.24
  282.7 47.8 reduce-scatter.22
  333.2 47.7 reduce-scatter.18
  383.8 32.6 all-reduce.3
  420.5 61.4 reduce-scatter.16
  486.2 62.3 reduce-scatter.14
  552.0 63.9 reduce-scatter.28
  619.7 62.9 reduce-scatter.20

commit v2 on v1

--- a/solution.py
+++ b/solution.py
@@ -314,7 +314,7 @@
 MESH = pl.DeviceIdType.MESH
 F32 = jnp.float32
 BF16 = jnp.bfloat16
-VMEM_BYTES = 60 * 1024 * 1024
+VMEM_BYTES = 63 * 1024 * 1024
 ROOT_HALF = math.sqrt(0.5)
 C0 = math.sqrt(2.0 / math.pi)
 C1 = 0.044715
@@ -480,6 +480,10 @@
     two = got[r, c, p, rows, :].astype(F32) * same[1, p, r:r + 1, :]
     value = cols[3 * c, rows, :] * now + cols[3 * c + 1, rows, :] * one + cols[3 * c + 2, rows, :] * two
     return value, (now, one, two)
+
+
+def folded(value):
+    return sum(value[:, at:at + 128] for at in range(0, value.shape[1], 128))
 
 
 def spread_cols(cols_in, cols):
@@ -706,15 +710,29 @@
         jnp.sum(mask_col[...], axis=0, keepdims=True) * (1.0 / width), (1, width)
     )
     stats[4:8, :] = jnp.zeros((4, width), F32)
-    share_out[...] = sum(dot_nn(mixed[r], mix_back[r]) for r in range(rows)).astype(BF16)
-
-    def weight_step(j, carry):
-        cols = pl.ds(pl.multiple_of(j * chunk, chunk), chunk)
-        share_up[:, cols] = dot_nn(turned[...], grad_act[:, cols]).astype(BF16)
-        share_down[:, cols] = dot_nn(turned_cot[...], act[:, cols]).astype(BF16)
-        return carry
-
-    lax.fori_loop(0, hidden // chunk, weight_step, 0)
+    side = each // 2
+
+    def put_rows(share, half, lanes, value):
+        for s in range(n):
+            for core in range(2):
+                low = (2 * s + core) * side
+                share[s // 4, (s // 2) % 2, s % 2, core, half, :, lanes] = value[low:low + side]
+
+    for half in range(2):
+        low = half * (width // 2)
+        value = sum(dot_nn(mixed[r], mix_back[r, :, low:low + width // 2]) for r in range(rows)).astype(BF16)
+        put_rows(share_out, half, slice(None), value)
+        for low in range(0, hidden // 2, chunk):
+            cols = slice(half * (hidden // 2) + low, half * (hidden // 2) + low + chunk)
+            put_rows(share_up, half, slice(low, low + chunk), dot_nn(turned[...], grad_act[:, cols]).astype(BF16))
+    span = hidden // n
+    quarter = width // 4
+    for s in range(n):
+        value = dot_nn(turned_cot[...], act[:, s * span:(s + 1) * span]).astype(BF16)
+        for core in range(2):
+            for half in range(2):
+                low = (2 * core + half) * quarter
+                share_down[s // 4, (s // 2) % 2, s % 2, core, half] = value[low:low + quarter]
     for r in range(rows):
         def wait(peer, j):
             part = pl.ds(pl.multiple_of(peer * each, each), each)
@@ -725,167 +743,519 @@
         all_peers(n, wait)
 
 
-def back_kernel(
+def place():
+    row, seq = lax.axis_index("rows"), lax.axis_index("seq")
+    return lax.div(row, 2), lax.rem(row, 2), lax.div(seq, 4), lax.rem(lax.div(seq, 2), 2), lax.rem(seq, 2)
+
+
+def partner(axis):
+    y, c, zh, zl, x = place()
+    if axis == "core":
+        return {"rows": 2 * y + 1 - c}
+    if axis == "y":
+        return {"rows": 2 * (1 - y) + c}
+    if axis == "x":
+        return {"seq": 4 * zh + 2 * zl + 1 - x}
+    if axis == "zl":
+        return {"seq": 4 * zh + 2 * (1 - zl) + x}
+    return {"seq": 4 * (1 - zh) + 2 * zl + x}
+
+
+def exchange(src, dst, send_sem, recv_sem, axis):
+    return pltpu.make_async_remote_copy(
+        src_ref=src, dst_ref=dst, send_sem=send_sem, recv_sem=recv_sem,
+        device_id=partner(axis), device_id_type=MESH,
+    )
+
+
+ALL = slice(None)
+
+
+class Tree:
+    def __init__(self, order, share, own, parts, gathered, sems):
+        self.order = ("core",) + order + ("zl", "zh", "back_y", "back_core")
+        self.share, self.own, self.parts, self.gathered, self.sems = share, own, parts, gathered, sems
+        self.started = []
+
+    def copies(self, step):
+        y, c, zh, zl, x = place()
+        axis = self.order[step]
+        parts, gathered = self.parts, self.gathered
+        own = self.share.at[:, :, :, c] if self.own is None else self.own
+        second = self.order[1]
+        if axis == "core":
+            src, dst = self.share.at[:, :, :, 1 - c], parts[0]
+        elif axis == "y":
+            src = own.at[:, :, :, 1 - y] if second == "y" else own.at[:, :, x, 1 - y]
+            dst = parts[step]
+        elif axis == "x":
+            src = own.at[:, :, 1 - x] if second == "x" else own.at[:, :, 1 - x, y]
+            dst = parts[step]
+        elif axis == "zl":
+            src, dst = own.at[:, 1 - zl, x, y], parts[3]
+        elif axis == "zh":
+            src, dst = own.at[1 - zh, zl, x, y], parts[4]
+        elif axis == "back_y":
+            src = dst = gathered.at[c, y]
+        else:
+            src = dst = gathered.at[c]
+        return exchange(src, dst, self.sems.at[0, step], self.sems.at[1, step], axis.replace("back_", ""))
+
+    def start(self, step):
+        self.copies(step).start()
+        self.started.append(step)
+
+    def mine(self, a, b, d, e):
+        c = place()[1]
+        return (self.share, (a, b, d, c, e)) if self.own is None else (self.own, (a, b, d, e))
+
+    def add(self, where, part):
+        rows = self.share.shape[-2]
+        size = 48 if rows % 48 == 0 else rows
+        own, where = self.mine(*where)
+
+        def body(i, carry):
+            here = pl.ds(pl.multiple_of(i * size, size), size)
+            own[where + (here, ALL)] = own[where + (here, ALL)] + part[0][part[1] + (here, ALL)]
+            return carry
+
+        lax.fori_loop(0, rows // size, body, 0)
+
+    def finish(self, step):
+        y, c, zh, zl, x = place()
+        axis = self.order[step]
+        self.copies(step).wait_recv()
+        second = self.order[1]
+        two = range(2)
+        if axis == "core":
+            for a in two:
+                for b in two:
+                    for d in two:
+                        for e in two:
+                            self.add((a, b, d, e), (self.parts[0], (a, b, d, e)))
+        elif axis in ("x", "y"):
+            for a in two:
+                for b in two:
+                    if step == 2:
+                        self.add((a, b, x, y), (self.parts[2], (a, b)))
+                    else:
+                        for d in two:
+                            self.add((a, b, d, y) if second == "y" else (a, b, x, d), (self.parts[1], (a, b, d)))
+        elif axis == "zl":
+            for a in two:
+                self.add((a, zl, x, y), (self.parts[3], (a,)))
+        elif axis == "zh":
+            own, where = self.mine(zh, zl, x, y)
+            self.gathered[c, y] = own[where] + self.parts[4][...]
+        if step + 1 < len(self.order):
+            self.start(step + 1)
+
+    def drain(self):
+        for step in self.started:
+            self.copies(step).wait_send()
+
+
+def tree_scratch(r, l):
+    shapes = [(2, 2, 2, 2, r, l)] * 2 + [(2, 2, 2, r, l), (2, 2, r, l), (2, r, l), (r, l), (2, 2, r, l)]
+    return [pltpu.VMEM(shape, BF16) for shape in shapes] + [pltpu.SemaphoreType.DMA((2, 7))]
+
+
+def tail_kernel(
     n, back, got, same, spec_taps, spec_gate, gated, long_out, cols_in, table, inverse, turns,
-    got_back, grad_taps, col_sums,
-    cols, sums, spec, spec_sum, grad_long, short, sent, send_sem, recv_sem,
+    share_up, share_down, share_out, w_in_far, turned_far, x_far, mid_far, gain, raw_far, sums_two, stats,
+    grad_flat, grad_in, grad_out, grad_up, grad_down, grad_kernel, vector_sums, channel_sums,
+    got_back, sent, send_sem, recv_sem, fetch_sem,
+    tap_own, tap_got, tap_half, tap_part, tap_all, tap_sems, tap_send, tap_recv,
+    vector_got, channel_got, vector_sems,
+    *tree_refs,
 ):
     me = lax.axis_index("seq")
+    y, c, zh, zl, xbit = place()
     rows, each, blocks = got.shape[0], got.shape[3], got.shape[4]
+    width = n * each
     mine = pl.ds(pl.multiple_of(me * each, each), each)
     barrier = greet(n)
-    spread_cols(cols_in, cols)
-    sums[...] = jnp.zeros_like(sums)
-    spec_sum[...] = jnp.zeros_like(spec_sum)
-
-    def tap_sums(c, part, grad, inputs):
-        for i in range(3):
-            sums[3 * c + i, part, :] += grad * inputs[i]
-
-    def spread_back(r, c):
-        for slot in range(2):
-            short[c, n + slot] = pltpu.roll(short[c, slot], blocks - 1, 1)
-
-        def step(p, carry):
-            for at in range(0, each, 32):
-                part = pl.ds(at, 32)
-                value = cols[3 * c, part, :] * short[c, p, part, :]
-                value += cols[3 * c + 1, part, :] * (short[c, p + 1, part, :] * same[0, p + 1, r:r + 1, :])
-                value += cols[3 * c + 2, part, :] * (short[c, p + 2, part, :] * same[1, p + 2, r:r + 1, :])
-                sent[r, c, p, part, :] = value.astype(BF16)
-            return carry
-
-        lax.fori_loop(0, n, step, 0)
-        all_peers(n, lambda peer, j: to_peer(
-            sent.at[r, c, peer], got_back.at[r, c, mine], send_sem.at[r, c, j], recv_sem.at[r, c, me], peer,
-        ).start())
-        got_back[r, c, mine] = sent[r, c, me]
-
-    for r in range(rows):
-        def query_step(p, carry):
-            for at in range(0, each, 32):
-                part = pl.ds(at, 32)
-                grad = back[r, p, part, :].astype(F32)
-                query, inputs = short_conv(got, cols, same, r, 0, p, part)
-                grad_query = grad * long_out[r, p, part, :]
-                value = grad * query
-                grad_long[p, part, :] = value
-                short[0, p, part, :] = grad_query
-                tap_sums(0, part, grad_query, inputs)
-                sums[9, part, :] += value * gated[r, p, part, :]
-            return carry
-
-        lax.fori_loop(0, n, query_step, 0)
-        if r == 0:
-            pl.semaphore_wait(barrier, n - 1)
-        spread_back(r, 0)
-        for p in range(n):
-            spec[p * each:(p + 1) * each, :] = dot_nn(grad_long[p].astype(BF16), table[...])
-
-        def product_group(at, lane):
-            re, im = load_phases(spec, n, each, at, lane, blocks)
-            re, im = turn_phases(re, im, turns, lane, -1)
-            re, im = fft_points(re, im, -1)
-            out_r, out_i = [], []
-            for k in range(n):
-                here = (pl.ds(at, 8), slice(lane, lane + 128))
-                tap_r, tap_i = spec_taps[(k, 0) + here], spec_taps[(k, 1) + here]
-                gate_r, gate_i = spec_gate[(r, k, 0) + here], spec_gate[(r, k, 1) + here]
-                spec_sum[(k, 0) + here] += gate_r * re[k] + gate_i * im[k]
-                spec_sum[(k, 1) + here] += gate_r * im[k] - gate_i * re[k]
-                out_r.append(tap_r * re[k] + tap_i * im[k])
-                out_i.append(tap_r * im[k] - tap_i * re[k])
-            re, im = fft_points(out_r, out_i, 1)
+    for axis in ("core", "y"):
+        pl.semaphore_signal(barrier, inc=1, device_id=partner(axis), device_id_type=MESH)
+
+    trees, at = {}, 0
+    specs = (("up", share_up, ("y", "x"), True), ("down", share_down, ("x", "y"), True), ("out", share_out, ("y", "x"), True))
+    for i, (name, share, order, far) in enumerate(specs):
+        own, parts, gathered, sems = tree_refs[at], tree_refs[at + 1:at + 6], tree_refs[at + 6], tree_refs[at + 7]
+        trees[name] = Tree(order, share, own, parts, gathered, sems)
+        at += 8
+    for name, order in (("in0", ("y", "x")), ("in1", ("x", "y")), ("in2", ("y", "x"))):
+        parts = tree_refs[at:at + 5]
+        trees[name] = Tree(order, None, None, parts, tree_refs[at + 5], tree_refs[at + 6])
+        at += 7
+
+    fetches = [
+        pltpu.make_async_copy(src, dst, fetch_sem.at[i])
+        for i, (src, dst) in enumerate(
+            [(trees[name].share.at[:, :, :, c], trees[name].own) for name in ("up", "down", "out")]
+            + [(mid_far, grad_flat), (raw_far, grad_kernel)]
+        )
+    ]
+    for copy in fetches:
+        copy.start()
+    side = each // 2
+
+    def tap_core():
+        return exchange(tap_own.at[1 - c], tap_got, tap_sems.at[0, 0], tap_sems.at[1, 0], "core")
+
+    def tap_y():
+        return exchange(tap_own.at[c, 1 - y], tap_half, tap_sems.at[0, 1], tap_sems.at[1, 1], "y")
+
+    def wait_back(r, k):
+        def wait(peer, j):
+            part = pl.ds(pl.multiple_of(peer * each, each), each)
+            to_peer(
+                sent.at[r, k, peer], got_back.at[r, k, part], send_sem.at[r, k, j], recv_sem.at[r, k, peer], peer,
+            ).wait()
+
+        all_peers(n, wait)
+
+    def conv_phase(cols, sums, spec, spec_sum, grad_long, short):
+        spread_cols(cols_in, cols)
+        sums[...] = jnp.zeros_like(sums)
+        spec_sum[...] = jnp.zeros_like(spec_sum)
+        pl.semaphore_wait(barrier, n + 1)
+        for name in ("up", "down", "out"):
+            trees[name].start(0)
+
+        def tap_sums(part_at, p_part, grad, inputs):
+            for i in range(3):
+                sums[3 * part_at + i, p_part, :] += folded(grad * inputs[i])
+
+        def spread_back(r, k):
+            for slot in range(2):
+                short[k, n + slot] = pltpu.roll(short[k, slot], blocks - 1, 1)
+
+            def step(p, carry):
+                for low in range(0, each, 32):
+                    part = pl.ds(low, 32)
+                    value = cols[3 * k, part, :] * short[k, p, part, :]
+                    value += cols[3 * k + 1, part, :] * (short[k, p + 1, part, :] * same[0, p + 1, r:r + 1, :])
+                    value += cols[3 * k + 2, part, :] * (short[k, p + 2, part, :] * same[1, p + 2, r:r + 1, :])
+                    sent[r, k, p, part, :] = value.astype(BF16)
+                return carry
+
+            lax.fori_loop(0, n, step, 0)
+            all_peers(n, lambda peer, j: to_peer(
+                sent.at[r, k, peer], got_back.at[r, k, mine], send_sem.at[r, k, j], recv_sem.at[r, k, me], peer,
+            ).start())
+            got_back[r, k, mine] = sent[r, k, me]
+
+        for r in range(rows):
+            def query_step(p, carry):
+                for low in range(0, each, 32):
+                    part = pl.ds(low, 32)
+                    grad = back[r, p, part, :].astype(F32)
+                    query, inputs = short_conv(got, cols, same, r, 0, p, part)
+                    grad_query = grad * long_out[r, p, part, :]
+                    value = grad * query
+                    grad_long[r, p, part, :] = value.astype(BF16)
+                    short[0, p, part, :] = grad_query
+                    tap_sums(0, part, grad_query, inputs)
+                    sums[9, part, :] += folded(value * gated[r, p, part, :])
+                return carry
+
+            lax.fori_loop(0, n, query_step, 0)
+            spread_back(r, 0)
+
+        for i, name in enumerate(("up", "down", "out")):
+            fetches[i].wait()
+            trees[name].finish(0)
+
+        for r in range(rows):
+            for p in range(n):
+                spec[p * each:(p + 1) * each, :] = dot_nn(grad_long[r, p], table[...])
+
+            def product_group(at, lane):
+                re, im = load_phases(spec, n, each, at, lane, blocks)
+                re, im = turn_phases(re, im, turns, lane, -1)
+                re, im = fft_points(re, im, -1)
+                out_r, out_i = [], []
+                for k in range(n):
+                    here = (pl.ds(at, 8), slice(lane, lane + 128))
+                    tap_r, tap_i = spec_taps[(k, 0) + here], spec_taps[(k, 1) + here]
+                    gate_r, gate_i = spec_gate[(r, k, 0) + here], spec_gate[(r, k, 1) + here]
+                    spec_sum[(k, 0) + here] += gate_r * re[k] + gate_i * im[k]
+                    spec_sum[(k, 1) + here] += gate_r * im[k] - gate_i * re[k]
+                    out_r.append(tap_r * re[k] + tap_i * im[k])
+                    out_i.append(tap_r * im[k] - tap_i * re[k])
+                re, im = fft_points(out_r, out_i, 1)
+                re, im = turn_phases(re, im, turns, lane, 1)
+                for p in range(n):
+                    spec[pl.ds(p * each + at, 8), lane:lane + 128] = re[p]
+                    spec[pl.ds(p * each + at, 8), blocks + lane:blocks + lane + 128] = im[p]
+
+            over_groups(each, blocks, product_group)
+            for p in range(n):
+                short[0, p] = dot_nn(spec[p * each:(p + 1) * each, :].astype(BF16), inverse[...])
+
+            def gate_step(p, carry):
+                for low in range(0, each, 32):
+                    part = pl.ds(low, 32)
+                    keys, key_inputs = short_conv(got, cols, same, r, 1, p, part)
+                    values, value_inputs = short_conv(got, cols, same, r, 2, p, part)
+                    grad = short[0, p, part, :] + cols[9, part, :] * grad_long[r, p, part, :].astype(F32)
+                    grad = grad * same[2, p, r:r + 1, :]
+                    grad_keys = grad * values
+                    grad_values = grad * keys
+                    short[1, p, part, :] = grad_keys
+                    short[2, p, part, :] = grad_values
+                    tap_sums(1, part, grad_keys, key_inputs)
+                    tap_sums(2, part, grad_values, value_inputs)
+                return carry
+
+            lax.fori_loop(0, n, gate_step, 0)
+            spread_back(r, 1)
+            spread_back(r, 2)
+
+        def taps_group(at, lane):
+            here = (pl.ds(at, 8), slice(lane, lane + 128))
+            re = [spec_sum[(k, 0) + here] for k in range(n)]
+            im = [spec_sum[(k, 1) + here] for k in range(n)]
+            re, im = fft_points(re, im, 1)
             re, im = turn_phases(re, im, turns, lane, 1)
             for p in range(n):
                 spec[pl.ds(p * each + at, 8), lane:lane + 128] = re[p]
                 spec[pl.ds(p * each + at, 8), blocks + lane:blocks + lane + 128] = im[p]
 
-        over_groups(each, blocks, product_group)
+        over_groups(each, blocks, taps_group)
         for p in range(n):
-            short[0, p] = dot_nn(spec[p * each:(p + 1) * each, :].astype(BF16), inverse[...])
-
-        def gate_step(p, carry):
-            for at in range(0, each, 32):
-                part = pl.ds(at, 32)
-                keys, key_inputs = short_conv(got, cols, same, r, 1, p, part)
-                values, value_inputs = short_conv(got, cols, same, r, 2, p, part)
-                grad = short[0, p, part, :] + cols[9, part, :] * grad_long[p, part, :]
-                grad = grad * same[2, p, r:r + 1, :]
-                grad_keys = grad * values
-                grad_values = grad * keys
-                short[1, p, part, :] = grad_keys
-                short[2, p, part, :] = grad_values
-                tap_sums(1, part, grad_keys, key_inputs)
-                tap_sums(2, part, grad_values, value_inputs)
-            return carry
-
-        lax.fori_loop(0, n, gate_step, 0)
-        spread_back(r, 1)
-        spread_back(r, 2)
-
-    def taps_group(at, lane):
-        here = (pl.ds(at, 8), slice(lane, lane + 128))
-        re = [spec_sum[(k, 0) + here] for k in range(n)]
-        im = [spec_sum[(k, 1) + here] for k in range(n)]
-        re, im = fft_points(re, im, 1)
-        re, im = turn_phases(re, im, turns, lane, 1)
-        for p in range(n):
-            spec[pl.ds(p * each + at, 8), lane:lane + 128] = re[p]
-            spec[pl.ds(p * each + at, 8), blocks + lane:blocks + lane + 128] = im[p]
-
-    over_groups(each, blocks, taps_group)
-    for p in range(n):
-        grad_taps[p] = dot_nn(spec[p * each:(p + 1) * each, :].astype(BF16), inverse[...])
-    lanes = lax.broadcasted_iota(jnp.int32, col_sums.shape, 1)
-    total = jnp.zeros(col_sums.shape, F32)
-    for i in range(sums.shape[0]):
-        total = jnp.where(lanes == i, jnp.sum(sums[i], axis=-1, keepdims=True), total)
-    col_sums[...] = total
-    for r in range(rows):
-        for c in range(3):
-            def wait(peer, j):
-                part = pl.ds(pl.multiple_of(peer * each, each), each)
-                to_peer(
-                    sent.at[r, c, peer], got_back.at[r, c, part], send_sem.at[r, c, j], recv_sem.at[r, c, peer], peer,
-                ).wait()
-
-            all_peers(n, wait)
-
-
-def final_kernel(got_back, turned, w_in, x, mid, gain, grad_in, share_in, gain_sum):
-    rows, parts, width, blocks = got_back.shape
-    gain_sum[...] = jnp.zeros_like(gain_sum)
-    for r in range(rows):
-        tokens = slice(r * blocks, (r + 1) * blocks)
-        grad = sum(
-            dot_nn(w_in[:, c * width:(c + 1) * width], got_back[r, c]) for c in range(parts)
-        ).T
-        value = x[tokens, :]
-        scale = lax.rsqrt(jnp.mean(value * value, axis=-1, keepdims=True) + EPS)
-        gain_sum[...] += jnp.sum(grad * value * scale, axis=0, keepdims=True)
-        scaled = grad * gain[...]
-        shift = jnp.mean(scaled * value, axis=-1, keepdims=True) * (scale * scale * scale)
-        grad_in[tokens, :] = mid[tokens, :] + scaled * scale - value * shift
-    for c in range(parts):
-        for at in range(0, width, 256):
-            share_in[:, c * width + at:c * width + at + 256] = sum(
-                dot_nt(turned[r], got_back[r, c, at:at + 256, :]) for r in range(rows)
-            ).astype(BF16)
+            piece = dot_nn(spec[p * each:(p + 1) * each, :].astype(BF16), inverse[...]).astype(BF16)
+            for half in range(2):
+                tap_own[half, p // 4, p % 4] = piece[half * side:(half + 1) * side]
+
+        tap_core().start()
+        lanes = lax.broadcasted_iota(jnp.int32, (each, 128), 1)
+        total = jnp.zeros((each, 128), F32)
+        for i in range(10):
+            total = jnp.where(lanes == i, jnp.sum(sums[i], axis=-1, keepdims=True), total)
+        channel_sums[...] = jnp.zeros_like(channel_sums)
+        channel_sums[me, :, 0:each] = total.T[0:16, :]
+
+        for name in ("up", "down", "out"):
+            trees[name].finish(1)
+
+        tap_core().wait_recv()
+        for half in range(2):
+            for q in range(4):
+                tap_own[c, half, q] = tap_own[c, half, q] + tap_got[half, q]
+        tap_y().start()
+
+    pl.run_scoped(
+        conv_phase,
+        pltpu.VMEM((10, each, blocks), F32),
+        pltpu.VMEM((10, each, 128), F32),
+        pltpu.VMEM((width, 2 * blocks), F32),
+        pltpu.VMEM((n, 2, each, blocks), F32),
+        pltpu.VMEM((rows, n, each, blocks), BF16),
+        pltpu.VMEM((3, n + 2, each, blocks), F32),
+    )
+
+    def in_phase(w_in, turned, x, spec, share0, share1, share2):
+        for k, share in enumerate((share0, share1, share2)):
+            trees["in%d" % k].share = share
+        near = [
+            pltpu.make_async_copy(src, dst, fetch_sem.at[5 + i])
+            for i, (src, dst) in enumerate(((w_in_far, w_in), (turned_far, turned), (x_far, x)))
+        ]
+        for copy in near:
+            copy.start()
+        for copy in near + fetches[3:]:
+            copy.wait()
+
+        def weight_part(k):
+            for r in range(rows):
+                wait_back(r, k)
+            share = trees["in%d" % k].share
+            for half in range(2):
+                low = half * (width // 2)
+                value = sum(dot_nt(turned[r], got_back[r, k, low:low + width // 2, :]) for r in range(rows)).astype(BF16)
+                for s in range(n):
+                    for core in range(2):
+                        block = (2 * s + core) * side
+                        share[s // 4, (s // 2) % 2, s % 2, core, half] = value[block:block + side]
+            trees["in%d" % k].start(0)
+            for r in range(rows):
+                value = dot_nn(w_in[:, k * width:(k + 1) * width], got_back[r, k])
+                if k == 0:
+                    spec[:, r * blocks:(r + 1) * blocks] = value
+                else:
+                    spec[:, r * blocks:(r + 1) * blocks] += value
+
+        weight_part(0)
+        for name in ("up", "down", "out"):
+            trees[name].finish(2)
+        trees["in0"].finish(0)
+
+        tap_y().wait_recv()
+        for q in range(4):
+            tap_part[q] = tap_own[c, y, q] + tap_half[q]
+
+        def tap_copy(src_q, there):
+            peer = 4 * y + src_q
+            return to_peer(tap_part.at[src_q], tap_all.at[c, there], tap_send.at[src_q], tap_recv.at[there], peer)
+
+        for q in range(4):
+            @pl.when(4 * y + q != me)
+            def _():
+                tap_copy(q, me).start()
+
+            @pl.when(4 * y + q == me)
+            def _():
+                tap_all[c, me] = tap_part[q]
+
+        for name in ("up", "down", "out"):
+            trees[name].finish(3)
+        weight_part(1)
+        trees["in0"].finish(1)
+        trees["in1"].finish(0)
+        for name in ("up", "down", "out"):
+            trees[name].finish(4)
+
+        home = zh == y
+
+        @pl.when(home)
+        def _():
+            for j in range(1, n):
+                peer = lax.rem(me + j, n)
+                pltpu.make_async_remote_copy(
+                    src_ref=tap_part.at[0], dst_ref=tap_all.at[c, peer], send_sem=tap_send.at[0], recv_sem=tap_recv.at[peer],
+                    device_id={"seq": peer}, device_id_type=MESH,
+                ).wait_recv()
+            exchange(tap_all.at[c], tap_all.at[c], tap_sems.at[0, 2], tap_sems.at[1, 2], "y").start()
+
+        for name in ("up", "down", "out"):
+            trees[name].finish(5)
+
+        weight_part(2)
+        trees["in0"].finish(2)
+        trees["in1"].finish(1)
+        trees["in2"].finish(0)
+
+        vector_sums[0:1, :] = jnp.zeros((1, width), F32)
+        for r in range(rows):
+            tokens = slice(r * blocks, (r + 1) * blocks)
+            grad = spec[:, r * blocks:(r + 1) * blocks].T
+            value = x[tokens, :]
+            scale = lax.rsqrt(jnp.mean(value * value, axis=-1, keepdims=True) + EPS)
+            vector_sums[0:1, :] += jnp.sum(grad * value * scale, axis=0, keepdims=True)
+            scaled = grad * gain[...]
+            shift = jnp.mean(scaled * value, axis=-1, keepdims=True) * (scale * scale * scale)
+            grad_flat[tokens, :] = grad_flat[tokens, :] + scaled * scale - value * shift
+        vector_sums[1:2, :] = sums_two[...]
+        vector_sums[2:6, :] = stats[0:4, :]
+        vector_sums[6:8, :] = jnp.zeros((2, width), F32)
+
+        def vector_copies(step):
+            axis = ("core", "y", "x", "zl", "zh")[step]
+            return (
+                exchange(vector_sums, vector_got.at[step], vector_sems.at[0, step], vector_sems.at[1, step], axis),
+                exchange(channel_sums, channel_got.at[step], vector_sems.at[2, step], vector_sems.at[3, step], axis),
+            )
+
+        def vector_finish(step):
+            for copy in vector_copies(step):
+                copy.wait()
+            vector_sums[...] += vector_got[step]
+            channel_sums[...] += channel_got[step]
+            if step < 4:
+                for copy in vector_copies(step + 1):
+                    copy.start()
+
+        for copy in vector_copies(0):
+            copy.start()
+
+        @pl.when(jnp.logical_not(home))
+        def _():
+            exchange(tap_all.at[c], tap_all.at[c], tap_sems.at[0, 2], tap_sems.at[1, 2], "y").wait_recv()
+
+        exchange(tap_all.at[c], tap_all.at[c], tap_sems.at[0, 3], tap_sems.at[1, 3], "core").start()
+        trees["in0"].finish(3)
+        trees["in1"].finish(2)
+        vector_finish(0)
+        trees["in2"].finish(1)
+        for name in ("up", "down", "out"):
+            trees[name].finish(6)
+        for half in range(2):
+            for core in range(2):
+                place_rows = slice(core * side, (core + 1) * side)
+                for tree, target in ((trees["up"], grad_up), (trees["out"], grad_out)):
+                    l = tree.share.shape[-1]
+                    target[place_rows, half * l:(half + 1) * l] = tree.gathered[core, half].astype(F32)
+        grad_down[...] = trees["down"].gathered[...].reshape(width, grad_down.shape[0]).astype(F32).T
+        trees["in0"].finish(4)
+        vector_finish(1)
+        trees["in1"].finish(3)
+        trees["in2"].finish(2)
+        exchange(tap_all.at[c], tap_all.at[c], tap_sems.at[0, 3], tap_sems.at[1, 3], "core").wait_recv()
+        tanh = jnp.tanh(grad_kernel[...] * (1.0 / THRESH))
+        kernel_grad = jnp.concatenate(
+            [tap_all[core, s] for s in range(n) for core in range(2)], axis=0
+        ).astype(F32).T
+        grad_kernel[...] = kernel_grad * tanh * tanh
+        vector_finish(2)
+        trees["in0"].finish(5)
+        trees["in1"].finish(4)
+        trees["in2"].finish(3)
+        vector_finish(3)
+        trees["in0"].finish(6)
+        trees["in1"].finish(5)
+        trees["in2"].finish(4)
+        vector_finish(4)
+        trees["in1"].finish(6)
+        trees["in2"].finish(5)
+        trees["in2"].finish(6)
+        for k in range(3):
+            tree = trees["in%d" % k]
+            l = tree.share.shape[-1]
+            for half in range(2):
+                for core in range(2):
+                    low = k * width + half * l
+                    grad_in[core * side:(core + 1) * side, low:low + l] = tree.gathered[core, half].astype(F32)
+
+        for tree in trees.values():
+            tree.drain()
+        tap_core().wait_send()
+        tap_y().wait_send()
+        for q in range(4):
+            @pl.when(4 * y + q != me)
+            def _():
+                tap_copy(q, me).wait_send()
+
+        @pl.when(home)
+        def _():
+            exchange(tap_all.at[c], tap_all.at[c], tap_sems.at[0, 2], tap_sems.at[1, 2], "y").wait_send()
+
+        exchange(tap_all.at[c], tap_all.at[c], tap_sems.at[0, 3], tap_sems.at[1, 3], "core").wait_send()
+
+
+    pl.run_scoped(
+        in_phase,
+        pltpu.VMEM(w_in_far.shape, BF16),
+        pltpu.VMEM(turned_far.shape, BF16),
+        pltpu.VMEM(x_far.shape, F32),
+        pltpu.VMEM((width, 2 * blocks), F32),
+        *[pltpu.VMEM((2, 2, 2, 2, 2, side, width // 2), BF16)] * 3,
+    )
 
 
 def vmem(count):
     return [pl.BlockSpec(memory_space=pltpu.VMEM)] * count
 
 
-def call(body, outs, scratch, inputs, collective_id=None):
+def call(body, outs, scratch, inputs, collective_id=None, far=()):
     extra = {}
     if collective_id is not None:
         extra = dict(collective_id=collective_id, has_side_effects=True)
     return pl.pallas_call(
         body,
         out_shape=tuple(jax.ShapeDtypeStruct(*out) for out in outs),
-        in_specs=vmem(len(inputs)),
+        in_specs=[pl.BlockSpec(memory_space=pl.ANY if i in far else pltpu.VMEM) for i in range(len(inputs))],
         out_specs=tuple(vmem(len(outs))),
         scratch_shapes=scratch,
         compiler_params=pltpu.CompilerParams(vmem_limit_bytes=VMEM_BYTES, **extra),
@@ -955,15 +1325,20 @@
     )
     mask_col = valid_mask[:, :, 0].astype(F32).reshape(tokens, 1)
     chunk = 512
+    side = each // 2
+    bits = (2, 2, 2, 2, 2)
+    up_shape = bits + (side, hidden // 2)
+    down_shape = bits + (width // 4, hidden // n)
+    out_shape = bits + (side, width // 2)
     block_out, back, mid, share_up, share_down, share_out, gain_two, stats = call(
         functools.partial(mlp_kernel, n, chunk),
         [
             ((tokens, width), F32),
             ((rows, n, each, blocks), BF16),
             ((tokens, width), F32),
-            ((width, hidden), BF16),
-            ((width, hidden), BF16),
-            ((width, width), BF16),
+            (up_shape, BF16),
+            (down_shape, BF16),
+            (out_shape, BF16),
             ((1, width), F32),
             ((8, width), F32),
         ],
@@ -983,68 +1358,61 @@
         (mixed, x, cot, mask_col, out_proj, gain_mlp[None], up_proj, down_proj),
         3,
     )
-    got_back, grad_taps, col_sums = call(
-        functools.partial(back_kernel, n),
+    half_taps = (4, side, blocks)
+    trees = []
+    for shape in (up_shape, down_shape, out_shape):
+        trees += tree_scratch(*shape[5:])
+    for _ in range(3):
+        trees += tree_scratch(*out_shape[5:])[1:]
+    grad_flat, grad_inp, grad_out, grad_up, grad_down, grad_kernel, vectors, channels = call(
+        functools.partial(tail_kernel, n),
         [
-            ((rows, 3, width, blocks), BF16),
-            ((n, each, blocks), F32),
-            ((each, 128), F32),
+            ((tokens, width), F32),
+            ((each, 3 * width), F32),
+            ((each, width), F32),
+            ((each, hidden), F32),
+            ((hidden // n, width), F32),
+            ((blocks, width), F32),
+            ((8, width), F32),
+            ((n, 16, 128), F32),
         ],
         [
-            pltpu.VMEM((10, each, blocks), F32),
-            pltpu.VMEM((10, each, blocks), F32),
-            pltpu.VMEM((width, 2 * blocks), F32),
-            pltpu.VMEM((n, 2, each, blocks), F32),
-            pltpu.VMEM((n, each, blocks), F32),
-            pltpu.VMEM((3, n + 2, each, blocks), F32),
+            pltpu.VMEM((rows, 3, width, blocks), BF16),
             pltpu.VMEM((rows, 3, n, each, blocks), BF16),
             dma((rows, 3, n)), dma((rows, 3, n)),
-        ],
-        (back, got, same, spec_taps, spec_gate, gated, long_out, cols_in, table, inverse, turns),
+            dma((8,)),
+            pltpu.VMEM((2, 2) + half_taps, BF16),
+            pltpu.VMEM((2,) + half_taps, BF16),
+            pltpu.VMEM(half_taps, BF16),
+            pltpu.VMEM(half_taps, BF16),
+            pltpu.VMEM((2, n, side, blocks), BF16),
+            dma((2, 4)), dma((4,)), dma((n,)),
+            pltpu.VMEM((5, 8, width), F32),
+            pltpu.VMEM((5, n, 16, 128), F32),
+            dma((4, 5)),
+        ] + trees,
+        (
+            back, got, same, spec_taps, spec_gate, gated, long_out, cols_in, table, inverse, turns,
+            share_up, share_down, share_out, in_proj, turned, x, mid, gain_mix[None], raw, gain_two, stats,
+        ),
         4,
-    )
-    grad_flat, share_in, gain_one = call(
-        final_kernel,
-        [((tokens, width), F32), ((width, 3 * width), BF16), ((1, width), F32)],
-        [],
-        (got_back, turned, in_proj, x, mid, gain_mix[None]),
-    )
-
-    def summed(share):
-        quarter = lax.psum_scatter(share, "rows", scatter_dimension=1, tiled=True)
-        own_rows = lax.psum_scatter(quarter, "seq", scatter_dimension=0, tiled=True)
-        return lax.all_gather(own_rows, "rows", axis=1, tiled=True).astype(F32)
-
-    grad_up = summed(share_up)
-    grad_out = summed(share_out)
-    grad_inp = summed(share_in)
-    quarter = lax.psum_scatter(share_down, "rows", scatter_dimension=0, tiled=True)
-    own_cols = lax.psum_scatter(quarter, "seq", scatter_dimension=1, tiled=True)
-    grad_down = lax.all_gather(own_cols, "rows", axis=0, tiled=True).T.astype(F32)
-
-    taps_back = lax.all_to_all(grad_taps.astype(BF16), "seq", split_axis=0, concat_axis=0, tiled=True)
-    taps_back = lax.psum(taps_back.reshape(width, blocks), "rows").T.astype(F32)
-    tanh = jnp.tanh(raw / THRESH)
-    grad_kernel = (taps_back * tanh * tanh)[:, None, :]
-
-    spread = lax.dynamic_update_slice_in_dim(
-        jnp.zeros((10, width), F32), col_sums[:, :10].T, me * each, axis=1
-    )
-    gain_one, gain_two, stats, spread = lax.psum(
-        (gain_one, gain_two, jnp.sum(stats, axis=1), spread), ("rows", "seq")
-    )
+        far=(11, 12, 13, 14, 15, 16, 17, 19),
+    )
+
+    stats = jnp.sum(vectors[2:6], axis=1)
+    spread = jnp.transpose(channels[:, :10, :each], (1, 0, 2)).reshape(10, width)
     grad_tap_rows = jnp.transpose(spread[:9].reshape(3, 3, width), (1, 0, 2)).reshape(3, 3 * width)
     rms_stats = jnp.sqrt(stats[:3] / (jnp.maximum(stats[3], 1.0) * width))
     return (
         block_out.reshape(block_in.shape),
         grad_flat.reshape(block_in.shape),
-        gain_one[0],
+        vectors[0],
         grad_inp,
         grad_tap_rows,
-        grad_kernel,
+        grad_kernel[:, None, :],
         spread[9],
         grad_out,
-        gain_two[0],
+        vectors[1],
         grad_up,
         grad_down,
         rms_stats,

time: 699 us -> 318 us (0.45)
  waiting for transfers between devices: 340 us -> 0 us
  blocking collectives: 86.1 us -> 0 us
  Pallas kernels: 212 us -> 289 us
  local copies, waits for them, and re-layouts: 40.1 us -> 25.6 us
  between operations: 14.7 us -> 1.46 us
    reduce_scatter x5 -> x0, waiting for transfers between devices: 260 us -> none  [the longest x3 165 us: summed(): own_rows = lax.psum_scatter(quarter, 'seq', scatter_dimension=0, tiled=True)]
    unnamed x12 -> x0, waiting for transfers between devices: 79.9 us -> none
    pallas_call x5 -> x4, Pallas kernels: 212 us -> 289 us  [call(): pl.pallas_call(body, out_shape=tuple((jax.ShapeDtypeStruct(*out) for out...]
    psum x1 -> x0, blocking collectives: 40.5 us -> none  [local(): lax.psum((gain_one, gain_two, jnp.sum(stats, axis=1), spread), ('rows', '...]
    all_gather x4 -> x0, blocking collectives: 28.1 us -> none  [the longest x3 20.5 us: summed(): return lax.all_gather(own_rows, 'rows', axis=1, tiled=True).astype(F32)]
    all_to_all x1 -> x0, blocking collectives: 17.6 us -> none  [local(): lax.all_to_all(grad_taps.astype(BF16), 'seq', split_axis=0, concat_axis=0...]
    unnamed x41 -> x39, local copies, waits for them, and re-layouts: 30.8 us -> 20.1 us
  transfers between devices with their start and end apart: 9 -> 0, of which waited for: 7 -> 0; matrix products, arithmetic and copies ran while one was open for 4% -> 0% of each run, Pallas kernels for 10% -> 0%
where the time goes in v2:
time: 318 us; the launch traced here: 317 us
  Pallas kernels  289 us (91%)
  local copies, waits for them, and re-layouts  25.6 us (8%)
    pallas_call x4, Pallas kernels, call(): pl.pallas_call(body, out_shape=tuple((jax.ShapeDtypeStruct(*out) for out...  289 us
    unnamed x39, local copies, waits for them, and re-layouts  20.1 us

profile of v2, /device:TPU:0, one launch (start us, length us, event | category | flops | bytes accessed | tf_op | source)
XLA Modules:
  0.0 317.2 jit_solution(10202018250789939659)
XLA Ops:
  0.6 0.0 copy-start.10
  0.7 0.0 copy-start.3
  0.7 2.7 copy.46
  3.4 0.0 copy-start.9
  3.4 0.0 copy-start.13
  3.4 0.0 copy-done.10
  3.4 0.6 broadcast_in_dim.16.gain
  4.0 0.0 copy-done.3
  4.0 0.9 copy.54
  4.9 0.0 copy-done.9
  4.9 0.0 copy-done.13
  4.9 0.1 pad.13.clone
  5.0 0.7 add_add_fusion.marks
  5.7 0.0 copy-start.12
  5.7 0.0 copy-start.7
  5.7 70.1 %shard_map.247 = (bf16[2,3,10,96,256]{4,3,2,1,0:T(8,128)(2,1)}, bf16[8,96,256]{2,1,0:T(8,128)(2,1)}, s32[8,8,256]{2,1,0:T(8,128)}, bf16[2,768,256]{2,1,0:T(8,128)(2,1)}) custom-call(f32[512,768]{1,0:T(8,128)} %bitcast.30, bf16[768,2304]{1,0:T(8,128)(2,1)} %w_in_far.1, f32[1,768]{1,0:T(1,128)} %broadcast_in_dim.16.gain, f32[256,768]{1,0:T(8,128)} %bitcast.33, ...), custom_call_target="tpu_custom_call" | custom-call | tf_op jit(solution)/shard_map/pallas_call | solution.py:1255
  75.8 0.0 copy-done.12
  75.8 0.0 copy-done.7
  75.9 0.1 fusion
  76.0 0.1 copy.40
  76.1 0.6 pad.4.cols_in
  76.7 30.2 %shard_map.248 = (bf16[2,768,256]{2,1,0:T(8,128)(2,1)}, f32[3,10,2,256]{3,2,1,0:T(2,128)}, f32[8,2,96,256]{3,2,1,0:T(8,128)}, f32[2,8,2,96,256]{4,3,2,1,0:T(8,12...) custom-call(bf16[2,3,10,96,256]{4,3,2,1,0:T(8,128)(2,1)} %get-tuple-element.38.got, ...), custom_call_target="tpu_custom_call" | custom-call | tf_op jit(solution)/shard_map/pallas_call | solution.py:1255
  106.9 0.0 copy-start.11
  106.9 2.7 copy.50
  109.6 0.9 copy.41.mask_col
  110.4 0.0 copy-done.11
  110.4 0.6 broadcast_in_dim.19.gain
  111.0 39.2 %shard_map.249 = (f32[512,768]{1,0:T(8,128)}, bf16[2,8,96,256]{3,2,1,0:T(8,128)(2,1)}, f32[512,768]{1,0:T(8,128)}, bf16[2,2,2,2,2,48,1536]{6,5,4,3,2,1,0:T(8,128...) custom-call(bf16[2,768,256]{2,1,0:T(8,128)(2,1)} %get-tuple-element., ...), custom_call_target="tpu_custom_call" | custom-call | tf_op jit(solution)/shard_map/pallas_call | solution.py:1255
  150.2 4.2 %copy.43 = f32[2,256,1,768]{3,2,1,0:T(1,128)} copy(f32[2,256,1,768]{3,1,0,2:T(8,128)} %bitcast.37) | data formatting | bytes 3145728
  154.3 149.3 %shard_map.250 = (f32[512,768]{1,0:T(8,128)}, f32[96,2304]{1,0:T(8,128)}, f32[96,768]{1,0:T(8,128)}, f32[96,3072]{1,0:T(8,128)}, f32[384,768]{1,0:T(8,128)}, /*i...) custom-call(bf16[2,8,96,256]{3,2,1,0:T(8,128)(2,1)} %get-tuple-element.43.back, ...), custom_call_target="tpu_custom_call" | custom-call | tf_op jit(solution)/shard_map/pallas_call | solution.py:1255
  303.7 0.0 copy-start.8
  303.7 0.0 copy-start.6
  303.7 0.0 copy-start.4
  303.7 4.2 %copy.44 = f32[2,256,1,768]{3,2,1,0:T(1,128)} copy(f32[2,256,1,768]{3,1,0,2:T(8,128)} %bitcast.36) | data formatting | bytes 3145728
  308.0 0.0 copy-start.2
  308.0 0.0 copy-done.8
  308.0 0.6 slice_reduce_fusion.2
  308.6 0.0 copy-done.6
  308.6 0.7 reshape.71
  309.3 0.0 copy-done.4
  309.3 0.0 copy-start.5
  309.3 1.7 copy.45
  311.0 0.0 copy-start.1
  311.0 0.7 squeeze.40
  311.7 0.1 slice_reduce_fusion
  311.8 0.6 slice.49
  313.1 0.5 divide_sqrt_fusion
  313.6 0.0 copy-done.2
  313.6 0.9 copy.59
  314.5 0.0 copy-done.5
  314.5 0.0 copy-start
  314.5 0.7 copy.60
  315.2 0.0 copy-done.1
  315.2 1.0 copy.61
  316.2 0.0 copy-done
  316.2 1.0 copy.62
  (10 shorter events, 0.1 us)
Async XLA Ops:
  0.6 2.8 copy-start.10
  0.7 3.3 %copy-start.3 = (f32[256,1,768]{2,1,0:T(1,128)S(1)}, f32[256,1,768]{2,1,0:T(1,128)}, u32[]{:S(2)}) copy-start(f32[256,1,768]{2,1,0:T(1,128)} %param.23) | copy-start | bytes 2359300
  3.4 1.5 copy-start.9
  3.4 1.5 copy-start.13
  5.7 70.1 %copy-start.12 = (f32[768]{0:T(1024)S(1)}, f32[768]{0:T(1024)}, u32[]{:S(2)}) copy-start(f32[768]{0:T(1024)} %param.24) | copy-start | bytes 9220
  5.7 70.2 %copy-start.7 = (f32[3,2304]{1,0:T(4,128)S(1)}, f32[3,2304]{1,0:T(4,128)}, u32[]{:S(2)}) copy-start(f32[3,2304]{1,0:T(4,128)} %param.22) | copy-start | bytes 82948
  106.9 3.5 %copy-start.11 = (f32[768]{0:T(1024)S(1)}, f32[768]{0:T(1024)}, u32[]{:S(2)}) copy-start(f32[768]{0:T(1024)} %param.26) | copy-start | bytes 9220
  303.7 4.3 %copy-start.8 = (f32[8,768]{1,0:T(8,128)S(1)}, f32[8,768]{1,0:T(8,128)}, u32[]{:S(2)}) copy-start(f32[8,768]{1,0:T(8,128)} %get-tuple-element.57) | copy-start | bytes 73732
  303.7 4.9 %copy-start.6 = (f32[8,16,128]{2,1,0:T(8,128)S(1)}, f32[8,16,128]{2,1,0:T(8,128)}, u32[]{:S(2)}) copy-start(f32[8,16,128]{2,1,0:T(8,128)} %get-tuple-element.59) | copy-start | bytes 196612
  303.7 5.6 %copy-start.4 = (f32[256,768]{1,0:T(8,128)S(1)}, f32[256,768]{1,0:T(8,128)}, u32[]{:S(2)}) copy-start(f32[256,768]{1,0:T(8,128)} %get-tuple-element.60) | copy-start | bytes 2359300
  308.0 5.6 %copy-start.2 = (f32[96,2304]{1,0:T(8,128)S(1)}, f32[96,2304]{1,0:T(8,128)}, u32[]{:S(2)}) copy-start(f32[96,2304]{1,0:T(8,128)} %get-tuple-element.122) | copy-start | bytes 2654212
  309.3 5.2 %copy-start.5 = (f32[96,768]{1,0:T(8,128)S(1)}, f32[96,768]{1,0:T(8,128)}, u32[]{:S(2)}) copy-start(f32[96,768]{1,0:T(8,128)} %get-tuple-element.126) | copy-start | bytes 884740
  311.0 4.2 %copy-start.1 = (f32[96,3072]{1,0:T(8,128)S(1)}, f32[96,3072]{1,0:T(8,128)}, u32[]{:S(2)}) copy-start(f32[96,3072]{1,0:T(8,128)} %get-tuple-element.128) | copy-start | bytes 3538948
  314.5 1.7 copy-start

commit v3 on v0

--- a/solution.py
+++ b/solution.py
@@ -1,8 +1,12 @@
+import functools
 import math
 
 import jax
 import jax.numpy as jnp
+import numpy as np
 from jax import lax
+from jax.experimental import pallas as pl
+from jax.experimental.pallas import tpu as pltpu
 from jax.sharding import PartitionSpec as P
 
 EPS = 1e-05
@@ -106,7 +110,7 @@
     )
 
 
-def local(
+def general_local(
     block_in,
     segment_ids,
     valid_mask,
@@ -307,9 +311,1293 @@
     )
 
 
+MESH = pl.DeviceIdType.MESH
+F32 = jnp.float32
+BF16 = jnp.bfloat16
+VMEM_BYTES = 62 * 1024 * 1024
+C0 = math.sqrt(2.0 / math.pi)
+C1 = 0.044715
+ALL = slice(None)
+
+
+def dot_nn(a, b):
+    return lax.dot_general(a, b, (((1,), (0,)), ((), ())), preferred_element_type=F32)
+
+
+def dot_nt(a, b):
+    return lax.dot_general(a, b, (((1,), (1,)), ((), ())), preferred_element_type=F32)
+
+
+def fft_points(re, im, sign):
+    n = len(re)
+    if n == 1:
+        return re, im
+    even_r, even_i = fft_points(re[0::2], im[0::2], sign)
+    odd_r, odd_i = fft_points(re[1::2], im[1::2], sign)
+    out_r, out_i = [None] * n, [None] * n
+    for k in range(n // 2):
+        if k == 0:
+            turn_r, turn_i = odd_r[0], odd_i[0]
+        elif 4 * k == n:
+            if sign > 0:
+                out_r[k], out_i[k] = even_r[k] - odd_i[k], even_i[k] + odd_r[k]
+                out_r[k + n // 2], out_i[k + n // 2] = even_r[k] + odd_i[k], even_i[k] - odd_r[k]
+            else:
+                out_r[k], out_i[k] = even_r[k] + odd_i[k], even_i[k] - odd_r[k]
+                out_r[k + n // 2], out_i[k + n // 2] = even_r[k] - odd_i[k], even_i[k] + odd_r[k]
+            continue
+        else:
+            cos, sin = math.cos(2 * math.pi * k / n), sign * math.sin(2 * math.pi * k / n)
+            turn_r = cos * odd_r[k] - sin * odd_i[k]
+            turn_i = cos * odd_i[k] + sin * odd_r[k]
+        out_r[k], out_i[k] = even_r[k] + turn_r, even_i[k] + turn_i
+        out_r[k + n // 2], out_i[k + n // 2] = even_r[k] - turn_r, even_i[k] - turn_i
+    return out_r, out_i
+
+
+def spectrum_tables(blocks, n):
+    lane = np.arange(blocks)
+    span = blocks // n
+    place_in = n * (lane % span) + lane // span
+    angle = 2.0 * np.pi * place_in[:, None] * np.arange(blocks)[None, :] / blocks
+    cos, sin = np.cos(angle), np.sin(angle)
+    table = np.block([[cos, -sin], [sin, cos]])
+    turn = 2.0 * np.pi * place_in[None, :] * (2.0 * np.arange(n)[:, None] + 0.5) / (2.0 * blocks * n)
+    turns = np.stack([np.cos(turn), np.sin(turn)], axis=1)[:, :, None, :]
+    return jnp.asarray(table, BF16), jnp.asarray(np.broadcast_to(turns, (n, 2, 8, blocks)), F32)
+
+
+def place():
+    row, seq = lax.axis_index("rows"), lax.axis_index("seq")
+    return lax.div(row, 2), lax.rem(row, 2), lax.div(seq, 4), lax.rem(lax.div(seq, 2), 2), lax.rem(seq, 2)
+
+
+def partner(axis):
+    y, c, zh, zl, x = place()
+    if axis == "core":
+        return {"rows": 2 * y + 1 - c}
+    if axis == "y":
+        return {"rows": 2 * (1 - y) + c}
+    if axis == "x":
+        return {"seq": 4 * zh + 2 * zl + 1 - x}
+    if axis == "zl":
+        return {"seq": 4 * zh + 2 * (1 - zl) + x}
+    return {"seq": 4 * (1 - zh) + 2 * zl + x}
+
+
+def remote(src, dst, send_sem, recv_sem, target):
+    return pltpu.make_async_remote_copy(
+        src_ref=src, dst_ref=dst, send_sem=send_sem, recv_sem=recv_sem, device_id=target, device_id_type=MESH,
+    )
+
+
+def exchange(src, dst, send_sem, recv_sem, axis):
+    return remote(src, dst, send_sem, recv_sem, partner(axis))
+
+
+def greet(n):
+    me = lax.axis_index("seq")
+    barrier = pltpu.get_barrier_semaphore()
+    for j in range(1, n):
+        pl.semaphore_signal(barrier, inc=1, device_id={"seq": lax.rem(me + j, n)}, device_id_type=MESH)
+    for axis in ("core", "y"):
+        pl.semaphore_signal(barrier, inc=1, device_id=partner(axis), device_id_type=MESH)
+    return barrier, n + 1
+
+
+def aligned(index, size):
+    return pl.ds(pl.multiple_of(index * size, size), size)
+
+
+class Post:
+    def __init__(self, n, source, target, sems):
+        self.n, self.source, self.target, self.sems = n, source, target, sems
+
+    def copies(self, sender):
+        me = lax.axis_index("seq")
+        for j in range(1, self.n):
+            peer = lax.rem(me + j, self.n)
+            come = sender(peer, me)
+            yield remote(
+                self.source(peer), self.target(come), self.sems.at[0, j], self.sems.at[1, come], {"seq": peer}
+            )
+
+    def start(self):
+        me = lax.axis_index("seq")
+        for copy in self.copies(lambda peer, me: me):
+            copy.start()
+        self.target(me)[...] = self.source(me)[...]
+
+    def arrive(self):
+        for copy in self.copies(lambda peer, me: peer):
+            copy.wait_recv()
+
+    def drain(self):
+        for copy in self.copies(lambda peer, me: me):
+            copy.wait_send()
+
+
+def over_groups(each, blocks, body):
+    for lane in range(0, blocks, 128):
+        def step(g, carry):
+            body(pl.multiple_of(g * 16, 16), lane)
+            return carry
+        lax.fori_loop(0, each // 16, step, 0)
+
+
+def matmul_rows(out, left, right, size=256):
+    for at in range(0, out.shape[0], size):
+        out[at:at + size, :] = left(at, size, right)
+
+
+def to_spectrum(n, source, table, turns, fin, spec):
+    each, blocks = spec.shape[0] // n, spec.shape[1] // 2
+
+    def group(at, lane):
+        loaded = [source(d, pl.ds(at, 16), pl.ds(lane, 128)).astype(F32) for d in range(n)]
+        halves = []
+        for half in (0, 8):
+            re, im = [], []
+            for d in range(n):
+                value = loaded[d][half:half + 8]
+                angle = 2.0 * math.pi * d / (4.0 * n)
+                re.append(value * math.cos(angle))
+                im.append(value * -math.sin(angle))
+            re, im = fft_points(re, im, -1)
+            turned = []
+            for k in range(n):
+                cos, sin = turns[k, 0, :, lane:lane + 128], turns[k, 1, :, lane:lane + 128]
+                turned.append((re[k] * cos + im[k] * sin, im[k] * cos - re[k] * sin))
+            halves.append(turned)
+        for k in range(n):
+            for part in range(2):
+                value = jnp.concatenate([halves[0][k][part], halves[1][k][part]], axis=0)
+                fin[pl.ds(k * each + at, 16), part * blocks + lane:part * blocks + lane + 128] = value.astype(BF16)
+
+    over_groups(each, blocks, group)
+    for at in range(0, spec.shape[0], 256):
+        spec[at:at + 256, :] = dot_nn(fin[at:at + 256, :], table[...])
+
+
+def from_spectrum(n, fin, table, turns, spec, store):
+    each, blocks = spec.shape[0] // n, spec.shape[1] // 2
+    for at in range(0, spec.shape[0], 256):
+        spec[at:at + 256, :] = dot_nt(fin[at:at + 256, :], table[...])
+    scale = 1.0 / (n * blocks)
+
+    def group(at, lane):
+        halves = []
+        for half in (0, 8):
+            re, im = [], []
+            for k in range(n):
+                rows = pl.ds(k * each + at + half, 8)
+                cos, sin = turns[k, 0, :, lane:lane + 128], turns[k, 1, :, lane:lane + 128]
+                old_r, old_i = spec[rows, lane:lane + 128], spec[rows, blocks + lane:blocks + lane + 128]
+                re.append(old_r * cos - old_i * sin)
+                im.append(old_i * cos + old_r * sin)
+            re, im = fft_points(re, im, 1)
+            out = []
+            for d in range(n):
+                angle = 2.0 * math.pi * d / (4.0 * n)
+                out.append(re[d] * (scale * math.cos(angle)) - im[d] * (scale * math.sin(angle)))
+            halves.append(out)
+        for d in range(n):
+            store(d, pl.ds(at, 16), pl.ds(lane, 128), jnp.concatenate([halves[0][d], halves[1][d]], axis=0))
+
+    over_groups(each, blocks, group)
+
+
+def over_rows(total, size, body):
+    def step(i, carry):
+        body(aligned(i, size))
+        return carry
+    lax.fori_loop(0, total // size, step, 0)
+
+
+def over_lanes(width, body):
+    def step(i, carry):
+        body(aligned(i, 128))
+        return carry
+    lax.fori_loop(0, width // 128, step, 0)
+
+
+def front_kernel(
+    n, chunk,
+    x_far, cot_far, taps_far, marks_in, gain_one, gain_two, w_in_far, w_out_far, w_up_far, w_down_far, weights, table, turns,
+    seen_out, proj_out, turned_out, saved_out, same_out, spec_taps_out, spec_gate_out, back_out,
+    share_up_out, share_down_out, share_out_out, vectors,
+    marks, mark_ends, marks_got, mark_ends_got, x_sent, cot_sent, ends, ends_sent, ends_got, ends_wide,
+    taps_sent, taps_chunk, taps_turned, taps_got,
+    seen, cot, query, saved, same, spec_gate, gate_sent, gate_got, long_sent, long_got, back_sent, back_got,
+    w_out, w_up, w_down, fetch, keep, x_sems, mark_sems, cot_sems, end_sems, tap_sems, gate_sems, long_sems, back_sems,
+):
+    me = lax.axis_index("seq")
+    y, c, zh, zl, xbit = place()
+    rows, blocks, width = x_sent.shape
+    hidden = w_up.shape[1]
+    each, span = width // n, blocks // n
+    ext = blocks + 2 * span
+    wide = width // 128
+    barrier, told = greet(n)
+
+    fetch_out = pltpu.make_async_copy(w_out_far, w_out, fetch.at[0])
+    fetch_up = pltpu.make_async_copy(w_up_far, w_up, fetch.at[1])
+    fetch_down = pltpu.make_async_copy(w_down_far, w_down, fetch.at[2])
+    posts_x = [
+        Post(n, lambda d, r=r: x_sent.at[r, aligned(d, span)], lambda p, r=r: seen.at[r, p + 2], x_sems.at[r])
+        for r in range(rows)
+    ]
+    posts_cot = [
+        Post(n, lambda d, r=r: cot_sent.at[r, aligned(d, span)], lambda p, r=r: cot.at[r, p], cot_sems.at[r])
+        for r in range(rows)
+    ]
+    post_marks = Post(n, lambda d: marks.at[aligned(d, span)], lambda p: marks_got.at[p + 2], mark_sems)
+    posts_gate = [
+        Post(n, lambda e, r=r: gate_sent.at[r, aligned(e, each)], lambda d, r=r: gate_got.at[r, d], gate_sems.at[r])
+        for r in range(rows)
+    ]
+    posts_long = [
+        Post(n, lambda d, r=r: long_sent.at[r, d], lambda e, r=r: long_got.at[r, aligned(e, each)], long_sems.at[r])
+        for r in range(rows)
+    ]
+    posts_back = [
+        Post(n, lambda e, r=r: back_sent.at[r, aligned(e, each)], lambda d, r=r: back_got.at[r, d], back_sems.at[r])
+        for r in range(rows)
+    ]
+
+    def end_copies(j, slot, peer):
+        return (
+            remote(ends_sent, ends_got.at[slot], end_sems.at[0, j], end_sems.at[2, slot], {"seq": peer}),
+            remote(mark_ends, mark_ends_got.at[slot], end_sems.at[1, j], end_sems.at[3, slot], {"seq": peer}),
+        )
+
+    def tap_hop_one(xd):
+        target = 4 * y + 2 * c + xd
+        return remote(taps_sent.at[y, c, xd], taps_chunk.at[me], tap_sems.at[0, xd], tap_sems.at[1, me], {"seq": target})
+
+    def tap_hop_two(j, slot, peer):
+        return remote(
+            taps_turned.at[aligned(peer, each)], taps_got.at[y, c, slot], tap_sems.at[2, j], tap_sems.at[3, slot], {"seq": peer}
+        )
+
+    def tap_core():
+        return exchange(taps_got.at[y, c], taps_got.at[y, c], tap_sems.at[4, 0], tap_sems.at[4, 1], "core")
+
+    def tap_y():
+        return exchange(taps_got.at[y], taps_got.at[y], tap_sems.at[4, 2], tap_sems.at[4, 3], "y")
+
+    chosen_chunk = jnp.logical_and(zh == y, zl == c)
+    sends_ends = me >= n - 2
+
+    def front(x, cot_in, taps, w_in, normed, turned, proj, gate_wide, fin, spec, spec_taps):
+        first = [
+            pltpu.make_async_copy(src, dst, fetch.at[3 + i])
+            for i, (src, dst) in enumerate(((x_far, x), (taps_far, taps), (w_in_far, w_in), (cot_far, cot_in)))
+        ]
+        for copy in first + [fetch_out, fetch_up, fetch_down]:
+            copy.start()
+        marks[...] = jnp.zeros_like(marks)
+        marks[:, 0:8] = marks_in[...].T
+        first[0].wait()
+
+        def narrow(source, r, target):
+            for j in range(wide):
+                target[r, :, j * 128:(j + 1) * 128] = source[pl.ds(r * blocks * wide + j, blocks, stride=wide), :].astype(BF16)
+
+        narrow(x, 0, x_sent)
+        pl.semaphore_wait(barrier, told)
+        posts_x[0].start()
+        post_marks.start()
+        ends[...] = jnp.zeros_like(ends)
+        for r in range(rows):
+            for d in range(1, n):
+                at = (r * blocks + d * span - 1) * wide
+                for j in range(wide):
+                    ends[r * n + d:r * n + d + 1, j * 128:(j + 1) * 128] = x[at + j:at + j + 1, :]
+        ends_sent[...] = ends[...].astype(BF16)
+        mark_ends[0:1, :] = jnp.full((1, 128), -1.0, F32)
+        for d in range(1, n):
+            mark_ends[d:d + 1, :] = marks[d * span - 1:d * span, :]
+
+        @pl.when(sends_ends)
+        def _():
+            for j in range(1, n):
+                for copy in end_copies(j, me - (n - 2), lax.rem(me + j, n)):
+                    copy.start()
+            ends_got[me - (n - 2)] = ends_sent[...]
+            mark_ends_got[me - (n - 2)] = mark_ends[...]
+
+        narrow(x, 1, x_sent)
+        posts_x[1].start()
+        first[1].wait()
+        for j in range(wide):
+            raw = taps[pl.ds(j, blocks, stride=wide), :]
+            low = (raw - THRESH * jnp.tanh(raw * (1.0 / THRESH))).astype(BF16)
+            for d in range(n):
+                taps_sent[d // 4, (d // 2) % 2, d % 2, :, j * 128:(j + 1) * 128] = low[d * span:(d + 1) * span]
+        for xd in range(2):
+            target = 4 * y + 2 * c + xd
+
+            @pl.when(target != me)
+            def _():
+                tap_hop_one(xd).start()
+
+            @pl.when(target == me)
+            def _():
+                taps_chunk[me] = taps_sent[y, c, xd]
+
+        first[3].wait()
+        for r in range(rows):
+            narrow(cot_in, r, cot_sent)
+
+        for slot in range(2):
+            @pl.when(me != n - 2 + slot)
+            def _():
+                for copy in end_copies(0, slot, n - 2 + slot):
+                    copy.wait_recv()
+        ends_wide[...] = ends_got[...].astype(F32)
+        post_marks.arrive()
+        top = lax.broadcasted_iota(jnp.int32, (span, 128), 0) == 0
+        for slot in range(2):
+            moved = pltpu.roll(marks_got[n + slot], 1, 0)
+            marks_got[slot] = jnp.where(top, mark_ends_got[slot, pl.ds(me, 1), :], moved)
+        first[2].wait()
+
+        def chunk_row(r):
+            posts_x[r].arrive()
+            top_row = lax.broadcasted_iota(jnp.int32, (span, width), 0) == 0
+            for slot in range(2):
+                moved = pltpu.roll(seen[r, n + slot].astype(F32), 1, 0)
+                seen[r, slot] = jnp.where(top_row, ends_wide[slot, pl.ds(r * n + me, 1), :], moved).astype(BF16)
+            marked = marks_got[...].reshape(ext, 128)
+            seg = marked[:, r:r + 1]
+            now, one, two = seg[2 * span:], seg[span:ext - span], seg[:blocks]
+            same[0, r] = jnp.broadcast_to((now == one).astype(F32), (blocks, 128))
+            same[1, r] = jnp.broadcast_to((now == two).astype(F32), (blocks, 128))
+            same[2, r] = jnp.broadcast_to(marked[2 * span:, rows + r:rows + r + 1], (blocks, 128))
+            for p in range(n + 2):
+                value = seen[r, p].astype(F32)
+                scale = lax.rsqrt(jnp.mean(value * value, axis=-1, keepdims=True) + EPS)
+                normed[r, p * span:(p + 1) * span, :] = (value * scale * gain_one[...]).astype(BF16)
+            for k in (1, 2, 0):
+                for at in range(0, width, 256):
+                    cols = slice(k * width + at, k * width + at + 256)
+                    proj[r, k, :, at:at + 256] = dot_nn(normed[r], w_in[:, cols]).astype(BF16)
+
+            def lanes_step(lanes):
+                for p in range(n):
+                    here = slice(p * span, (p + 1) * span)
+                    one_mask, two_mask, mask = same[0, r, here, :], same[1, r, here, :], same[2, r, here, :]
+                    value = []
+                    for k in range(3):
+                        total = weights[3 * k:3 * k + 1, lanes] * proj[r, k, (p + 2) * span:(p + 3) * span, lanes].astype(F32)
+                        total += weights[3 * k + 1:3 * k + 2, lanes] * (proj[r, k, (p + 1) * span:(p + 2) * span, lanes].astype(F32) * one_mask)
+                        total += weights[3 * k + 2:3 * k + 3, lanes] * (proj[r, k, p * span:(p + 1) * span, lanes].astype(F32) * two_mask)
+                        value.append(total)
+                    query[r, here, lanes] = value[0].astype(BF16)
+                    keys, values = value[1] * mask, value[2] * mask
+                    gate = value[1] * values
+                    saved[0, r, here, lanes] = keys.astype(BF16)
+                    saved[1, r, here, lanes] = values.astype(BF16)
+                    saved[2, r, here, lanes] = gate.astype(BF16)
+                    gate_wide[here, lanes] = gate
+
+            over_lanes(width, lanes_step)
+            gate_sent[r] = gate_wide[...].T.astype(BF16)
+            posts_gate[r].start()
+
+        chunk_row(0)
+
+        @pl.when(chosen_chunk)
+        def _():
+            for p in range(n):
+                @pl.when(me != p)
+                def _():
+                    remote(taps_sent.at[y, c, 0], taps_chunk.at[p], tap_sems.at[0, 0], tap_sems.at[1, p], {"seq": p}).wait_recv()
+            taps_turned[...] = taps_chunk[...].reshape(blocks, width).astype(F32).T.astype(BF16)
+            for j in range(1, n):
+                tap_hop_two(j, xbit, lax.rem(me + j, n)).start()
+            taps_got[y, c, xbit] = taps_turned[aligned(me, each)]
+
+        chunk_row(1)
+        for xd in range(2):
+            @pl.when(4 * y + 2 * c + xd != me)
+            def _():
+                tap_hop_two(0, xd, 4 * y + 2 * c + xd).wait_recv()
+        tap_core().start()
+        for r in range(rows):
+            posts_cot[r].start()
+        for r in range(rows):
+            turned[:, r * ext:(r + 1) * ext] = normed[r].T
+        tap_core().wait_recv()
+        tap_y().start()
+        keeps = [
+            pltpu.make_async_copy(src, dst, keep.at[i])
+            for i, (src, dst) in enumerate(((seen, seen_out), (proj, proj_out), (turned, turned_out)))
+        ]
+        for copy in keeps:
+            copy.start()
+        tap_y().wait_recv()
+        to_spectrum(n, lambda d, at, lanes: taps_got[d // 4, (d // 2) % 2, d % 2, at, lanes], table, turns, fin, spec)
+        spec_taps[...] = spec[...]
+        keeps.append(pltpu.make_async_copy(spec_taps, spec_taps_out, keep.at[3]))
+        keeps[3].start()
+
+        for r in range(rows):
+            posts_gate[r].arrive()
+            to_spectrum(n, lambda d, at, lanes: gate_got[r, d, at, lanes], table, turns, fin, spec)
+
+            def product(part):
+                re, im = spec[part, 0:blocks], spec[part, blocks:2 * blocks]
+                tap_r, tap_i = spec_taps[part, 0:blocks], spec_taps[part, blocks:2 * blocks]
+                spec_gate[r, part, 0:blocks] = re.astype(BF16)
+                spec_gate[r, part, blocks:2 * blocks] = im.astype(BF16)
+                fin[part, 0:blocks] = (re * tap_r - im * tap_i).astype(BF16)
+                fin[part, blocks:2 * blocks] = (re * tap_i + im * tap_r).astype(BF16)
+
+            over_rows(width, 32, product)
+
+            def store(d, at, lanes, value):
+                long_sent[r, d, at, lanes] = value.astype(BF16)
+
+            from_spectrum(n, fin, table, turns, spec, store)
+            posts_long[r].start()
+        for copy in keeps:
+            copy.wait()
+
+    pl.run_scoped(
+        front,
+        pltpu.VMEM(x_far.shape, F32),
+        pltpu.VMEM(cot_far.shape, F32),
+        pltpu.VMEM(taps_far.shape, F32),
+        pltpu.VMEM(w_in_far.shape, BF16),
+        pltpu.VMEM((rows, ext, width), BF16),
+        pltpu.VMEM((width, rows * ext), BF16),
+        pltpu.VMEM((rows, 3, ext, width), BF16),
+        pltpu.VMEM((blocks, width), F32),
+        pltpu.VMEM((width, 2 * blocks), BF16),
+        pltpu.VMEM((width, 2 * blocks), F32),
+        pltpu.VMEM((width, 2 * blocks), F32),
+    )
+    later_keeps = [
+        pltpu.make_async_copy(spec_gate, spec_gate_out, keep.at[4]),
+        pltpu.make_async_copy(same, same_out, keep.at[5]),
+    ]
+    for copy in later_keeps:
+        copy.start()
+
+    def middle(act, grad_act, resid, long_out, acc_out, acc_back, normed, turned, turned_cot, mixed, mix_back, up, down, out):
+        vectors[...] = jnp.zeros_like(vectors)
+        fetch_out.wait()
+        for r in range(rows):
+            tokens = slice(r * blocks, (r + 1) * blocks)
+            posts_long[r].arrive()
+            gated = saved[2, r].astype(F32)
+            long_out[...] = long_got[r].astype(F32).T + weights[9:10, :] * gated
+            low = (query[r].astype(F32) * long_out[...]).astype(BF16)
+            mixer = dot_nn(low, w_out[...])
+            mixed[r] = low.T
+            mask = same[2, r, :, 0:1]
+            vectors[1:2, :] += jnp.sum(mixer * mixer * mask, axis=0, keepdims=True)
+            values = seen[r, 2:n + 2].reshape(blocks, width).astype(F32)
+            state = values + mixer
+            resid[...] = state
+            scale = lax.rsqrt(jnp.mean(state * state, axis=-1, keepdims=True) + EPS)
+            normed[...] = (state * scale * gain_two[...]).astype(BF16)
+            acc_out[...] = mixer
+            acc_back[...] = jnp.zeros_like(acc_back)
+            if r == 0:
+                fetch_up.wait()
+                fetch_down.wait()
+            posts_cot[r].arrive()
+
+            def hidden_step(j, carry):
+                cols = aligned(j, chunk)
+                up_val = dot_nn(normed[...], w_up[:, cols])
+                square = up_val * up_val
+                tanh = jnp.tanh(up_val * (C0 + (C0 * C1) * square))
+                half = 0.5 * (1.0 + tanh)
+                act_low = (up_val * half).astype(BF16)
+                slope = half + (0.5 * up_val) * (1.0 - tanh * tanh) * (C0 + (3.0 * C0 * C1) * square)
+                act[tokens, cols] = act_low
+                acc_out[...] += dot_nn(act_low, w_down[cols, :])
+                grad = dot_nt(cot[r].reshape(blocks, width), w_down[cols, :])
+                grad_low = (grad * slope).astype(BF16)
+                grad_act[tokens, cols] = grad_low
+                acc_back[...] += dot_nt(grad_low, w_up[:, cols])
+                return carry
+
+            lax.fori_loop(0, hidden // chunk, hidden_step, 0)
+            state = resid[...]
+            scale = lax.rsqrt(jnp.mean(state * state, axis=-1, keepdims=True) + EPS)
+            grad = acc_back[...]
+            vectors[4:5, :] += jnp.sum(grad * state * scale, axis=0, keepdims=True)
+            scaled = grad * gain_two[...]
+            shift = jnp.mean(scaled * state, axis=-1, keepdims=True) * (scale * scale * scale)
+            change = scaled * scale - state * shift
+            saved[5, r] = change.astype(BF16)
+            mix_back[r] = (cot[r].reshape(blocks, width).astype(F32) + change).astype(BF16)
+            grad_prod = dot_nt(mix_back[r], w_out[...])
+            grad_long = grad_prod * query[r].astype(F32)
+            back_sent[r] = grad_long.T.astype(BF16)
+            posts_back[r].start()
+            saved[3, r] = grad_long.astype(BF16)
+            saved[4, r] = (grad_prod * long_out[...]).astype(BF16)
+            vectors[5:6, :] += jnp.sum(grad_long * saved[2, r].astype(F32), axis=0, keepdims=True)
+            both = acc_out[...]
+            saved[6, r] = both.astype(BF16)
+            mixer = state - seen[r, 2:n + 2].reshape(blocks, width).astype(F32)
+            mlp = both - mixer
+            vectors[2:3, :] += jnp.sum(mlp * mlp * mask, axis=0, keepdims=True)
+            whole = state + mlp
+            vectors[0:1, :] += jnp.sum(whole * whole * mask, axis=0, keepdims=True)
+            vectors[3:4, :] += jnp.broadcast_to(jnp.sum(mask, axis=0, keepdims=True) * (1.0 / width), (1, width))
+            turned[:, tokens] = normed[...].T
+            turned_cot[:, tokens] = cot[r].reshape(blocks, width).T
+
+        kept = [pltpu.make_async_copy(saved, saved_out, keep.at[6])]
+        kept[0].start()
+        side, quarter, part = each // 2, width // 4, hidden // n
+
+        def put_rows(share, half, lanes, value):
+            for s in range(n):
+                for core in range(2):
+                    low = (2 * s + core) * side
+                    share[s // 4, (s // 2) % 2, s % 2, core, half, :, lanes] = value[low:low + side]
+
+        for half in range(2):
+            for low in range(0, hidden // 2, chunk):
+                cols = slice(half * (hidden // 2) + low, half * (hidden // 2) + low + chunk)
+                put_rows(up, half, slice(low, low + chunk), dot_nn(turned[...], grad_act[:, cols]).astype(BF16))
+        kept.append(pltpu.make_async_copy(up, share_up_out, keep.at[7]))
+        kept[-1].start()
+        for s in range(n):
+            value = dot_nn(turned_cot[...], act[:, s * part:(s + 1) * part]).astype(BF16)
+            for core in range(2):
+                for half in range(2):
+                    low = (2 * core + half) * quarter
+                    down[s // 4, (s // 2) % 2, s % 2, core, half] = value[low:low + quarter]
+        kept.append(pltpu.make_async_copy(down, share_down_out, keep.at[8]))
+        kept[-1].start()
+        for half in range(2):
+            low = half * (width // 2)
+            value = sum(dot_nn(mixed[r], mix_back[r, :, low:low + width // 2]) for r in range(rows)).astype(BF16)
+            put_rows(out, half, ALL, value)
+        kept.append(pltpu.make_async_copy(out, share_out_out, keep.at[9]))
+        kept[-1].start()
+        for r in range(rows):
+            posts_back[r].arrive()
+        kept.append(pltpu.make_async_copy(back_got, back_out, keep.at[10]))
+        kept[-1].start()
+        for copy in kept:
+            copy.wait()
+
+    pl.run_scoped(
+        middle,
+        pltpu.VMEM((rows * blocks, hidden), BF16),
+        pltpu.VMEM((rows * blocks, hidden), BF16),
+        pltpu.VMEM((blocks, width), F32),
+        pltpu.VMEM((blocks, width), F32),
+        pltpu.VMEM((blocks, width), F32),
+        pltpu.VMEM((blocks, width), F32),
+        pltpu.VMEM((blocks, width), BF16),
+        pltpu.VMEM((width, rows * blocks), BF16),
+        pltpu.VMEM((width, rows * blocks), BF16),
+        pltpu.VMEM((rows, width, blocks), BF16),
+        pltpu.VMEM((rows, blocks, width), BF16),
+        pltpu.VMEM(share_up_out.shape, BF16),
+        pltpu.VMEM(share_down_out.shape, BF16),
+        pltpu.VMEM(share_out_out.shape, BF16),
+    )
+    for copy in later_keeps:
+        copy.wait()
+    for post in posts_x + posts_cot + [post_marks] + posts_gate + posts_long + posts_back:
+        post.drain()
+
+    @pl.when(sends_ends)
+    def _():
+        for j in range(1, n):
+            for copy in end_copies(j, me - (n - 2), lax.rem(me + j, n)):
+                copy.wait_send()
+
+    for xd in range(2):
+        @pl.when(4 * y + 2 * c + xd != me)
+        def _():
+            tap_hop_one(xd).wait_send()
+
+    @pl.when(chosen_chunk)
+    def _():
+        for j in range(1, n):
+            tap_hop_two(j, xbit, lax.rem(me + j, n)).wait_send()
+
+    tap_core().wait_send()
+    tap_y().wait_send()
+
+
+class Tree:
+    def __init__(self, order, share, own, parts, gathered, sems):
+        self.order = ("core",) + order + ("zl", "zh", "back_y", "back_core")
+        self.share, self.own, self.parts, self.gathered, self.sems = share, own, parts, gathered, sems
+        self.started = []
+
+    def copies(self, step):
+        y, c, zh, zl, x = place()
+        axis = self.order[step]
+        parts, gathered = self.parts, self.gathered
+        own = self.share.at[:, :, :, c] if self.own is None else self.own
+        second = self.order[1]
+        if axis == "core":
+            src, dst = self.share.at[:, :, :, 1 - c], parts[0]
+        elif axis == "y":
+            src = own.at[:, :, :, 1 - y] if second == "y" else own.at[:, :, x, 1 - y]
+            dst = parts[step]
+        elif axis == "x":
+            src = own.at[:, :, 1 - x] if second == "x" else own.at[:, :, 1 - x, y]
+            dst = parts[step]
+        elif axis == "zl":
+            src, dst = own.at[:, 1 - zl, x, y], parts[3]
+        elif axis == "zh":
+            src, dst = own.at[1 - zh, zl, x, y], parts[4]
+        elif axis == "back_y":
+            src = dst = gathered.at[c, y]
+        else:
+            src = dst = gathered.at[c]
+        return exchange(src, dst, self.sems.at[0, step], self.sems.at[1, step], axis.replace("back_", ""))
+
+    def start(self, step):
+        self.copies(step).start()
+        self.started.append(step)
+
+    def mine(self, a, b, d, e):
+        c = place()[1]
+        return (self.share, (a, b, d, c, e)) if self.own is None else (self.own, (a, b, d, e))
+
+    def add(self, where, part):
+        rows = self.share.shape[-2]
+        size = 48 if rows % 48 == 0 else rows
+        own, where = self.mine(*where)
+
+        def body(i, carry):
+            here = aligned(i, size)
+            own[where + (here, ALL)] = own[where + (here, ALL)] + part[0][part[1] + (here, ALL)]
+            return carry
+
+        lax.fori_loop(0, rows // size, body, 0)
+
+    def finish(self, step):
+        y, c, zh, zl, x = place()
+        axis = self.order[step]
+        self.copies(step).wait_recv()
+        second = self.order[1]
+        two = range(2)
+        if axis == "core":
+            for a in two:
+                for b in two:
+                    for d in two:
+                        for e in two:
+                            self.add((a, b, d, e), (self.parts[0], (a, b, d, e)))
+        elif axis in ("x", "y"):
+            for a in two:
+                for b in two:
+                    if step == 2:
+                        self.add((a, b, x, y), (self.parts[2], (a, b)))
+                    else:
+                        for d in two:
+                            self.add((a, b, d, y) if second == "y" else (a, b, x, d), (self.parts[1], (a, b, d)))
+        elif axis == "zl":
+            for a in two:
+                self.add((a, zl, x, y), (self.parts[3], (a,)))
+        elif axis == "zh":
+            own, where = self.mine(zh, zl, x, y)
+            self.gathered[c, y] = own[where] + self.parts[4][...]
+        if step + 1 < len(self.order):
+            self.start(step + 1)
+
+    def drain(self):
+        for step in self.started:
+            self.copies(step).wait_send()
+
+
+def tree_scratch(r, l):
+    shapes = [(2, 2, 2, 2, r, l)] * 2 + [(2, 2, 2, r, l), (2, 2, r, l), (2, r, l), (r, l), (2, 2, r, l)]
+    return [pltpu.VMEM(shape, BF16) for shape in shapes] + [pltpu.SemaphoreType.DMA((2, 7))]
+
+
+def back_kernel(
+    n,
+    back_far, spec_taps_far, spec_gate_far, table, turns, share_up, share_down, share_out, saved_far, proj_far, turned_far,
+    seen_far, same_far, w_in_far, weights, gain_one, sums_in, x_far, cot_far, taps_far,
+    out, grad_flat, grad_in, grad_out, grad_up, grad_down, grad_kernel, vectors,
+    gate_sent, gate_got, out_got, grad_sent, grad_got, end_got, out_sems, gate_sems, grad_sems, end_sems, fetch,
+    tap_own, tap_one, tap_two, tap_rows, tap_cols, tap_home, tap_sems, tap_send, tap_recv,
+    vector_got, vector_sems,
+    *tree_refs,
+):
+    me = lax.axis_index("seq")
+    y, c, zh, zl, xbit = place()
+    rows, blocks, width = gate_got.shape[0], gate_got.shape[2], gate_got.shape[1]
+    each, span = width // n, blocks // n
+    ext, wide, side = blocks + 2 * span, width // 128, each // 2
+    barrier, told = greet(n)
+
+    trees, at = {}, 0
+    for name, share, order in (("up", share_up, ("y", "x")), ("down", share_down, ("x", "y")), ("out", share_out, ("y", "x"))):
+        trees[name] = Tree(order, share, tree_refs[at], tree_refs[at + 1:at + 6], tree_refs[at + 6], tree_refs[at + 7])
+        at += 8
+    for name, order in (("in0", ("y", "x")), ("in1", ("x", "y")), ("in2", ("y", "x"))):
+        trees[name] = Tree(order, None, None, tree_refs[at:at + 5], tree_refs[at + 5], tree_refs[at + 6])
+        at += 7
+    early = ("up", "down", "out")
+
+    posts_out = [
+        Post(n, lambda p, r=r: saved_far.at[6, r, aligned(p, span)], lambda d, r=r: out_got.at[r, aligned(d, span)], out_sems.at[r])
+        for r in range(rows)
+    ]
+    posts_gate = [
+        Post(n, lambda d, r=r: gate_sent.at[r, d], lambda e, r=r: gate_got.at[r, aligned(e, each)], gate_sems.at[r])
+        for r in range(rows)
+    ]
+    posts_grad = [
+        Post(n, lambda p, r=r: grad_sent.at[r, p + 2], lambda d, r=r: grad_got.at[r, aligned(d, span)], grad_sems.at[r])
+        for r in range(rows)
+    ]
+    tall = 16
+
+    def end_copy(r, slot, sender):
+        return remote(
+            grad_sent.at[r, slot, 0:tall], end_got.at[r, sender], end_sems.at[0, r, slot], end_sems.at[1, r, sender], {"seq": n - 2 + slot}
+        )
+
+    def tap_core():
+        return exchange(tap_own.at[:, 1 - c], tap_one, tap_sems.at[0, 0], tap_sems.at[1, 0], "core")
+
+    def tap_y():
+        return exchange(tap_own.at[1 - y, c], tap_two, tap_sems.at[0, 1], tap_sems.at[1, 1], "y")
+
+    def tap_hop_one(xd):
+        target = 4 * y + 2 * c + xd
+        return remote(tap_own.at[y, c, xd], tap_rows.at[aligned(me, each)], tap_send.at[0, xd], tap_recv.at[0, me], {"seq": target})
+
+    def tap_hop_two(j, slot, peer):
+        return remote(tap_cols.at[peer], tap_home.at[y, c, slot], tap_send.at[1, j], tap_recv.at[1, slot], {"seq": peer})
+
+    def tap_back_core():
+        return exchange(tap_home.at[y, c], tap_home.at[y, c], tap_sems.at[0, 2], tap_sems.at[1, 2], "core")
+
+    def tap_back_y():
+        return exchange(tap_home.at[y], tap_home.at[y], tap_sems.at[0, 3], tap_sems.at[1, 3], "y")
+
+    chosen_chunk = jnp.logical_and(zh == y, zl == c)
+    own_halves = [
+        pltpu.make_async_copy(trees[name].share.at[:, :, :, c], trees[name].own, fetch.at[i]) for i, name in enumerate(early)
+    ]
+
+    def conv_phase(back, spec_taps, spec_gate, fin, spec, spec_sum):
+        near = [
+            pltpu.make_async_copy(src, dst, fetch.at[3 + i])
+            for i, (src, dst) in enumerate(((back_far, back), (spec_taps_far, spec_taps), (spec_gate_far, spec_gate)))
+        ]
+        for copy in near + own_halves:
+            copy.start()
+        pl.semaphore_wait(barrier, told)
+        for name in early:
+            trees[name].start(0)
+        for copy in near:
+            copy.wait()
+        for r in range(rows):
+            to_spectrum(n, lambda d, at, lanes: back[r, d, at, lanes], table, turns, fin, spec)
+
+            def product(part):
+                re, im = spec[part, 0:blocks], spec[part, blocks:2 * blocks]
+                tap_r, tap_i = spec_taps[part, 0:blocks], spec_taps[part, blocks:2 * blocks]
+                gate_r, gate_i = spec_gate[r, part, 0:blocks].astype(F32), spec_gate[r, part, blocks:2 * blocks].astype(F32)
+                sum_r, sum_i = gate_r * re + gate_i * im, gate_r * im - gate_i * re
+                if r == 0:
+                    spec_sum[part, 0:blocks] = sum_r
+                    spec_sum[part, blocks:2 * blocks] = sum_i
+                else:
+                    spec_sum[part, 0:blocks] += sum_r
+                    spec_sum[part, blocks:2 * blocks] += sum_i
+                fin[part, 0:blocks] = (tap_r * re + tap_i * im).astype(BF16)
+                fin[part, blocks:2 * blocks] = (tap_r * im - tap_i * re).astype(BF16)
+
+            over_rows(width, 32, product)
+
+            def store(d, at, lanes, value):
+                gate_sent[r, d, at, lanes] = value.astype(BF16)
+
+            from_spectrum(n, fin, table, turns, spec, store)
+            posts_gate[r].start()
+            if r == 0:
+                for i, name in enumerate(early):
+                    own_halves[i].wait()
+                    trees[name].finish(0)
+        for at in range(0, width, 256):
+            fin[at:at + 256, :] = spec_sum[at:at + 256, :].astype(BF16)
+
+        def store_taps(d, at, lanes, value):
+            tap_own[d // 4, (d // 2) % 2, d % 2, at, lanes] = value.astype(BF16)
+
+        from_spectrum(n, fin, table, turns, spec, store_taps)
+        tap_core().start()
+
+    pl.run_scoped(
+        conv_phase,
+        pltpu.VMEM((rows, n, each, blocks), BF16),
+        pltpu.VMEM((width, 2 * blocks), F32),
+        pltpu.VMEM((rows, width, 2 * blocks), BF16),
+        pltpu.VMEM((width, 2 * blocks), BF16),
+        pltpu.VMEM((width, 2 * blocks), F32),
+        pltpu.VMEM((width, 2 * blocks), F32),
+    )
+
+    def token_phase(saved, proj, turned, seen, same, w_in, gate_back, grad_proj, sums, share0, share1, share2):
+        for k, share in enumerate((share0, share1, share2)):
+            trees["in%d" % k].share = share
+        near = [
+            pltpu.make_async_copy(src, dst, fetch.at[6 + i])
+            for i, (src, dst) in enumerate((
+                (saved_far.at[0:6], saved), (proj_far, proj), (same_far, same), (w_in_far, w_in), (seen_far, seen),
+                (turned_far, turned), (x_far, out), (cot_far, grad_flat), (taps_far, grad_kernel),
+            ))
+        ]
+        for copy in near:
+            copy.start()
+        for post in posts_out:
+            for copy in post.copies(lambda peer, me: me):
+                copy.start()
+        own_out = [
+            pltpu.make_async_copy(post.source(me), post.target(me), fetch.at[15 + r]) for r, post in enumerate(posts_out)
+        ]
+        for copy in own_out:
+            copy.start()
+        sums[...] = jnp.zeros_like(sums)
+        tap_core().wait_recv()
+        for a in range(2):
+            for xd in range(2):
+                tap_own[a, c, xd] = tap_own[a, c, xd] + tap_one[a, xd]
+        tap_y().start()
+        trees["up"].finish(1)
+        trees["out"].finish(1)
+        trees["down"].finish(1)
+        for copy in near[:3]:
+            copy.wait()
+        last_row = lax.broadcasted_iota(jnp.int32, (span, 128), 0) == span - 1
+        first_row = lax.broadcasted_iota(jnp.int32, (span, 128), 0) == 0
+
+        def token_row(r):
+            posts_gate[r].arrive()
+            gate_back[...] = gate_got[r].astype(F32).T
+
+            def lanes_step(lanes):
+                skip = weights[9:10, lanes]
+                for k in range(3):
+                    taps = [weights[3 * k + i:3 * k + i + 1, lanes] for i in range(3)]
+                    grads, ends = [], []
+                    total = [jnp.zeros((span, 128), F32) for _ in range(3)]
+                    for p in range(n + 2):
+                        if p < n:
+                            here = slice(p * span, (p + 1) * span)
+                            if k == 0:
+                                grad = saved[4, r, here, lanes].astype(F32)
+                            else:
+                                grad = gate_back[here, lanes] + skip * saved[3, r, here, lanes].astype(F32)
+                                grad = grad * saved[2 - k, r, here, lanes].astype(F32)
+                            one = grad * same[0, r, here, :]
+                            two = grad * same[1, r, here, :]
+                            grads.append((grad, one, two))
+                            total[0] += grad * proj[r, k, (p + 2) * span:(p + 3) * span, lanes].astype(F32)
+                            total[1] += one * proj[r, k, (p + 1) * span:(p + 2) * span, lanes].astype(F32)
+                            total[2] += two * proj[r, k, p * span:(p + 1) * span, lanes].astype(F32)
+                        value = jnp.zeros((span, 128), F32)
+                        if p >= 2:
+                            value += taps[0] * grads[p - 2][0]
+                        if 1 <= p <= n:
+                            value += taps[1] * grads[p - 1][1]
+                        if p < n:
+                            value += taps[2] * grads[p][2]
+                        if p < 2:
+                            ends.append(value)
+                            value = jnp.where(first_row, value, 0.0)
+                        if p >= n:
+                            value += jnp.where(last_row, 0.0, pltpu.roll(ends[p - n], span - 1, 0))
+                        grad_proj[r, p * span:(p + 1) * span, pl.ds(pl.multiple_of(lanes.start + k * width, 128), 128)] = value.astype(BF16)
+                    for i in range(3):
+                        folded = total[i][0:8] + total[i][8:16] + total[i][16:24] + total[i][24:32]
+                        sums[3 * k + i, :, lanes] += folded
+
+            over_lanes(width, lanes_step)
+
+        def grad_row(r):
+            grad = dot_nt(grad_proj[r], w_in[...])
+            value = seen[r].reshape(ext, width).astype(F32)
+            scale = lax.rsqrt(jnp.mean(value * value, axis=-1, keepdims=True) + EPS)
+            vectors[10:11, :] += jnp.sum(grad * value * scale, axis=0, keepdims=True)
+            scaled = grad * gain_one[...]
+            shift = jnp.mean(scaled * value, axis=-1, keepdims=True) * (scale * scale * scale)
+            change = scaled * scale - value * shift
+            for p in range(n + 2):
+                block = change[p * span:(p + 1) * span]
+                if p >= 2:
+                    block += saved[5, r, (p - 2) * span:(p - 1) * span, :].astype(F32)
+                grad_sent[r, p] = block.astype(BF16)
+            posts_grad[r].start()
+            for slot in range(2):
+                @pl.when(me != n - 2 + slot)
+                def _():
+                    end_copy(r, slot, me).start()
+
+                @pl.when(me == n - 2 + slot)
+                def _():
+                    end_got[r, me] = grad_sent[r, slot, 0:tall]
+
+        def weight_part(k):
+            share = trees["in%d" % k].share
+            both = grad_proj[...].reshape(rows * ext, 3 * width)
+            for half in range(2):
+                low = k * width + half * (width // 2)
+                value = dot_nn(turned[...], both[:, low:low + width // 2]).astype(BF16)
+                for s in range(n):
+                    for core in range(2):
+                        block = (2 * s + core) * side
+                        share[s // 4, (s // 2) % 2, s % 2, core, half] = value[block:block + side]
+            trees["in%d" % k].start(0)
+
+        vectors[...] = jnp.zeros_like(vectors)
+        token_row(0)
+        for copy in near[3:5]:
+            copy.wait()
+        trees["up"].finish(2)
+        trees["out"].finish(2)
+        grad_row(0)
+        tap_y().wait_recv()
+        for xd in range(2):
+            tap_own[y, c, xd] = tap_own[y, c, xd] + tap_two[xd]
+        for xd in range(2):
+            @pl.when(4 * y + 2 * c + xd != me)
+            def _():
+                tap_hop_one(xd).start()
+
+            @pl.when(4 * y + 2 * c + xd == me)
+            def _():
+                tap_rows[aligned(me, each)] = tap_own[y, c, xd]
+
+        token_row(1)
+        trees["down"].finish(2)
+        near[5].wait()
+        for k in range(3):
+            weight_part(k)
+        trees["up"].finish(3)
+        trees["out"].finish(3)
+        trees["in0"].finish(0)
+        trees["in1"].finish(0)
+        trees["in2"].finish(0)
+        grad_row(1)
+        trees["down"].finish(3)
+        trees["up"].finish(4)
+        trees["out"].finish(4)
+
+        @pl.when(chosen_chunk)
+        def _():
+            for e in range(n):
+                @pl.when(me != e)
+                def _():
+                    remote(tap_own.at[y, c, 0], tap_rows.at[e * each:(e + 1) * each], tap_send.at[0, 0], tap_recv.at[0, e], {"seq": e}).wait_recv()
+            tap_cols[...] = tap_rows[...].astype(F32).T.astype(BF16).reshape(tap_cols.shape)
+            for j in range(1, n):
+                tap_hop_two(j, xbit, lax.rem(me + j, n)).start()
+            tap_home[y, c, xbit] = tap_cols[me]
+
+        vectors[0:9, :] = jnp.concatenate([jnp.sum(sums[i], axis=0, keepdims=True) for i in range(9)], axis=0)
+        vectors[9:10, :] = sums_in[5:6, :]
+        vectors[11:12, :] = sums_in[4:5, :]
+        vectors[12:16, :] = sums_in[0:4, :]
+
+        def vector_copy(step):
+            axis = ("core", "y", "x", "zl", "zh")[step]
+            return exchange(vectors, vector_got.at[step], vector_sems.at[0, step], vector_sems.at[1, step], axis)
+
+        def vector_finish(step):
+            vector_copy(step).wait()
+            vectors[...] += vector_got[step]
+            if step < 4:
+                vector_copy(step + 1).start()
+
+        vector_copy(0).start()
+        trees["in0"].finish(1)
+        trees["in1"].finish(1)
+        trees["down"].finish(4)
+        trees["up"].finish(5)
+        trees["out"].finish(5)
+        vector_finish(0)
+        trees["in2"].finish(1)
+        for xd in range(2):
+            @pl.when(4 * y + 2 * c + xd != me)
+            def _():
+                tap_hop_two(0, xd, 4 * y + 2 * c + xd).wait_recv()
+        tap_back_core().start()
+        trees["in0"].finish(2)
+        trees["in1"].finish(2)
+        trees["down"].finish(5)
+        for copy in own_out + near[6:8]:
+            copy.wait()
+
+        def home(target, r, block):
+            for d in range(n):
+                value = block(d)
+                for j in range(wide):
+                    place_at = pl.ds((r * blocks + d * span) * wide + j, span, stride=wide)
+                    target[place_at, :] += value[:, j * 128:(j + 1) * 128]
+
+        for r in range(rows):
+            posts_out[r].arrive()
+            home(out, r, lambda d: out_got[r, d * span:(d + 1) * span, :].astype(F32))
+        vector_finish(1)
+        trees["in2"].finish(2)
+        trees["in0"].finish(3)
+        trees["in1"].finish(3)
+        tap_back_core().wait_recv()
+        tap_back_y().start()
+        trees["up"].finish(6)
+        trees["out"].finish(6)
+        trees["down"].finish(6)
+        vector_finish(2)
+        trees["in2"].finish(3)
+        trees["in0"].finish(4)
+        trees["in1"].finish(4)
+        for half in range(2):
+            for core in range(2):
+                place_rows = slice(core * side, (core + 1) * side)
+                for tree, target in ((trees["up"], grad_up), (trees["out"], grad_out)):
+                    l = tree.share.shape[-1]
+                    target[place_rows, half * l:(half + 1) * l] = tree.gathered[core, half].astype(F32)
+        grad_down[...] = trees["down"].gathered[...].reshape(width, grad_down.shape[0]).astype(F32).T
+        vector_finish(3)
+        trees["in2"].finish(4)
+        trees["in0"].finish(5)
+        trees["in1"].finish(5)
+        for r in range(rows):
+            posts_grad[r].arrive()
+
+            @pl.when(me >= n - 2)
+            def _():
+                for d in range(n):
+                    @pl.when(me != d)
+                    def _():
+                        end_copy(r, 0, d).wait_recv()
+
+            keep_end = (me >= n - 2).astype(F32)
+            low_row = lax.broadcasted_iota(jnp.int32, (span, width), 0) == span - 1
+
+            def block(d):
+                value = grad_got[r, d * span:(d + 1) * span, :].astype(F32)
+                if d + 1 < n:
+                    end = jnp.where(me >= n - 2, end_got[r, d + 1, 0:8, :].astype(F32)[0:1, :], 0.0)
+                    value = value + jnp.where(low_row, end, 0.0)
+                return value
+
+            home(grad_flat, r, block)
+        vector_finish(4)
+        trees["in2"].finish(5)
+        trees["in0"].finish(6)
+        trees["in1"].finish(6)
+        tap_back_y().wait_recv()
+        near[8].wait()
+        for d in range(n):
+            value = tap_home[d // 4, (d // 2) % 2, d % 2].astype(F32)
+            for j in range(wide):
+                place_at = pl.ds(d * span * wide + j, span, stride=wide)
+                tanh = jnp.tanh(grad_kernel[place_at, :] * (1.0 / THRESH))
+                grad_kernel[place_at, :] = value[:, j * 128:(j + 1) * 128] * (tanh * tanh)
+        trees["in2"].finish(6)
+        for k in range(3):
+            tree = trees["in%d" % k]
+            l = tree.share.shape[-1]
+            for half in range(2):
+                for core in range(2):
+                    low = k * width + half * l
+                    grad_in[core * side:(core + 1) * side, low:low + l] = tree.gathered[core, half].astype(F32)
+
+        for tree in trees.values():
+            tree.drain()
+        for post in posts_out + posts_gate + posts_grad:
+            post.drain()
+        for r in range(rows):
+            for slot in range(2):
+                @pl.when(me != n - 2 + slot)
+                def _():
+                    end_copy(r, slot, me).wait_send()
+        tap_core().wait_send()
+        tap_y().wait_send()
+        for xd in range(2):
+            @pl.when(4 * y + 2 * c + xd != me)
+            def _():
+                tap_hop_one(xd).wait_send()
+
+        @pl.when(chosen_chunk)
+        def _():
+            for j in range(1, n):
+                tap_hop_two(j, xbit, lax.rem(me + j, n)).wait_send()
+
+        tap_back_core().wait_send()
+        tap_back_y().wait_send()
+
+    pl.run_scoped(
+        token_phase,
+        pltpu.VMEM((6, rows, blocks, width), BF16),
+        pltpu.VMEM(proj_far.shape, BF16),
+        pltpu.VMEM(turned_far.shape, BF16),
+        pltpu.VMEM(seen_far.shape, BF16),
+        pltpu.VMEM(same_far.shape, F32),
+        pltpu.VMEM(w_in_far.shape, BF16),
+        pltpu.VMEM((blocks, width), F32),
+        pltpu.VMEM((rows, ext, 3 * width), BF16),
+        pltpu.VMEM((9, 8, width), F32),
+        *[pltpu.VMEM((2, 2, 2, 2, 2, side, width // 2), BF16)] * 3,
+    )
+
+
+def call(body, outs, scratch, inputs, collective_id, far=(), far_outs=()):
+    return pl.pallas_call(
+        body,
+        out_shape=tuple(jax.ShapeDtypeStruct(*out) for out in outs),
+        in_specs=[pl.BlockSpec(memory_space=pl.ANY if i in far else pltpu.VMEM) for i in range(len(inputs))],
+        out_specs=tuple(pl.BlockSpec(memory_space=pl.ANY if i in far_outs else pltpu.VMEM) for i in range(len(outs))),
+        scratch_shapes=scratch,
+        compiler_params=pltpu.CompilerParams(
+            vmem_limit_bytes=VMEM_BYTES, collective_id=collective_id, has_side_effects=True
+        ),
+    )(*inputs)
+
+
+def local(
+    block_in, segment_ids, valid_mask, cotangent, gain_mix, in_proj, short_taps, long_kernel,
+    skip_gain, out_proj, gain_mlp, up_proj, down_proj,
+):
+    rows, blocks, _, width = block_in.shape
+    hidden = up_proj.shape[1]
+    n = lax.axis_size("seq")
+    each, span = width // n, blocks // n
+    tokens, ext = rows * blocks, blocks + 2 * span
+    side, wide = each // 2, width // 128
+    chunk = 512
+    x = block_in.reshape(tokens * wide, 128)
+    cot = cotangent.reshape(tokens * wide, 128)
+    raw = long_kernel.reshape(blocks * wide, 128)
+    marks = jnp.concatenate(
+        [segment_ids[:, :, 0], valid_mask[:, :, 0], jnp.zeros((8 - 2 * rows, blocks), jnp.int32)]
+    ).astype(F32)
+    weights = jnp.concatenate([
+        short_taps.reshape(3, 3, width).transpose(1, 0, 2).reshape(9, width), skip_gain[None], jnp.zeros((6, width), F32),
+    ])
+    table, turns = spectrum_tables(blocks, n)
+    dma = pltpu.SemaphoreType.DMA
+    bits = (2, 2, 2, 2, 2)
+    up_shape = bits + (side, hidden // 2)
+    down_shape = bits + (width // 4, hidden // n)
+    out_shape = bits + (side, width // 2)
+    low = lambda *shape: pltpu.VMEM(shape, BF16)
+    full = lambda *shape: pltpu.VMEM(shape, F32)
+
+    (seen, proj, turned, saved, same, spec_taps, spec_gate, back, share_up, share_down, share_out, sums) = call(
+        functools.partial(front_kernel, n, chunk),
+        [
+            ((rows, n + 2, span, width), BF16),
+            ((rows, 3, ext, width), BF16),
+            ((width, rows * ext), BF16),
+            ((7, rows, blocks, width), BF16),
+            ((3, rows, blocks, 128), F32),
+            ((width, 2 * blocks), F32),
+            ((rows, width, 2 * blocks), BF16),
+            ((rows, n, each, blocks), BF16),
+            (up_shape, BF16),
+            (down_shape, BF16),
+            (out_shape, BF16),
+            ((8, width), F32),
+        ],
+        [
+            full(blocks, 128), full(n, 128), full(n + 2, span, 128), full(2, n, 128),
+            low(rows, blocks, width), low(rows, blocks, width),
+            full(2 * n, width), low(2 * n, width), low(2, 2 * n, width), full(2, 2 * n, width),
+            low(2, 2, 2, span, width), low(n, span, width), low(width, blocks), low(2, 2, 2, each, blocks),
+            low(rows, n + 2, span, width), low(rows, n, span, width), low(rows, blocks, width), low(7, rows, blocks, width),
+            full(3, rows, blocks, 128), low(rows, width, 2 * blocks),
+            low(rows, width, blocks), low(rows, n, each, blocks), low(rows, n, each, blocks), low(rows, width, blocks),
+            low(rows, width, blocks), low(rows, n, each, blocks),
+            low(width, width), low(width, hidden), low(hidden, width),
+            dma((7,)), dma((11,)),
+            dma((rows, 2, n)), dma((2, n)), dma((rows, 2, n)), dma((4, n)), dma((5, n)),
+            dma((rows, 2, n)), dma((rows, 2, n)), dma((rows, 2, n)),
+        ],
+        (x, cot, raw, marks, gain_mix[None], gain_mlp[None], in_proj, out_proj, up_proj, down_proj, weights, table, turns),
+        1,
+        far=(0, 1, 2, 6, 7, 8, 9),
+        far_outs=range(11),
+    )
+
+    trees = []
+    for shape in (up_shape, down_shape, out_shape):
+        trees += tree_scratch(*shape[5:])
+    for _ in range(3):
+        trees += tree_scratch(*out_shape[5:])[1:]
+    block_out, grad_flat, grad_inp, grad_out, grad_up, grad_down, grad_kernel, vectors = call(
+        functools.partial(back_kernel, n),
+        [
+            (x.shape, F32),
+            (x.shape, F32),
+            ((each, 3 * width), F32),
+            ((each, width), F32),
+            ((each, hidden), F32),
+            ((hidden // n, width), F32),
+            (raw.shape, F32),
+            ((16, width), F32),
+        ],
+        [
+            low(rows, n, each, blocks), low(rows, width, blocks), low(rows, blocks, width),
+            low(rows, n + 2, span, width), low(rows, blocks, width), low(rows, n, 16, width),
+            dma((rows, 2, n)), dma((rows, 2, n)), dma((rows, 2, n)), dma((2, rows, n)), dma((17,)),
+            low(2, 2, 2, each, blocks), low(2, 2, each, blocks), low(2, each, blocks),
+            low(width, blocks), low(n, span, width), low(2, 2, 2, span, width),
+            dma((2, 4)), dma((2, n)), dma((2, n)),
+            full(5, 16, width), dma((2, 5)),
+        ] + trees,
+        (
+            back, spec_taps, spec_gate, table, turns, share_up, share_down, share_out, saved, proj, turned,
+            seen, same, in_proj, weights, gain_mix[None], sums, x, cot, raw,
+        ),
+        2,
+        far=(0, 1, 2, 5, 6, 7, 8, 9, 10, 11, 12, 13, 17, 18, 19),
+    )
+
+    stats = jnp.sum(vectors[12:16], axis=1)
+    grad_tap_rows = jnp.transpose(vectors[:9].reshape(3, 3, width), (1, 0, 2)).reshape(3, 3 * width)
+    rms_stats = jnp.sqrt(stats[:3] / (jnp.maximum(stats[3], 1.0) * width))
+    return (
+        block_out.reshape(block_in.shape),
+        grad_flat.reshape(block_in.shape),
+        vectors[10],
+        grad_inp,
+        grad_tap_rows,
+        grad_kernel.reshape(long_kernel.shape),
+        vectors[9],
+        grad_out,
+        vectors[11],
+        grad_up,
+        grad_down,
+        rms_stats,
+    )
+
+
+def chosen(block_in, *rest):
+    rows, blocks, _, width = block_in.shape
+    n = lax.axis_size("seq")
+    fits = blocks % (32 * n) == 0 and width % (32 * n) == 0 and n == 8 and rows == 2 and lax.axis_size("rows") == 4
+    return (local if fits else general_local)(block_in, *rest)
+
+
 def solution(mesh):
     return jax.shard_map(
-        local,
+        chosen,
         mesh=mesh,
         in_specs=(
             P("rows", None, "seq", None),

time: 1230 us -> 274 us (0.22)
  waiting for transfers between devices: 683 us -> 0 us
  Pallas kernels: 0 us -> 251 us
  matrix products: 220 us -> 0 us
  starting transfers between devices: 93.8 us -> 0 us
  other arithmetic: 82.7 us -> 2.75 us
  local copies, waits for them, and re-layouts: 80.1 us -> 18.4 us
  blocking collectives: 41.4 us -> 0 us
  between operations: 16.2 us -> 1.34 us
    all_to_all x12 -> x0, waiting for transfers between devices: 265 us -> none  [the longest x1 57.2 us: local(): lax.all_to_all(back_re.astype(jnp.bfloat16), 'seq', split_axis=1, concat_...]
    ppermute x6 -> x0, waiting for transfers between devices: 254 us -> none  [passed_along(): return lax.ppermute(block, axis, route)]
    pallas_call x0 -> x2, Pallas kernels: none -> 251 us  [call(): pl.pallas_call(body, out_shape=tuple((jax.ShapeDtypeStruct(*out) for out...]
    dot_general x48 -> x0, matrix products: 220 us -> none  [the longest x4 25.8 us: trans_times(): lax.dot_general(left, right, (((0,), (0,)), ((), ())), preferred_element_...]
    reduce_scatter x4 -> x0, waiting for transfers between devices: 162 us -> none  [the longest x1 130 us: local(): lax.psum_scatter(grad_inp, 'seq', scatter_dimension=0, tiled=True)]
    all_to_all x12 -> x0, starting transfers between devices: 79.6 us -> none  [the longest x1 23.9 us: local(): lax.all_to_all(tap_im.astype(jnp.bfloat16), 'seq', split_axis=2, concat_a...]
    psum x1 -> x0, blocking collectives: 41.4 us -> none  [local(): lax.psum((grad_gain_one, grad_gain_two, grad_tap_rows, grad_skip, stat_su...]
    unnamed x205 -> x20, local copies, waits for them, and re-layouts: 47 us -> 10.7 us
  transfers between devices with their start and end apart: 23 -> 0, of which waited for: 17 -> 0; matrix products, arithmetic and copies ran while one was open for 24% -> 0% of each run, Pallas kernels for 0% -> 0%
where the time goes in v3:
time: 274 us
  Pallas kernels  251 us (92%)
  local copies, waits for them, and re-layouts  18.4 us (7%)
  other arithmetic  2.75 us (1%)
    pallas_call x2, Pallas kernels, call(): pl.pallas_call(body, out_shape=tuple((jax.ShapeDtypeStruct(*out) for out...  251 us
    unnamed x20, local copies, waits for them, and re-layouts  10.7 us

profile of v3, /device:TPU:0, one launch (start us, length us, event | category | flops | bytes accessed | tf_op | source)
XLA Modules:
  0.0 273.5 jit_solution(11166321115065610087)
XLA Ops:
  0.7 0.1 pad.5.clone
  0.7 0.1 pad.2.clone
  0.8 1.3 broadcast_in_dim.17.gain_one
  2.1 0.7 broadcast_in_dim.19
  2.8 1.3 broadcast_in_dim.18.gain_two
  4.0 0.7 copy_bitcast_fusion
  4.7 0.7 add_convert_fusion.marks_in
  5.4 0.8 reshape.62
  6.2 0.7 maximum_maximum_fusion.weights
  6.9 113.3 %shard_map.238 = (bf16[2,10,32,768]{3,2,1,0:T(8,128)(2,1)}, bf16[2,3,320,768]{3,2,1,0:T(8,128)(2,1)}, bf16[768,640]{1,0:T(8,128)(2,1)}, bf16[7,2,256,768]{3,2,1,...) custom-call(f32[3072,128]{1,0:T(8,128)} %bitcast.18, ...), custom_call_target="tpu_custom_call" | custom-call | tf_op jit(solution)/shard_map/pallas_call | solution.py:1461
  120.2 137.8 %shard_map.239 = (f32[3072,128]{1,0:T(8,128)}, f32[3072,128]{1,0:T(8,128)}, f32[96,2304]{1,0:T(8,128)}, f32[96,768]{1,0:T(8,128)}, f32[96,3072]{1,0:T(8,128)}, /...) custom-call(bf16[2,8,96,256]{3,2,1,0:T(8,128)(2,1)} %get-tuple-element.32.back_far, ...), custom_call_target="tpu_custom_call" | custom-call | tf_op jit(solution)/shard_map/pallas_call | solution.py:1461
  258.0 0.9 slice_reduce_fusion
  258.8 0.6 slice.27
  260.0 0.5 divide_sqrt_fusion
  260.6 1.5 slice_reduce_fusion.1
  262.1 1.4 reshape.65
  263.5 0.0 copy-start
  263.5 3.7 %copy.43 = f32[2,256,1,768]{3,2,1,0:T(1,128)} copy(f32[2,256,1,768]{3,2,1,0:T(1,128)} %bitcast.25) | data formatting | bytes 3145728
  267.2 0.0 copy-done
  267.2 0.0 copy-start.3
  267.2 0.0 copy-start.4
  267.2 1.1 copy.44
  268.4 0.6 copy-done.3
  269.0 0.0 copy-start.5
  269.0 0.0 copy-start.2
  269.0 0.9 copy.45
  269.9 0.0 copy-done.4
  269.9 0.9 copy.46
  270.8 0.0 copy-done.5
  270.8 0.0 copy-start.1
  270.8 0.7 copy.47
  271.5 0.0 copy-done.2
  271.5 1.0 copy.48
  272.5 0.0 copy-done.1
  272.5 1.0 copy.49
  (2 shorter events, 0.0 us)
Async XLA Ops:
  263.5 3.8 %copy-start = (f32[3072,128]{1,0:T(8,128)S(1)}, f32[3072,128]{1,0:T(8,128)}, u32[]{:S(2)}) copy-start(f32[3072,128]{1,0:T(8,128)} %get-tuple-element.45) | copy-start | bytes 4718596
  267.2 1.7 copy-start.3
  267.2 2.7 copy-start.4
  269.0 1.8 copy-start.5
  269.0 2.5 copy-start.2
  270.8 1.7 copy-start.1
